TPU v7x, 32 devices: a whole 2x2x4 slice. The times are simulated.
32 devices in a mesh: ctx: 16 (over z, y, x), tp: 2 (over core).
Axes of the slice: x: 2, y: 2, z: 4, core: 2. Of those that a mesh axis runs over, the one named last changes fastest.
Arguments:
- tokens: bfloat16 [2048, 1024], P('ctx', 'tp'), may hold values from -6 to 6
- segment_ids: int32 [2048], P('ctx'), may hold values from 0 to 2, as said below
- ln1_gain: float32 [1024], replicated, may hold values from 0.25 to 1.75
- ln1_bias: float32 [1024], replicated, may hold values from -4 to 4
- w_qkv: bfloat16 [3, 1024, 1024], P(None, None, 'tp'), may hold values from -0.1875 to 0.1875
- b_qv: float32 [2, 1024], P(None, 'tp'), may hold values from -6 to 6
- w_out: bfloat16 [1024, 1024], P('tp'), may hold values from -0.375 to 0.375
- b_out: float32 [1024], P('tp'), may hold values from -6 to 6
- ln2_gain: float32 [1024], replicated, may hold values from 0.25 to 1.75
- ln2_bias: float32 [1024], replicated, may hold values from -4 to 4
- w_up: bfloat16 [1024, 4096], P(None, 'tp'), may hold values from -0.1875 to 0.1875
- b_up: float32 [4096], P('tp'), may hold values from -6 to 6
- w_down: bfloat16 [4096, 1024], P('tp'), may hold values from -0.09375 to 0.09375
- b_down: float32 [1024], P('tp'), may hold values from -6 to 6
- cotangent: bfloat16 [2048, 1024], P('ctx', 'tp'), may hold values from -6 to 6
Outputs:
- mixed: bfloat16 [2048, 1024], P('ctx', 'tp')
- input_grad: bfloat16 [2048, 1024], P('ctx', 'tp')
- ln1_gain_grad: float32 [1024], P(('tp', 'ctx'))
- ln1_bias_grad: float32 [1024], P(('tp', 'ctx'))
- w_qkv_grad: float32 [3, 1024, 1024], P(None, 'ctx', 'tp')
- b_qv_grad: float32 [2, 1024], P(None, ('tp', 'ctx'))
- w_out_grad: float32 [1024, 1024], P('tp', 'ctx')
- b_out_grad: float32 [1024], P(('tp', 'ctx'))
- ln2_gain_grad: float32 [1024], P(('tp', 'ctx'))
- ln2_bias_grad: float32 [1024], P(('tp', 'ctx'))
- w_up_grad: float32 [1024, 4096], P('ctx', 'tp')
- b_up_grad: float32 [4096], P(('tp', 'ctx'))
- w_down_grad: float32 [4096, 1024], P('tp', 'ctx')
- b_down_grad: float32 [1024], P(('tp', 'ctx'))
Inputs may be any that keep to these rules, and one draw needn't show every extreme that they name: `segment_ids`: document numbers never fall along the tokens; documents 0 and 2 hold 1 to 64 tokens each, so document 1 starts in the first block of 128 tokens and ends in the last one.
All inputs are finite; a program needn't handle non-finite values.
Results may differ from a plain program's by a relative error of at most 0.039.
Values may be sent and summed in bfloat16 or wider, within the bound.
No kernel may reach another device: no remote copies, remote signals or barrier semaphores. Data moves between devices by JAX's collectives and lax.ppermute only.
A program may use at most 128 MiB of HBM per device.

v0:
```python
import math

import jax
import jax.numpy as jnp
from jax import lax
from jax.sharding import PartitionSpec as P

HEADS = 16
HDIM = 64


norm_eps = 1e-05
mask_fill = -1e30
score_block = 512


def head_slopes(first_head, head_count):
    index_list = first_head + jnp.arange(head_count, dtype=jnp.int32)
    return jnp.exp2(-8.0 * (index_list + 1).astype(jnp.float32) / HEADS)


def pair_scores(query_heads, query_pos, query_seg, key_heads, key_pos, key_seg, slopes):
    logits = jnp.einsum(
        "qhd,khd->hqk", query_heads, key_heads, preferred_element_type=jnp.float32
    ) / math.sqrt(HDIM)
    distance = (key_pos[None, :] - query_pos[:, None]).astype(jnp.float32)
    allowed = (key_pos[None, :] <= query_pos[:, None]) & (key_seg[None, :] == query_seg[:, None])
    return (
        jnp.where(allowed[None], logits + slopes[:, None, None] * distance[None], mask_fill),
        allowed,
    )


def block_grads(
    query_heads,
    query_pos,
    query_seg,
    grad_heads,
    lse_rows,
    delta_rows,
    key_heads,
    value_heads,
    key_pos,
    key_seg,
    slopes,
):
    score, allowed = pair_scores(
        query_heads, query_pos, query_seg, key_heads, key_pos, key_seg, slopes
    )
    prob = jnp.where(allowed[None], jnp.exp(score - lse_rows.T[:, :, None]), 0.0)
    grad_prob = jnp.einsum(
        "qhd,khd->hqk", grad_heads, value_heads, preferred_element_type=jnp.float32
    )
    grad_score = (prob * (grad_prob - delta_rows.T[:, :, None])).astype(jnp.bfloat16)
    return (prob.astype(jnp.bfloat16), grad_score)


def over_blocks(row_count, step_fn, state_now):
    return lax.fori_loop(
        0,
        row_count // score_block,
        lambda number, inner_state: step_fn(number * score_block, score_block, inner_state),
        state_now,
    )


def seg_at(seg_array, where_row):
    return lax.dynamic_slice_in_dim(seg_array, where_row, 1)[0]


def gather_features(local_rows):
    return lax.all_gather(local_rows, "tp", axis=1, tiled=True)


def norm_stats(full_rows):
    center = full_rows - jnp.mean(full_rows, axis=-1, keepdims=True)
    inverse = lax.rsqrt(jnp.mean(center * center, axis=-1, keepdims=True) + norm_eps)
    return (center * inverse, inverse)


def norm_backward(part_grad, normed, inverse, gain, tp_rank, local_width):
    offset = tp_rank * local_width
    whole_grad = lax.psum(part_grad.astype(jnp.bfloat16), "tp").astype(jnp.float32)
    scaled = whole_grad * gain
    mean_one = jnp.mean(scaled, axis=-1, keepdims=True)
    mean_two = jnp.mean(scaled * normed, axis=-1, keepdims=True)
    input_grad = lax.dynamic_slice_in_dim(
        inverse * (scaled - mean_one - normed * mean_two), offset, local_width, 1
    )
    share_grad = lax.dynamic_slice_in_dim(whole_grad, offset, local_width, 1)
    normed_share = lax.dynamic_slice_in_dim(normed, offset, local_width, 1)
    gain_grad = jnp.sum(share_grad * normed_share, axis=0)
    bias_grad = jnp.sum(share_grad, axis=0)
    return (input_grad, gain_grad, bias_grad)


def on_device(
    tokens,
    segment_ids,
    ln1_gain,
    ln1_bias,
    w_qkv,
    b_qv,
    w_out,
    b_out,
    ln2_gain,
    ln2_bias,
    w_up,
    b_up,
    w_down,
    b_down,
    cotangent,
):
    local_rows, local_width = tokens.shape
    heads_local = local_width // HDIM
    tp_rank = lax.axis_index("tp")
    ctx_rank = lax.axis_index("ctx")
    slopes = head_slopes(tp_rank * heads_local, heads_local)
    own_pos = ctx_rank * local_rows + jnp.arange(local_rows, dtype=jnp.int32)
    own_first_seg = segment_ids[0]
    own_last_seg = segment_ids[-1]
    full_in = gather_features(tokens)
    normed_one, inverse_one = norm_stats(full_in.astype(jnp.float32))
    hidden_one = (normed_one * ln1_gain + ln1_bias).astype(jnp.bfloat16)
    projected = jnp.einsum("td,cde->cte", hidden_one, w_qkv, preferred_element_type=jnp.float32)
    query_rows = (projected[0] + b_qv[0]).astype(jnp.bfloat16)
    key_rows = projected[1].astype(jnp.bfloat16)
    value_rows = (projected[2] + b_qv[1]).astype(jnp.bfloat16)
    query_heads = query_rows.reshape(local_rows, heads_local, HDIM)
    key_heads = key_rows.reshape(local_rows, heads_local, HDIM)
    value_heads = value_rows.reshape(local_rows, heads_local, HDIM)
    start_state = (
        jnp.full((heads_local, local_rows), mask_fill, jnp.float32),
        jnp.zeros((heads_local, local_rows), jnp.float32),
        jnp.zeros((heads_local, local_rows, HDIM), jnp.float32),
    )
    piece_keys = lax.all_gather(key_rows, "ctx", axis=0, tiled=True)
    piece_values = lax.all_gather(value_rows, "ctx", axis=0, tiled=True)
    piece_seg = lax.all_gather(segment_ids, "ctx", axis=0, tiled=True)

    def forward_one_block(offset, size_each, inner_state):

        def attend(running):
            high_now, total_now, acc_now = running
            block_keys = lax.dynamic_slice_in_dim(piece_keys, offset, size_each).reshape(
                size_each, heads_local, HDIM
            )
            block_values = lax.dynamic_slice_in_dim(piece_values, offset, size_each).reshape(
                size_each, heads_local, HDIM
            )
            block_seg = lax.dynamic_slice_in_dim(piece_seg, offset, size_each)
            key_pos = offset + jnp.arange(size_each, dtype=jnp.int32)
            score, allowed = pair_scores(
                query_heads, own_pos, segment_ids, block_keys, key_pos, block_seg, slopes
            )
            high_new = jnp.maximum(high_now, jnp.max(score, axis=-1))
            weights = jnp.where(allowed[None], jnp.exp(score - high_new[:, :, None]), 0.0)
            factor = jnp.exp(high_now - high_new)
            total_new = total_now * factor + jnp.sum(weights, axis=-1)
            acc_new = acc_now * factor[:, :, None] + jnp.einsum(
                "hqk,khd->hqd",
                weights.astype(jnp.bfloat16),
                block_values,
                preferred_element_type=jnp.float32,
            )
            return (high_new, total_new, acc_new)

        needed = (offset <= own_pos[-1]) & (
            seg_at(piece_seg, offset + size_each - 1) >= own_first_seg
        )
        return lax.cond(needed, attend, lambda running: running, inner_state)

    high_fin, total_fin, acc_fin = over_blocks(piece_keys.shape[0], forward_one_block, start_state)
    attn_raw = jnp.transpose(acc_fin / total_fin[:, :, None], (1, 0, 2)).reshape(
        local_rows, local_width
    )
    lse_rows = (high_fin + jnp.log(total_fin)).T
    attn_low = attn_raw.astype(jnp.bfloat16)
    attn_share = lax.psum_scatter(
        jnp.dot(attn_low, w_out, preferred_element_type=jnp.float32).astype(jnp.bfloat16),
        "tp",
        scatter_dimension=1,
        tiled=True,
    ).astype(jnp.float32)
    middle = tokens.astype(jnp.float32) + attn_share + b_out
    full_mid = gather_features(middle.astype(jnp.bfloat16))
    normed_two, inverse_two = norm_stats(full_mid.astype(jnp.float32))
    hidden_two = (normed_two * ln2_gain + ln2_bias).astype(jnp.bfloat16)
    pre_act = jnp.dot(hidden_two, w_up, preferred_element_type=jnp.float32) + b_up
    gelu_out, gelu_back = jax.vjp(
        lambda pre_value: jax.nn.gelu(pre_value, approximate=True), pre_act
    )
    activated = gelu_out.astype(jnp.bfloat16)
    mlp_share = lax.psum_scatter(
        jnp.dot(activated, w_down, preferred_element_type=jnp.float32).astype(jnp.bfloat16),
        "tp",
        scatter_dimension=1,
        tiled=True,
    ).astype(jnp.float32)
    output = middle + mlp_share + b_down
    contract_rows = (((0,), (0,)), ((), ()))
    contract_cols = (((1,), (1,)), ((), ()))
    out_grad = cotangent.astype(jnp.float32)
    full_cot = gather_features(cotangent)
    grad_down = lax.dot_general(
        activated, full_cot, contract_rows, preferred_element_type=jnp.float32
    )
    grad_act = lax.dot_general(full_cot, w_down, contract_cols, preferred_element_type=jnp.float32)
    grad_pre = gelu_back(grad_act)[0].astype(jnp.bfloat16)
    grad_bup = jnp.sum(grad_pre.astype(jnp.float32), axis=0)
    grad_up = lax.dot_general(
        hidden_two, grad_pre, contract_rows, preferred_element_type=jnp.float32
    )
    part_two = lax.dot_general(grad_pre, w_up, contract_cols, preferred_element_type=jnp.float32)
    grad_mid_norm, grad_gain_two, grad_bias_two = norm_backward(
        part_two, normed_two, inverse_two, ln2_gain, tp_rank, local_width
    )
    grad_middle = out_grad + grad_mid_norm
    grad_bdown = jnp.sum(out_grad, axis=0)
    grad_bout = jnp.sum(grad_middle, axis=0)
    full_back = gather_features(grad_middle.astype(jnp.bfloat16))
    grad_wout = lax.dot_general(
        attn_low, full_back, contract_rows, preferred_element_type=jnp.float32
    )
    grad_attn = lax.dot_general(
        full_back, w_out, contract_cols, preferred_element_type=jnp.float32
    ).astype(jnp.bfloat16)
    grad_heads = grad_attn.reshape(local_rows, heads_local, HDIM)
    delta_rows = jnp.sum(
        grad_heads.astype(jnp.float32) * attn_raw.reshape(local_rows, heads_local, HDIM), axis=-1
    )
    query_zero = jnp.zeros((local_rows, heads_local, HDIM), jnp.float32)
    back_state = (query_zero,)
    backward_piece_keys = lax.all_gather(key_rows, "ctx", axis=0, tiled=True)
    backward_piece_values = lax.all_gather(value_rows, "ctx", axis=0, tiled=True)
    backward_piece_seg = lax.all_gather(segment_ids, "ctx", axis=0, tiled=True)

    def backward_one_block(offset, size_each, inner_state):

        def backward_work(running):
            block_keys = lax.dynamic_slice_in_dim(backward_piece_keys, offset, size_each).reshape(
                size_each, heads_local, HDIM
            )
            block_values = lax.dynamic_slice_in_dim(
                backward_piece_values, offset, size_each
            ).reshape(size_each, heads_local, HDIM)
            block_seg = lax.dynamic_slice_in_dim(backward_piece_seg, offset, size_each)
            key_pos = offset + jnp.arange(size_each, dtype=jnp.int32)
            prob_low, grad_score = block_grads(
                query_heads,
                own_pos,
                segment_ids,
                grad_heads,
                lse_rows,
                delta_rows,
                block_keys,
                block_values,
                key_pos,
                block_seg,
                slopes,
            )
            query_acc = running[0] + jnp.einsum(
                "hqk,khd->qhd", grad_score, block_keys, preferred_element_type=jnp.float32
            ) / math.sqrt(HDIM)
            return (query_acc,)

        needed = (offset <= own_pos[-1]) & (
            seg_at(backward_piece_seg, offset + size_each - 1) >= own_first_seg
        )
        return lax.cond(needed, backward_work, lambda running: running, inner_state)

    back_result = over_blocks(backward_piece_keys.shape[0], backward_one_block, back_state)
    query_grad = back_result[0].reshape(local_rows, local_width)
    piece_query = lax.all_gather(query_rows, "ctx", axis=0, tiled=True)
    piece_grad = lax.all_gather(grad_attn, "ctx", axis=0, tiled=True)
    piece_lse = lax.all_gather(lse_rows.astype(jnp.bfloat16), "ctx", axis=0, tiled=True).astype(
        jnp.float32
    )
    piece_delta = lax.all_gather(delta_rows.astype(jnp.bfloat16), "ctx", axis=0, tiled=True).astype(
        jnp.float32
    )
    owner_piece_seg = lax.all_gather(segment_ids, "ctx", axis=0, tiled=True)

    def owner_one_block(offset, size_each, inner_state):

        def owner_work(running):
            key_acc, value_acc = running
            block_query = lax.dynamic_slice_in_dim(piece_query, offset, size_each).reshape(
                size_each, heads_local, HDIM
            )
            block_grad = lax.dynamic_slice_in_dim(piece_grad, offset, size_each).reshape(
                size_each, heads_local, HDIM
            )
            block_lse = lax.dynamic_slice_in_dim(piece_lse, offset, size_each)
            block_delta = lax.dynamic_slice_in_dim(piece_delta, offset, size_each)
            block_seg = lax.dynamic_slice_in_dim(owner_piece_seg, offset, size_each)
            query_pos = offset + jnp.arange(size_each, dtype=jnp.int32)
            prob_low, grad_score = block_grads(
                block_query,
                query_pos,
                block_seg,
                block_grad,
                block_lse,
                block_delta,
                key_heads,
                value_heads,
                own_pos,
                segment_ids,
                slopes,
            )
            key_acc = key_acc + jnp.einsum(
                "hqk,qhd->khd", grad_score, block_query, preferred_element_type=jnp.float32
            ) / math.sqrt(HDIM)
            value_acc = value_acc + jnp.einsum(
                "hqk,qhd->khd", prob_low, block_grad, preferred_element_type=jnp.float32
            )
            return (key_acc, value_acc)

        needed = (offset + size_each - 1 >= own_pos[0]) & (
            seg_at(owner_piece_seg, offset) <= own_last_seg
        )
        return lax.cond(needed, owner_work, lambda running: running, inner_state)

    key_acc, value_acc = over_blocks(
        piece_query.shape[0], owner_one_block, (query_zero, query_zero)
    )
    key_grad = key_acc.reshape(local_rows, local_width)
    value_grad = value_acc.reshape(local_rows, local_width)
    query_low = query_grad.astype(jnp.bfloat16)
    key_low = key_grad.astype(jnp.bfloat16)
    value_low = value_grad.astype(jnp.bfloat16)
    grad_bqv = jnp.stack(
        (
            jnp.sum(query_low.astype(jnp.float32), axis=0),
            jnp.sum(value_low.astype(jnp.float32), axis=0),
        )
    )
    stacked_grads = jnp.stack((query_low, key_low, value_low))
    grad_qkv = jnp.einsum(
        "td,cte->cde", hidden_one, stacked_grads, preferred_element_type=jnp.float32
    )
    part_one = jnp.einsum("cte,cde->td", stacked_grads, w_qkv, preferred_element_type=jnp.float32)
    grad_in_norm, grad_gain_one, grad_bias_one = norm_backward(
        part_one, normed_one, inverse_one, ln1_gain, tp_rank, local_width
    )
    input_grad = (grad_middle + grad_in_norm).astype(jnp.bfloat16)
    reduced = (
        lax.psum_scatter(
            grad_gain_one.astype(jnp.bfloat16), "ctx", scatter_dimension=0, tiled=True
        ).astype(jnp.float32),
        lax.psum_scatter(
            grad_bias_one.astype(jnp.bfloat16), "ctx", scatter_dimension=0, tiled=True
        ).astype(jnp.float32),
        lax.psum_scatter(
            grad_qkv.astype(jnp.bfloat16), "ctx", scatter_dimension=1, tiled=True
        ).astype(jnp.float32),
        lax.psum_scatter(
            grad_bqv.astype(jnp.bfloat16), "ctx", scatter_dimension=1, tiled=True
        ).astype(jnp.float32),
        lax.psum_scatter(
            grad_wout.astype(jnp.bfloat16), "ctx", scatter_dimension=1, tiled=True
        ).astype(jnp.float32),
        lax.psum_scatter(
            grad_bout.astype(jnp.bfloat16), "ctx", scatter_dimension=0, tiled=True
        ).astype(jnp.float32),
        lax.psum_scatter(
            grad_gain_two.astype(jnp.bfloat16), "ctx", scatter_dimension=0, tiled=True
        ).astype(jnp.float32),
        lax.psum_scatter(
            grad_bias_two.astype(jnp.bfloat16), "ctx", scatter_dimension=0, tiled=True
        ).astype(jnp.float32),
        lax.psum_scatter(
            grad_up.astype(jnp.bfloat16), "ctx", scatter_dimension=0, tiled=True
        ).astype(jnp.float32),
        lax.psum_scatter(
            grad_bup.astype(jnp.bfloat16), "ctx", scatter_dimension=0, tiled=True
        ).astype(jnp.float32),
        lax.psum_scatter(
            grad_down.astype(jnp.bfloat16), "ctx", scatter_dimension=1, tiled=True
        ).astype(jnp.float32),
        lax.psum_scatter(
            grad_bdown.astype(jnp.bfloat16), "ctx", scatter_dimension=0, tiled=True
        ).astype(jnp.float32),
    )
    return (output.astype(jnp.bfloat16), input_grad) + tuple(reduced)


def solution(mesh):
    in_specs = (
        P("ctx", "tp"),
        P("ctx"),
        P(),
        P(),
        P(None, None, "tp"),
        P(None, "tp"),
        P("tp", None),
        P("tp"),
        P(),
        P(),
        P(None, "tp"),
        P("tp"),
        P("tp", None),
        P("tp"),
        P("ctx", "tp"),
    )
    out_specs = (
        P("ctx", "tp"),
        P("ctx", "tp"),
        P(("tp", "ctx")),
        P(("tp", "ctx")),
        P(None, "ctx", "tp"),
        P(None, ("tp", "ctx")),
        P("tp", "ctx"),
        P(("tp", "ctx")),
        P(("tp", "ctx")),
        P(("tp", "ctx")),
        P("ctx", "tp"),
        P(("tp", "ctx")),
        P("tp", "ctx"),
        P(("tp", "ctx")),
    )
    return jax.shard_map(
        on_device, mesh=mesh, in_specs=in_specs, out_specs=out_specs, check_vma=False
    )
```

profile of v0, /device:TPU:0, one launch (start us, length us, event | category | flops | bytes accessed | tf_op | source)
XLA Modules:
  0.0 919.7 jit_solution(5398359457708733254)
XLA Ops:
  18.7 44.0 %all-gather.1 = s32[16,1,128]{2,1,0:T(1,128)} all-gather(s32[1,1,128]{2,1,0:T(1,128)} %bitcast.15), channel_id=1, replica_groups=mesh['ctx'=16,'tp'=2] {'ctx'}, dimensions={0}, use_global_device_ids=true | all-gather | bytes 8704 | tf_op jit(solution)/shard_map/all_gather | solution.py:139
  64.6 12.0 %all-gather.13.cloned.1.call-done = bf16[1,2048,512]{2,1,0:T(8,128)(2,1)} async-done(((bf16[1,128,512]{2,1,0:T(8,128)(2,1)}), bf16[1,2048,512]{2,1,0:T(8,128)(2,1)}) %all-gather.13.cloned.1.call-update) | async-done | bytes 2097168 | tf_op jit(solution)/shard_map/all_gather | solution.py:137
  76.6 3.9 copy.66
  80.5 58.8 %all-gather.7.cloned.1.call-done = bf16[2048,512]{1,0:T(8,128)(2,1)} async-done(((bf16[128,512]{1,0:T(8,128)(2,1)}), bf16[2048,512]{1,0:T(8,128)(2,1)}) %all-gather.7.cloned.1.call-update) | async-done | bytes 2097168 | tf_op jit(solution)/shard_map/all_gather | solution.py:138
  139.3 4.0 copy.67
  143.3 24.9 %while.63 = (s32[]{:T(128)}, f32[8,128]{1,0:T(8,128)S(1)}, f32[8,128]{1,0:T(8,128)S(1)}, f32[8,128,64]{1,2,0:T(8,128)S(1)}, s32[128]{0:T(128)}, /*index=5*/s32[2...) while((s32[]{:T(128)}, f32[8,128]{1,0:T(8,128)S(1)}, ...), condition=%wide.region_7.8_spmd.clone, body=%wide.region_2.7_spmd.clone.sunk | while | flops 140446240 | bytes 12007687 | solution.py:59
  147.8 6.8 conditional.9
  174.2 4.7 fusion.87
  179.0 19.1 %reduce-scatter.9.cloned.1.call-done = bf16[128,512]{1,0:T(8,128)(2,1)} async-done(((bf16[128,1024]{1,0:T(8,128)(2,1)}), bf16[128,512]{1,0:T(8,128)(2,1)}) %reduce-scatter.9.cloned.1.call-update) | async-done | bytes 131088 | tf_op jit(solution)/shard_map/reduce_scatter | solution.py:179
  201.5 5.8 fusion.79
  211.0 18.9 %all-reduce.13.cloned.1.call-done = bf16[128,1024]{1,0:T(8,128)(2,1)} async-done(((bf16[128,1024]{1,0:T(8,128)(2,1)}), bf16[128,1024]{1,0:T(8,128)(2,1)}) %all-reduce.13.cloned.1.call-update) | async-done | bytes 262160 | tf_op jit(solution)/shard_map/psum | solution.py:83
  238.3 4.1 convolution_convert_fusion.5
  250.3 41.4 %all_gather.45 = bf16[2048,8]{0,1:T(8,128)(2,1)S(1)} all-gather(bf16[128,8]{0,1:T(8,128)(2,1)S(1)} %get-tuple-element.1846), channel_id=1, replica_groups=mesh['ctx'=16,'tp'=2] {'ctx'}, dimensions={0}, use_global_device_ids=true | all-gather | bytes 34816 | tf_op jit(solution)/shard_map/all_gather | solution.py:276
  295.1 4.0 copy.73
  301.7 38.8 %all_gather.47 = bf16[2048,8]{0,1:T(8,128)(2,1)S(1)} all-gather(bf16[128,8]{0,1:T(8,128)(2,1)S(1)} %convert_element_type.337), channel_id=1, replica_groups=mesh['ctx'=16,'tp'=2] {'ctx'}, dimensions={0}, use_global_device_ids=true | all-gather | bytes 34816 | tf_op jit(solution)/shard_map/all_gather | solution.py:279
  341.9 29.8 %while.64 = (s32[]{:T(128)}, f32[128,8,64]{0,2,1:T(8,128)}, s32[128]{0:T(128)}, s32[2048]{0:T(1024)}, s32[]{:T(128)}, /*index=5*/bf16[2048,512]{0,1:T(8,128)(2,1...) while((s32[]{:T(128)}, f32[128,8,64]{0,2,1:T(8,128)}, ...), condition=%wide.region_19.20_spmd.clone, body=%wide.region_16.19_spmd.clone.sunk | while | flops 206504480 | bytes 11425867 | solution.py:59
  346.4 11.8 %conditional.10 = (f32[128,8,64]{0,2,1:T(8,128)}) conditional(s32[]{:T(128)} %convert_element_type.531, f32[128,8,64]{0,2,1:T(8,128)} %get-tuple-element.2203, (s32[]{:T(128)}, bf16[2048,512]{0,1:T(8,128)(2,1)}, s32[128]{0:T(128)}, s32[2048]{0:T(1024)}, s32[128]{0:T(128)}, /*index=5*/bf16[128,8,64]{0,2,1:T(8,128)(2,1)S(1)}, f32[8]{0:T(128)S(1)}, ...), branch_computations={%region_17.17_spmd, %region_18.18_spmd.clone} | conditional | flops 206504448 | bytes 11425458 | solution.py:270
  371.8 4.0 copy.74
  376.5 68.5 %while.65 = (s32[]{:T(128)}, f32[128,8,64]{0,2,1:T(8,128)}, f32[128,8,64]{0,2,1:T(8,128)S(1)}, s32[128]{0:T(128)}, s32[2048]{0:T(1024)}, /*index=5*/s32[]{:T(128...) while((s32[]{:T(128)}, f32[128,8,64]{0,2,1:T(8,128)}, ...), condition=%wide.region_23.0_spmd.clone, body=%wide.region_20.23_spmd.clone.sunk | while | flops 274203168 | bytes 15186223 | solution.py:59
  380.3 13.4 %conditional.11 = ((f32[128,8,64]{0,2,1:T(8,128)}, f32[128,8,64]{0,2,1:T(8,128)S(1)})) conditional(s32[]{:T(128)} %convert_element_type.533, (f32[128,8,64]{0,2,1:T(8,128)}, f32[128,8,64]{0,2,1:T(8,128)S(1)}) %tuple.229, (s32[]{:T(128)}, bf16[2048,512]{0,1:T(8,128)(2,1)}, s32[128]{0:T(128)}, s32[128]{0:T(128)}, s32[2048]{0:T(1024)}, ...), branch_computations={%region_21.21_spmd, %region_22.22_spmd.clone} | conditional | flops 274203136 | bytes 15185790 | solution.py:322
  397.4 13.3 %conditional.11 = ((f32[128,8,64]{0,2,1:T(8,128)}, f32[128,8,64]{0,2,1:T(8,128)S(1)})) conditional(s32[]{:T(128)} %convert_element_type.533, (f32[128,8,64]{0,2,1:T(8,128)}, f32[128,8,64]{0,2,1:T(8,128)S(1)}) %tuple.229, (s32[]{:T(128)}, bf16[2048,512]{0,1:T(8,128)(2,1)}, s32[128]{0:T(128)}, s32[128]{0:T(128)}, s32[2048]{0:T(1024)}, ...), branch_computations={%region_21.21_spmd, %region_22.22_spmd.clone} | conditional | flops 274203136 | bytes 15185790 | solution.py:322
  414.5 13.3 %conditional.11 = ((f32[128,8,64]{0,2,1:T(8,128)}, f32[128,8,64]{0,2,1:T(8,128)S(1)})) conditional(s32[]{:T(128)} %convert_element_type.533, (f32[128,8,64]{0,2,1:T(8,128)}, f32[128,8,64]{0,2,1:T(8,128)S(1)}) %tuple.229, (s32[]{:T(128)}, bf16[2048,512]{0,1:T(8,128)(2,1)}, s32[128]{0:T(128)}, s32[128]{0:T(128)}, s32[2048]{0:T(1024)}, ...), branch_computations={%region_21.21_spmd, %region_22.22_spmd.clone} | conditional | flops 274203136 | bytes 15185790 | solution.py:322
  431.6 13.4 %conditional.11 = ((f32[128,8,64]{0,2,1:T(8,128)}, f32[128,8,64]{0,2,1:T(8,128)S(1)})) conditional(s32[]{:T(128)} %convert_element_type.533, (f32[128,8,64]{0,2,1:T(8,128)}, f32[128,8,64]{0,2,1:T(8,128)S(1)}) %tuple.229, (s32[]{:T(128)}, bf16[2048,512]{0,1:T(8,128)(2,1)}, s32[128]{0:T(128)}, s32[128]{0:T(128)}, s32[2048]{0:T(1024)}, ...), branch_computations={%region_21.21_spmd, %region_22.22_spmd.clone} | conditional | flops 274203136 | bytes 15185790 | solution.py:322
  459.0 7.6 copy.79
  467.3 4.5 convolution_convert_fusion.1
  471.9 4.5 convolution_convert_fusion
  484.4 39.8 %reduce-scatter.19.cloned.1.call-done = bf16[32,2]{1,0:T(8,128)(2,1)} async-done(((bf16[512,2]{1,0:T(8,128)(2,1)}), bf16[32,2]{1,0:T(8,128)(2,1)}) %reduce-scatter.19.cloned.1.call-update) | async-done | bytes 144
  525.6 16.1 %all-reduce.15.cloned.1.call-done = bf16[128,1024]{1,0:T(8,128)(2,1)} async-done(((bf16[128,1024]{1,0:T(8,128)(2,1)}), bf16[128,1024]{1,0:T(8,128)(2,1)}) %all-reduce.15.cloned.1.call-update) | async-done | bytes 262160 | tf_op jit(solution)/shard_map/psum | solution.py:83
  544.8 79.3 %all-reduce.8 = (bf16[512]{0:T(512)(128)(2,1)S(1)}, bf16[512]{0:T(512)(128)(2,1)S(1)}, bf16[512]{0:T(512)(128)(2,1)S(1)}, bf16[512]{0:T(512)(128)(2,1)S(1)}, bf1...) all-reduce(bf16[512]{0:T(512)(128)(2,1)S(1)} %get-tuple-element.174, ...), channel_id=5, replica_groups=mesh['ctx'=16,'tp'=2] {'ctx'}, use_global_device_ids=true, to_apply=%region_28.29.clone | all-reduce | flops 5120 | bytes 20480
  628.1 89.8 %all-reduce.17.cloned.1.call-done = bf16[3,1024,512]{2,0,1:T(4,128)(2,1)} async-done(((bf16[3,1024,512]{2,0,1:T(4,128)(2,1)}), bf16[3,1024,512]{2,0,1:T(4,128)(2,1)}) %all-reduce.17.cloned.1.call-update) | async-done | bytes 3145744
  719.8 94.5 %reduce-scatter.15.cloned.1.call-done = bf16[64,2048]{1,0:T(8,128)(2,1)} async-done(((bf16[1024,2048]{1,0:T(8,128)(2,1)}), bf16[64,2048]{1,0:T(8,128)(2,1)}) %reduce-scatter.15.cloned.1.call-update) | async-done | bytes 262160 | tf_op jit(solution)/shard_map/reduce_scatter | solution.py:372
  816.1 95.4 %reduce-scatter.17.cloned.1.call-done = bf16[2048,64]{0,1:T(8,128)(2,1)} async-done(((bf16[2048,1024]{0,1:T(8,128)(2,1)}), bf16[2048,64]{0,1:T(8,128)(2,1)}) %reduce-scatter.17.cloned.1.call-update) | async-done | bytes 262160 | tf_op jit(solution)/shard_map/reduce_scatter | solution.py:378
  (309 shorter events, 184.2 us)
Async XLA Ops:
  7.2 69.4 %all-gather.13.cloned.1.call-start = ((), (), s32[]{:S(2)}) async-start(), calls=%async_computation.16 | async-start | bytes 2228224 | tf_op jit(solution)/shard_map/all_gather | solution.py:137
  13.2 126.2 %all-gather.7.cloned.1.call-start = ((), (), s32[]{:S(2)}) async-start(), calls=%async_computation.6 | async-start | bytes 2228224 | tf_op jit(solution)/shard_map/all_gather | solution.py:138
  15.6 182.5 %reduce-scatter.9.cloned.1.call-start = ((), (), s32[]{:S(2)}) async-start(), calls=%async_computation.7 | async-start | bytes 393216 | tf_op jit(solution)/shard_map/reduce_scatter | solution.py:179
  171.2 58.7 %all-reduce.13.cloned.1.call-start = ((), (), s32[]{:S(2)}) async-start(), calls=%async_computation.9 | async-start | bytes 524288 | tf_op jit(solution)/shard_map/psum | solution.py:83
  174.2 27.2 %copy-start.20 = (f32[1024]{0:T(1024)S(1)}, f32[1024]{0:T(1024)}, u32[]{:S(2)}) copy-start(f32[1024]{0:T(1024)} %param.35) | copy-start | bytes 12292
  174.2 27.2 %copy-start.22 = (f32[1024]{0:T(1024)S(1)}, f32[1024]{0:T(1024)}, u32[]{:S(2)}) copy-start(f32[1024]{0:T(1024)} %param.36) | copy-start | bytes 12292
  201.1 6.2 copy-start.5
  201.2 6.1 copy-start.31
  201.5 5.8 copy-start.34
  201.5 6.6 copy-start.9
  208.1 22.9 %copy-start.32 = (f32[128]{0:T(128)S(1)}, f32[128]{0:T(128)}, u32[]{:S(2)}) copy-start(f32[128]{0:T(128)} %copy-done.31) | copy-start | bytes 1540
  210.3 84.8 %all-gather.9.cloned.1.call-start = ((), (), s32[]{:S(2)}) async-start(), calls=%async_computation.10 | async-start | bytes 2228224 | tf_op jit(solution)/shard_map/all_gather | solution.py:274
  210.9 160.9 %all-gather.11.cloned.1.call-start = ((), (), s32[]{:S(2)}) async-start(), calls=%async_computation.11 | async-start | bytes 2228224 | tf_op jit(solution)/shard_map/all_gather | solution.py:275
  229.9 7.2 copy-start.10
  238.3 242.9 %reduce-scatter.11.cloned.1.call-start = ((), (), s32[]{:S(2)}) async-start(), calls=%async_computation.8 | async-start | bytes 393216 | tf_op jit(solution)/shard_map/reduce_scatter | solution.py:194
  242.4 6.1 copy-start.36
  242.5 240.4 %reduce-scatter.13.cloned.1.call-start = ((), (), s32[]{:S(2)}) async-start(), calls=%async_computation.13 | async-start | bytes 1114112 | tf_op jit(solution)/shard_map/reduce_scatter | solution.py:360
  245.0 279.2 %reduce-scatter.19.cloned.1.call-start = ((), (), s32[]{:S(2)}) async-start(), calls=%async_computation.17 | async-start | bytes 139264
  380.3 5.3 copy-start.19
  382.4 5.4 copy-start.2
  397.4 5.3 copy-start.19
  399.5 5.4 copy-start.2
  414.5 5.3 copy-start.19
  416.6 5.4 copy-start.2
  431.6 5.3 copy-start.19
  433.7 5.4 copy-start.2
  452.2 89.5 %all-reduce.15.cloned.1.call-start = ((), (), s32[]{:S(2)}) async-start(), calls=%async_computation.12 | async-start | bytes 524288 | tf_op jit(solution)/shard_map/psum | solution.py:83
  455.1 262.8 %all-reduce.17.cloned.1.call-start = ((), (), s32[]{:S(2)}) async-start(), calls=%async_computation.18 | async-start | bytes 8388608
  466.7 347.6 %reduce-scatter.15.cloned.1.call-start = ((), (), s32[]{:S(2)}) async-start(), calls=%async_computation.14 | async-start | bytes 4456448 | tf_op jit(solution)/shard_map/reduce_scatter | solution.py:372
  471.8 439.6 %reduce-scatter.17.cloned.1.call-start = ((), (), s32[]{:S(2)}) async-start(), calls=%async_computation.15 | async-start | bytes 4456448 | tf_op jit(solution)/shard_map/reduce_scatter | solution.py:378
  476.4 4.8 copy-start.16
  476.4 4.8 copy-start.26
  (30 other events, 64.0 us)
Sparse Core Ops, SparseCore 0:
  13.3 63.2 all-gather.12
  79.9 59.3 all-gather.6
  171.3 26.7 reduce-scatter.8
  210.4 19.4 all-reduce.12
  233.1 61.9 all-gather.8
  298.3 59.4 all-gather.10
  360.0 6.3 reduce-scatter.10
  368.8 78.7 reduce-scatter.12
  452.3 71.9 reduce-scatter.18
  527.1 14.5 all-reduce.14
  547.4 170.5 all-reduce.16
  720.2 94.0 reduce-scatter.14
  816.7 94.7 reduce-scatter.16
where the time goes:
time: 923 us; the launch traced here: 920 us
  waiting for transfers between devices  448 us (49%)
  blocking collectives  212 us (23%)
  local copies, waits for them, and re-layouts  93.5 us (10%)
  matrix products  78.8 us (9%)
  other arithmetic  45.9 us (5%)
  loops' own time  24.3 us (3%)
  between operations  16.3 us (2%)
    unnamed x15, waiting for transfers between devices  130 us
    reduce_scatter x1, waiting for transfers between devices, on_device(): lax.psum_scatter(grad_down.astype(jnp.bfloat16), 'ctx', scatter_dimension...  95.4 us
    reduce_scatter x1, waiting for transfers between devices, on_device(): lax.psum_scatter(grad_up.astype(jnp.bfloat16), 'ctx', scatter_dimension=0...  94.5 us
    unnamed x1, blocking collectives  79.3 us
    all_gather x1, waiting for transfers between devices, on_device(): piece_values = lax.all_gather(value_rows, 'ctx', axis=0, tiled=True)  58.8 us
    all_gather x1, blocking collectives, on_device(): piece_seg = lax.all_gather(segment_ids, 'ctx', axis=0, tiled=True)  44 us
    all_gather x1, blocking collectives, on_device(): lax.all_gather(lse_rows.astype(jnp.bfloat16), 'ctx', axis=0, tiled=True)  41.4 us
    all_gather x1, blocking collectives, on_device(): lax.all_gather(delta_rows.astype(jnp.bfloat16), 'ctx', axis=0, tiled=True)  38.8 us
  transfers between devices with their start and end apart: 13, of which 10 were waited for; matrix products, arithmetic and copies ran while one was open for 19% of the time, Pallas kernels for 0%

commit v1 on v0

--- a/solution.py
+++ b/solution.py
@@ -1,8 +1,11 @@
+import functools
 import math
 
 import jax
 import jax.numpy as jnp
 from jax import lax
+from jax.experimental import pallas as pl
+from jax.experimental.pallas import tpu as pltpu
 from jax.sharding import PartitionSpec as P
 
 HEADS = 16
@@ -12,6 +15,15 @@
 norm_eps = 1e-05
 mask_fill = -1e30
 score_block = 512
+
+HALF = 64
+SOURCES = 4
+QUERIES = SOURCES * HALF
+SEG_ROW = 5 * HDIM // 2
+FWD_ROWS = SEG_ROW + 16
+BACK_ROWS = SEG_ROW + 3 * HDIM // 2
+GELU_A = math.sqrt(2.0 / math.pi)
+GELU_B = 0.044715
 
 
 def head_slopes(first_head, head_count):
@@ -385,6 +397,721 @@
     return (output.astype(jnp.bfloat16), input_grad) + tuple(reduced)
 
 
+def swap_halves(first, second):
+    lane = lax.broadcasted_iota(jnp.int32, first.shape, 1)
+    low = lane < HALF
+    return (
+        jnp.where(low, first, pltpu.roll(second, HALF, 1)),
+        jnp.where(low, pltpu.roll(first, HALF, 1), second),
+    )
+
+
+def unpack_pair(ref, index, first_row, count):
+    one = ref[index, first_row : first_row + count, :].astype(jnp.float32)
+    two = ref[index + 1, first_row : first_row + count, :].astype(jnp.float32)
+    return jnp.concatenate(swap_halves(one, two), axis=0)
+
+
+def pack_pair(ref, index, first_row, count, rows):
+    one, two = swap_halves(rows[:count], rows[count:])
+    ref[index, first_row : first_row + count, :] = one.astype(ref.dtype)
+    ref[index + 1, first_row : first_row + count, :] = two.astype(ref.dtype)
+
+
+def both_halves(ref, first_row, count):
+    return jnp.concatenate(
+        [ref[0, first_row : first_row + count, :], ref[1, first_row : first_row + count, :]],
+        axis=1,
+    )
+
+
+def dot_of(left, right, left_dim, right_dim):
+    return lax.dot_general(
+        left, right, (((left_dim,), (right_dim,)), ((), ())), preferred_element_type=jnp.float32
+    )
+
+
+def qkv_kernel(rank_ref, x_ref, gain_ref, bias_ref, w_ref, b_ref, seg_ref, send_ref, own_ref, h_ref):
+    step = pl.program_id(0)
+    rows = own_ref.shape[0]
+    width = own_ref.shape[1]
+    heads = width // HDIM
+
+    @pl.when(step == 0)
+    def _():
+        normed, _ = norm_stats(both_halves(x_ref, 0, rows).astype(jnp.float32))
+        h_ref[...] = (normed * gain_ref[...] + bias_ref[...]).astype(jnp.bfloat16)
+        own_ref[...] = h_ref[:, pl.ds(pl.multiple_of(rank_ref[0] * width, width), width)]
+
+    flat = jnp.dot(h_ref[...], w_ref[0], preferred_element_type=jnp.float32) + b_ref[0]
+    turned = flat.T
+
+    @pl.when(step == 0)
+    def _():
+        scaled = turned.astype(jnp.bfloat16).astype(jnp.float32) * (1.0 / math.sqrt(HDIM))
+        seg_rows = jnp.broadcast_to(seg_ref[...].astype(jnp.float32), (16, rows)).astype(
+            jnp.bfloat16
+        )
+        for head in range(heads):
+            pack_pair(send_ref, 2 * head, 2 * HDIM, HDIM // 2, scaled[head * HDIM : (head + 1) * HDIM])
+            send_ref[2 * head, SEG_ROW : SEG_ROW + 16, :] = seg_rows
+            send_ref[2 * head + 1, SEG_ROW : SEG_ROW + 16, :] = seg_rows
+
+    for which in (1, 2):
+
+        @pl.when(step == which)
+        def _(which=which):
+            low = turned.astype(jnp.bfloat16)
+            for head in range(heads):
+                piece = low[head * HDIM : (head + 1) * HDIM]
+                send_ref[2 * head, (which - 1) * HDIM : which * HDIM, :] = piece
+                send_ref[2 * head + 1, (which - 1) * HDIM : which * HDIM, :] = piece
+
+
+def masked_scores(keys, query, slope, query_pos, begin, first_key, top):
+    score = dot_of(keys, query, 1, 0)
+    key_pos = first_key + lax.broadcasted_iota(jnp.int32, score.shape, 0)
+    score = score + slope * (key_pos - top).astype(jnp.float32)
+    allowed = (key_pos <= query_pos) & (key_pos >= begin)
+    return jnp.where(allowed, score, mask_fill)
+
+
+def doc_starts(recv_ref):
+    seg = recv_ref[:, SEG_ROW : SEG_ROW + 16, :].astype(jnp.float32)[:, 0, :]
+    one = jnp.sum(jnp.where(seg < 0.5, 1.0, 0.0))
+    two = jnp.sum(jnp.where(seg < 1.5, 1.0, 0.0))
+    return one.astype(jnp.int32), two.astype(jnp.int32)
+
+
+def query_geometry(tile, place, starts):
+    lane = lax.broadcasted_iota(jnp.int32, (1, QUERIES), 1)
+    query_pos = 2 * HALF * (tile * SOURCES + lane // HALF) + HALF * place + lane % HALF
+    begin_one, begin_two = starts
+    begin = jnp.where(
+        query_pos >= begin_two, begin_two, jnp.where(query_pos >= begin_one, begin_one, 0)
+    )
+    return query_pos, begin
+
+
+def tile_rows(ref, tile, first_row):
+    return jnp.concatenate(
+        [
+            unpack_pair(ref, tile * SOURCES + pair, first_row, HDIM // 2)
+            for pair in range(0, SOURCES, 2)
+        ],
+        axis=1,
+    )
+
+
+def forward_kernel(slope_ref, place_ref, recv_ref, send_ref, out_ref, lse_ref, key_ref):
+    count = recv_ref.shape[0]
+    block = 2 * HALF
+    slope, place = slope_ref[0], place_ref[0]
+    starts = doc_starts(recv_ref)
+    for source in range(count):
+        key_ref[source * block : (source + 1) * block, :] = (
+            recv_ref[source, 0:HDIM, :].astype(jnp.float32).T.astype(jnp.bfloat16)
+        )
+    values = jnp.concatenate([recv_ref[s, HDIM : 2 * HDIM, :] for s in range(count)], axis=1)
+    for tile in range(count // SOURCES):
+        reach = (tile + 1) * SOURCES * block
+        query = tile_rows(recv_ref, tile, 2 * HDIM).astype(jnp.bfloat16)
+        query_pos, begin = query_geometry(tile, place, starts)
+        score = masked_scores(key_ref[0:reach, :], query, slope, query_pos, begin, 0, reach)
+        high = jnp.max(score, axis=0, keepdims=True)
+        weights = jnp.exp(score - high)
+        total = jnp.sum(weights, axis=0, keepdims=True)
+        out = dot_of(values[:, 0:reach], weights.astype(jnp.bfloat16), 1, 0) / total
+        here = slice(tile * QUERIES, (tile + 1) * QUERIES)
+        out_ref[:, here] = out
+        lse_ref[:, here] = high + jnp.log(total)
+        for pair in range(0, SOURCES, 2):
+            pack_pair(
+                send_ref,
+                tile * SOURCES + pair,
+                0,
+                HDIM // 2,
+                out[:, pair * HALF : (pair + 2) * HALF],
+            )
+
+
+def heads_of(ref, first_row):
+    return jnp.concatenate(
+        [unpack_pair(ref, index, first_row, HDIM // 2) for index in range(0, ref.shape[0], 2)],
+        axis=0,
+    )
+
+
+def out_kernel(rank_ref, recv_ref, w_ref, b_ref, part_ref, attn_ref, acc_ref):
+    width = w_ref.shape[0]
+    turned = heads_of(recv_ref, 0).astype(jnp.bfloat16)
+    attn_ref[...] = turned
+    acc_ref[...] = dot_of(turned, w_ref[...], 0, 0)
+    own = pl.ds(pl.multiple_of(rank_ref[0] * width, width), width)
+    acc_ref[:, own] = acc_ref[:, own] + b_ref[...]
+    part_ref[...] = acc_ref[...].astype(jnp.bfloat16)
+
+
+def gelu_pair(value):
+    inner = GELU_A * (value + GELU_B * (value * value * value))
+    tanh = jnp.tanh(inner)
+    half = 0.5 * (1.0 + tanh)
+    slope = half + 0.5 * value * (1.0 - tanh * tanh) * (
+        GELU_A * (1.0 + 3.0 * GELU_B * (value * value))
+    )
+    return value * half, slope
+
+
+def mlp_kernel(
+    rank_ref,
+    x_ref,
+    own_ref,
+    other_ref,
+    gain_ref,
+    bias_ref,
+    up_ref,
+    b_up_ref,
+    down_ref,
+    middle_ref,
+    hidden_ref,
+    act_ref,
+    back_ref,
+    b_grad_ref,
+    share_ref,
+    swap_ref,
+    grad_acc,
+    mlp_acc,
+):
+    step = pl.program_id(0)
+    rows = act_ref.shape[0]
+    width = share_ref.shape[1]
+
+    @pl.when(step == 0)
+    def _():
+        middle = (
+            both_halves(x_ref, 0, rows).astype(jnp.float32)
+            + own_ref[...].astype(jnp.float32)
+            + other_ref[...].astype(jnp.float32)
+        )
+        middle_ref[...] = middle
+        normed, _ = norm_stats(middle.astype(jnp.bfloat16).astype(jnp.float32))
+        hidden_ref[...] = (normed * gain_ref[...] + bias_ref[...]).astype(jnp.bfloat16)
+        grad_acc[...] = jnp.zeros_like(grad_acc)
+        mlp_acc[...] = jnp.zeros_like(mlp_acc)
+
+    pre = jnp.dot(hidden_ref[...], up_ref[...], preferred_element_type=jnp.float32) + b_up_ref[...]
+    act, slope = gelu_pair(pre)
+    act = act.astype(jnp.bfloat16)
+    act_ref[...] = act
+    grad_act = dot_of(both_halves(x_ref, rows, rows), down_ref[...], 1, 1)
+    grad_pre = (grad_act * slope).astype(jnp.bfloat16)
+    back_ref[...] = grad_pre
+    b_grad_ref[...] = jnp.sum(grad_pre.astype(jnp.float32), axis=0, keepdims=True)
+    grad_acc[...] += dot_of(grad_pre, up_ref[...], 1, 1)
+    mlp_acc[...] += jnp.dot(act, down_ref[...], preferred_element_type=jnp.float32)
+
+    @pl.when(step == pl.num_programs(0) - 1)
+    def _():
+        rank = rank_ref[0]
+        swap_ref[:, 0 : 2 * width] = grad_acc[...].astype(jnp.bfloat16)
+        swap_ref[:, 2 * width :] = mlp_acc[
+            :, pl.ds(pl.multiple_of((1 - rank) * width, width), width)
+        ].astype(jnp.bfloat16)
+        share_ref[...] = mlp_acc[:, pl.ds(pl.multiple_of(rank * width, width), width)]
+
+
+def norm_back(whole, normed, inverse, gain):
+    scaled = whole * gain
+    mean_one = jnp.mean(scaled, axis=-1, keepdims=True)
+    mean_two = jnp.mean(scaled * normed, axis=-1, keepdims=True)
+    return inverse * (scaled - mean_one - normed * mean_two)
+
+
+def middle_kernel(
+    rank_ref,
+    x_ref,
+    own_ref,
+    other_ref,
+    middle_ref,
+    share_ref,
+    gain_ref,
+    b_down_ref,
+    w_out_ref,
+    mixed_ref,
+    grad_ref,
+    low_ref,
+    send_ref,
+    small_ref,
+    wide_ref,
+):
+    rows, width = mixed_ref.shape
+    own = pl.ds(pl.multiple_of(rank_ref[0] * width, width), width)
+    mixed_ref[...] = (
+        middle_ref[:, own]
+        + share_ref[...]
+        + other_ref[:, 2 * width :].astype(jnp.float32)
+        + b_down_ref[...]
+    ).astype(jnp.bfloat16)
+    whole = own_ref[:, 0 : 2 * width].astype(jnp.float32) + other_ref[:, 0 : 2 * width].astype(
+        jnp.float32
+    )
+    normed, inverse = norm_stats(middle_ref[...].astype(jnp.bfloat16).astype(jnp.float32))
+    cot = both_halves(x_ref, rows, rows).astype(jnp.float32)
+    grad = cot + norm_back(whole, normed, inverse, gain_ref[...])
+    low = grad.astype(jnp.bfloat16)
+    low_ref[...] = low
+    wide_ref[0:1] = jnp.sum(whole * normed, axis=0, keepdims=True)
+    wide_ref[1:2] = jnp.sum(whole, axis=0, keepdims=True)
+    wide_ref[2:3] = jnp.sum(grad, axis=0, keepdims=True)
+    wide_ref[3:4] = jnp.sum(cot, axis=0, keepdims=True)
+    wide_ref[8:, :] = grad
+    small_ref[...] = wide_ref[0:8, own]
+    grad_ref[...] = wide_ref[8:, own]
+    back = dot_of(w_out_ref[...], low, 1, 1).astype(jnp.bfloat16).astype(jnp.float32)
+    for head in range(width // HDIM):
+        pack_pair(send_ref, 2 * head, 0, HDIM // 2, back[head * HDIM : (head + 1) * HDIM])
+
+
+def backward_kernel(
+    slope_ref,
+    place_ref,
+    rank_ref,
+    recv_ref,
+    grad_ref,
+    out_ref,
+    lse_ref,
+    own_ref,
+    other_ref,
+    send_ref,
+    key_ref,
+    value_ref,
+    key_acc,
+    value_acc,
+    all_ref,
+    weight_ref,
+):
+    count = recv_ref.shape[0]
+    block = 2 * HALF
+    slope, place, rank = slope_ref[0], place_ref[0], rank_ref[0]
+    starts = doc_starts(recv_ref)
+    for source in range(count):
+        there = slice(source * block, (source + 1) * block)
+        key_ref[there, :] = recv_ref[source, 0:HDIM, :].astype(jnp.float32).T.astype(jnp.bfloat16)
+        value_ref[there, :] = (
+            recv_ref[source, HDIM : 2 * HDIM, :].astype(jnp.float32).T.astype(jnp.bfloat16)
+        )
+    keys_turned = jnp.concatenate([recv_ref[s, 0:HDIM, :] for s in range(count)], axis=1)
+    key_acc[...] = jnp.zeros_like(key_acc)
+    value_acc[...] = jnp.zeros_like(value_acc)
+    for tile in range(count // SOURCES):
+        reach = (tile + 1) * SOURCES * block
+        here = slice(tile * QUERIES, (tile + 1) * QUERIES)
+        query = tile_rows(recv_ref, tile, 2 * HDIM).astype(jnp.bfloat16)
+        grad_wide = tile_rows(grad_ref, tile, 0)
+        grad = grad_wide.astype(jnp.bfloat16)
+        delta = jnp.sum(grad_wide * out_ref[:, here], axis=0, keepdims=True)
+        query_pos, begin = query_geometry(tile, place, starts)
+        score = masked_scores(key_ref[0:reach, :], query, slope, query_pos, begin, 0, reach)
+        prob = jnp.exp(score - lse_ref[:, here])
+        grad_prob = dot_of(value_ref[0:reach, :], grad, 1, 0)
+        grad_score = (prob * (grad_prob - delta)).astype(jnp.bfloat16)
+        key_acc[:, 0:reach] += dot_of(query, grad_score, 1, 1)
+        value_acc[:, 0:reach] += dot_of(grad, prob.astype(jnp.bfloat16), 1, 1)
+        query_grad = dot_of(keys_turned[:, 0:reach], grad_score, 1, 0) * (1.0 / math.sqrt(HDIM))
+        query_grad = query_grad.astype(jnp.bfloat16).astype(jnp.float32)
+        for pair in range(0, SOURCES, 2):
+            index = tile * SOURCES + pair
+            piece = query_grad[:, pair * HALF : (pair + 2) * HALF]
+            pack_pair(send_ref, index, 2 * HDIM, HDIM // 2, piece)
+            other = pltpu.roll(piece, HALF, 1)
+            lane = lax.broadcasted_iota(jnp.int32, piece.shape, 1)
+            mine = lane // HALF == place
+            is_low = place == 0
+            all_ref[0:HDIM, index * block : (index + 1) * block] = jnp.where(
+                mine, jnp.where(is_low, piece, other), 0.0
+            ).astype(jnp.bfloat16)
+            all_ref[0:HDIM, (index + 1) * block : (index + 2) * block] = jnp.where(
+                mine, jnp.where(is_low, other, piece), 0.0
+            ).astype(jnp.bfloat16)
+    all_ref[HDIM : 2 * HDIM, :] = key_acc[...].astype(jnp.bfloat16)
+    all_ref[2 * HDIM :, :] = value_acc[...].astype(jnp.bfloat16)
+    for source in range(count):
+        there = slice(source * block, (source + 1) * block)
+        send_ref[source, 0 : 2 * HDIM, :] = all_ref[HDIM:, there]
+    width = own_ref.shape[1]
+    weight_ref[:, pl.ds(pl.multiple_of(rank * width, width), width)] = jnp.dot(
+        all_ref[...], own_ref[...], preferred_element_type=jnp.float32
+    )
+    weight_ref[:, pl.ds(pl.multiple_of((1 - rank) * width, width), width)] = jnp.dot(
+        all_ref[...], other_ref[...], preferred_element_type=jnp.float32
+    )
+    for index in range(0, count, 2):
+        pack_pair(
+            send_ref,
+            index,
+            SEG_ROW,
+            3 * HDIM // 2,
+            weight_ref[:, index * HALF : (index + 2) * HALF],
+        )
+
+
+def hidden_kernel(recv_ref, w_ref, part_ref, weight_ref, b_ref, acc_ref):
+    step = pl.program_id(0)
+    count = recv_ref.shape[0]
+
+    @pl.when(step == 0)
+    def _():
+        acc_ref[...] = jnp.zeros_like(acc_ref)
+        for index in range(0, count, 2):
+            weight_ref[index // 2] = recv_ref[index, SEG_ROW:, :].astype(jnp.float32) + recv_ref[
+                index + 1, SEG_ROW:, :
+            ].astype(jnp.float32)
+
+    def add(turned):
+        acc_ref[...] += dot_of(turned, w_ref[0], 0, 1)
+        ones = jnp.ones((8, turned.shape[1]), jnp.bfloat16)
+        b_ref[0] = dot_of(ones, turned, 1, 1)
+
+    @pl.when(step == 0)
+    def _():
+        add(heads_of(recv_ref, 2 * HDIM).astype(jnp.bfloat16))
+
+    for which in (1, 2):
+
+        @pl.when(step == which)
+        def _(which=which):
+            span = slice((which - 1) * HDIM, which * HDIM)
+            add(
+                jnp.concatenate(
+                    [
+                        recv_ref[index, span, :].astype(jnp.float32)
+                        + recv_ref[index + 1, span, :].astype(jnp.float32)
+                        for index in range(0, count, 2)
+                    ],
+                    axis=0,
+                ).astype(jnp.bfloat16)
+            )
+
+    @pl.when(step == 2)
+    def _():
+        part_ref[...] = acc_ref[...].astype(jnp.bfloat16)
+
+
+def input_kernel(rank_ref, x_ref, own_ref, other_ref, gain_ref, grad_ref, out_ref, small_ref, wide_ref):
+    rows, width = out_ref.shape
+    own = pl.ds(pl.multiple_of(rank_ref[0] * width, width), width)
+    normed, inverse = norm_stats(both_halves(x_ref, 0, rows).astype(jnp.float32))
+    whole = own_ref[...].astype(jnp.float32) + other_ref[...].astype(jnp.float32)
+    wide_ref[0:1] = jnp.sum(whole * normed, axis=0, keepdims=True)
+    wide_ref[1:2] = jnp.sum(whole, axis=0, keepdims=True)
+    wide_ref[8:, :] = norm_back(whole, normed, inverse, gain_ref[...])
+    small_ref[...] = wide_ref[0:8, own]
+    out_ref[...] = (grad_ref[...] + wide_ref[8:, own]).astype(jnp.bfloat16)
+
+
+def call(kernel, outs, ins, scratch=(), grid=None, in_specs=None, out_specs=None, cost=None):
+    vmem = pl.BlockSpec(memory_space=pltpu.VMEM)
+    smem = pl.BlockSpec(memory_space=pltpu.SMEM)
+    specs = in_specs or [smem if value.ndim == 1 else vmem for value in ins]
+    options = {} if grid is None else {"grid": grid}
+    return pl.pallas_call(
+        kernel,
+        out_shape=[jax.ShapeDtypeStruct(shape, dtype) for shape, dtype in outs],
+        in_specs=specs,
+        out_specs=out_specs or [vmem] * len(outs),
+        scratch_shapes=list(scratch),
+        compiler_params=pltpu.CompilerParams(vmem_limit_bytes=48 * 1024 * 1024),
+        cost_estimate=pl.CostEstimate(
+            flops=cost or 10**8, bytes_accessed=4 * 10**6, transcendentals=0
+        ),
+        **options,
+    )(*ins)
+
+
+def stripes(left, ctx_bits, axis_bits, chosen, value):
+    dims = (left.shape[0],) + (2,) * len(ctx_bits) + (-1,)
+    spread = left.reshape(dims)
+    at = 1 + ctx_bits.index(chosen)
+    kept = lax.dynamic_index_in_dim(spread, value, at, keepdims=False)
+    rest = [bit for bit in ctx_bits if bit != chosen]
+    order = [0] + [1 + rest.index(bit) for bit in axis_bits] + [1 + len(rest)]
+    return jnp.transpose(kept, order).reshape(left.shape[0], -1)
+
+
+def swap_over(value, bit, count):
+    return lax.ppermute(value, "ctx", [(place, place ^ (1 << bit)) for place in range(count)])
+
+
+def reduce_rows(left, right, right_dim, place, count, order, gather):
+    bits = tuple(reversed(range(count.bit_length() - 1)))
+    bit_of = lambda bit: (place >> bit) & 1
+    if gather:
+        first, order = order[0], order[1:]
+        mine = stripes(left, bits, order, first, bit_of(first))
+        theirs = stripes(left, bits, order, first, 1 - bit_of(first))
+        left = jnp.concatenate([mine, swap_over(theirs, first, count)], axis=0)
+        right = jnp.concatenate([right, swap_over(right, first, count)], axis=0)
+        bits = order
+    first, order = order[0], order[1:]
+    send = dot_of(
+        stripes(left, bits, order, first, 1 - bit_of(first)), right, 0, right_dim
+    ).astype(jnp.bfloat16)
+    keep = dot_of(stripes(left, bits, order, first, bit_of(first)), right, 0, right_dim)
+    total = keep + swap_over(send, first, count).astype(jnp.float32)
+    for bit in order:
+        half = total.shape[0] // 2
+        send = lax.dynamic_slice_in_dim(total, (1 - bit_of(bit)) * half, half, 0)
+        keep = lax.dynamic_slice_in_dim(total, bit_of(bit) * half, half, 0)
+        total = keep + swap_over(send.astype(jnp.bfloat16), bit, count).astype(jnp.float32)
+    return total
+
+
+def on_device_paired(
+    tokens,
+    segment_ids,
+    ln1_gain,
+    ln1_bias,
+    w_qkv,
+    b_qv,
+    w_out,
+    b_out,
+    ln2_gain,
+    ln2_bias,
+    w_up,
+    b_up,
+    w_down,
+    b_down,
+    cotangent,
+    count,
+):
+    bf16, f32 = jnp.bfloat16, jnp.float32
+    rows, width = tokens.shape
+    model = w_out.shape[1]
+    hidden = w_up.shape[1]
+    heads = width // HDIM
+    block = 2 * HALF
+    all_tokens = count * rows
+    tp_rank = lax.axis_index("tp")
+    place = lax.axis_index("ctx")
+    rank = tp_rank.reshape(1)
+    side = (place % 2).reshape(1)
+    slope = head_slopes(tp_rank * heads + place // 2, 1)
+    gain_one, bias_one = ln1_gain.reshape(1, model), ln1_bias.reshape(1, model)
+    gain_two, bias_two = ln2_gain.reshape(1, model), ln2_bias.reshape(1, model)
+    other_core = lambda value: lax.ppermute(value, "tp", [(0, 1), (1, 0)])
+    to_heads = lambda value: lax.all_to_all(value, "ctx", 0, 0, tiled=True)
+    smem = pl.BlockSpec(memory_space=pltpu.SMEM)
+    whole = lambda *shape: pl.BlockSpec(shape, lambda step: (0,) * len(shape))
+
+    pair_in = lax.all_gather(jnp.concatenate([tokens, cotangent], axis=0), "tp")
+    b_three = jnp.stack([b_qv[0], jnp.zeros_like(b_qv[0]), b_qv[1]]).reshape(3, 1, width)
+    sent, h_own, _ = call(
+        qkv_kernel,
+        [((count, FWD_ROWS, rows), bf16), ((rows, width), bf16), ((rows, model), bf16)],
+        [rank, pair_in, gain_one, bias_one, w_qkv, b_three, segment_ids.reshape(1, rows)],
+        grid=(3,),
+        in_specs=[
+            smem,
+            whole(2, 2 * rows, width),
+            whole(1, model),
+            whole(1, model),
+            pl.BlockSpec((1, model, width), lambda step: (step, 0, 0)),
+            pl.BlockSpec((1, 1, width), lambda step: (step, 0, 0)),
+            whole(1, rows),
+        ],
+        out_specs=[whole(count, FWD_ROWS, rows), whole(rows, width), whole(rows, model)],
+    )
+    h_all_own = lax.all_gather(h_own, "ctx", axis=0, tiled=True)
+    h_all_other = other_core(h_all_own)
+    got = to_heads(sent)
+    attn_sent, attn_raw, lse = call(
+        forward_kernel,
+        [
+            ((count, HDIM // 2, rows), bf16),
+            ((HDIM, all_tokens // 2), f32),
+            ((1, all_tokens // 2), f32),
+        ],
+        [slope, side, got],
+        scratch=[pltpu.VMEM((all_tokens, HDIM), bf16)],
+    )
+    attn_got = to_heads(attn_sent)
+    part, attn_turned = call(
+        out_kernel,
+        [((rows, model), bf16), ((width, rows), bf16)],
+        [rank, attn_got, w_out, b_out.reshape(1, width)],
+        scratch=[pltpu.VMEM((rows, model), f32)],
+    )
+    chunk = 512
+    middle, h_two, act, grad_pre, grad_b_up, share, swap = call(
+        mlp_kernel,
+        [
+            ((rows, model), f32),
+            ((rows, model), bf16),
+            ((rows, hidden), bf16),
+            ((rows, hidden), bf16),
+            ((1, hidden), f32),
+            ((rows, width), f32),
+            ((rows, model + width), bf16),
+        ],
+        [
+            rank,
+            pair_in,
+            part,
+            other_core(part),
+            gain_two,
+            bias_two,
+            w_up,
+            b_up.reshape(1, hidden),
+            w_down,
+        ],
+        grid=(hidden // chunk,),
+        in_specs=[
+            smem,
+            whole(2, 2 * rows, width),
+            whole(rows, model),
+            whole(rows, model),
+            whole(1, model),
+            whole(1, model),
+            pl.BlockSpec((model, chunk), lambda step: (0, step)),
+            pl.BlockSpec((1, chunk), lambda step: (0, step)),
+            pl.BlockSpec((chunk, model), lambda step: (step, 0)),
+        ],
+        out_specs=[
+            whole(rows, model),
+            whole(rows, model),
+            pl.BlockSpec((rows, chunk), lambda step: (0, step)),
+            pl.BlockSpec((rows, chunk), lambda step: (0, step)),
+            pl.BlockSpec((1, chunk), lambda step: (0, step)),
+            whole(rows, width),
+            whole(rows, model + width),
+        ],
+        scratch=[pltpu.VMEM((rows, model), f32), pltpu.VMEM((rows, model), f32)],
+    )
+    mixed, grad_mid, grad_low, grad_sent, small_two = call(
+        middle_kernel,
+        [
+            ((rows, width), bf16),
+            ((rows, width), f32),
+            ((rows, model), bf16),
+            ((count, HDIM // 2, rows), bf16),
+            ((8, width), f32),
+        ],
+        [
+            rank,
+            pair_in,
+            swap,
+            other_core(swap),
+            middle,
+            share,
+            gain_two,
+            b_down.reshape(1, width),
+            w_out,
+        ],
+        scratch=[pltpu.VMEM((rows + 8, model), f32)],
+    )
+    cot_full = jnp.concatenate([pair_in[0, rows:], pair_in[1, rows:]], axis=1)
+    bit_x, bit_y, bit_z, bit_far = 0, 1, 2, 3
+    grad_down = reduce_rows(
+        cot_full, act, 0, place, count, (bit_x, bit_y, bit_z, bit_far), True
+    )
+    grad_up = reduce_rows(
+        h_two, grad_pre, 0, place, count, (bit_y, bit_x, bit_z, bit_far), True
+    )
+    grad_out = reduce_rows(
+        grad_low, attn_turned, 1, place, count, (bit_x, bit_y, bit_z, bit_far), False
+    )
+    (back_sent,) = call(
+        backward_kernel,
+        [((count, BACK_ROWS, rows), bf16)],
+        [slope, side, rank, got, to_heads(grad_sent), attn_raw, lse, h_all_own, h_all_other],
+        scratch=[
+            pltpu.VMEM((all_tokens, HDIM), bf16),
+            pltpu.VMEM((all_tokens, HDIM), bf16),
+            pltpu.VMEM((HDIM, all_tokens), f32),
+            pltpu.VMEM((HDIM, all_tokens), f32),
+            pltpu.VMEM((3 * HDIM, all_tokens), bf16),
+            pltpu.VMEM((3 * HDIM, model), f32),
+        ],
+    )
+    back_got = to_heads(back_sent)
+    part_one, grad_qkv, sums = call(
+        hidden_kernel,
+        [
+            ((rows, model), bf16),
+            ((heads, BACK_ROWS - SEG_ROW, rows), f32),
+            ((3, 8, width), f32),
+        ],
+        [back_got, w_qkv],
+        grid=(3,),
+        in_specs=[
+            whole(count, BACK_ROWS, rows),
+            pl.BlockSpec((1, model, width), lambda step: (step, 0, 0)),
+        ],
+        out_specs=[
+            whole(rows, model),
+            whole(heads, BACK_ROWS - SEG_ROW, rows),
+            pl.BlockSpec((1, 8, width), lambda step: (step, 0, 0)),
+        ],
+        scratch=[pltpu.VMEM((rows, model), f32)],
+    )
+    input_grad, small_one = call(
+        input_kernel,
+        [((rows, width), bf16), ((8, width), f32)],
+        [rank, pair_in, part_one, other_core(part_one), gain_one, grad_mid],
+        scratch=[pltpu.VMEM((rows + 8, model), f32)],
+    )
+    share_w = width // count
+    vectors = jnp.concatenate(
+        [
+            small_one[0:2].reshape(2, count, share_w),
+            sums[0:3:2, 0].reshape(2, count, share_w),
+            small_two[0:4].reshape(4, count, share_w),
+            grad_b_up.reshape(count, -1, share_w).transpose(1, 0, 2),
+        ],
+        axis=0,
+    )
+    lanes = vectors.shape[0] * share_w
+    spread = vectors.transpose(1, 0, 2).reshape(count, 1, lanes)
+    total = jnp.sum(to_heads(spread), axis=0).reshape(-1, share_w)
+    stripe = model // count
+    grad_qkv = (
+        grad_qkv.reshape(heads, 3 * HDIM // 2, 2, stripe)
+        .transpose(0, 2, 1, 3)
+        .reshape(heads, 3, HDIM, stripe)
+        .transpose(1, 3, 0, 2)
+        .reshape(3, stripe, width)
+    )
+    return (
+        mixed,
+        input_grad,
+        total[0],
+        total[1],
+        grad_qkv,
+        total[2:4],
+        grad_out.T,
+        total[6],
+        total[4],
+        total[5],
+        grad_up,
+        total[8:].reshape(-1),
+        grad_down.T,
+        total[7],
+    )
+
+
+def paired(mesh, arrays):
+    sizes = dict(mesh.shape)
+    count, cores = sizes["ctx"], sizes["tp"]
+    rows = arrays[0].shape[0] // count
+    return (
+        cores == 2
+        and count == 16
+        and rows == 2 * HALF
+        and count * cores == 2 * HEADS
+        and arrays[0].shape[1] == HEADS * HDIM
+    )
+
+
 def solution(mesh):
     in_specs = (
         P("ctx", "tp"),
@@ -419,6 +1146,14 @@
         P("tp", "ctx"),
         P(("tp", "ctx")),
     )
-    return jax.shard_map(
-        on_device, mesh=mesh, in_specs=in_specs, out_specs=out_specs, check_vma=False
-    )
+
+    def run(*arrays):
+        if paired(mesh, arrays):
+            body = functools.partial(on_device_paired, count=dict(mesh.shape)["ctx"])
+        else:
+            body = on_device
+        return jax.shard_map(
+            body, mesh=mesh, in_specs=in_specs, out_specs=out_specs, check_vma=False
+        )(*arrays)
+
+    return run

time: 923 us -> 231 us (0.25)
  waiting for transfers between devices: 448 us -> 69.5 us
  blocking collectives: 212 us -> 15.6 us
  matrix products: 78.8 us -> 8.67 us
  local copies, waits for them, and re-layouts: 93.5 us -> 38 us
  starting transfers between devices: 0.54 us -> 42.7 us
  other arithmetic: 45.9 us -> 11 us
  Pallas kernels: 0 us -> 29.2 us
  loops' own time: 24.3 us -> 0 us
    reduce_scatter x5 -> x0, waiting for transfers between devices: 209 us -> none  [the longest x1 95.4 us: on_device(): lax.psum_scatter(grad_down.astype(jnp.bfloat16), 'ctx', scatter_dimension...]
    all_gather x7 -> x1, blocking collectives: 133 us -> 2.26 us  [on_device_paired(): pair_in = lax.all_gather(jnp.concatenate([tokens, cotangent], axis=0), 'tp')]
    unnamed x15 -> x1, waiting for transfers between devices: 130 us -> 0.68 us
    unnamed x1 -> x0, blocking collectives: 79.3 us -> none
    all_gather x4 -> x1, waiting for transfers between devices: 73.6 us -> 0.01 us  [on_device_paired(): h_all_own = lax.all_gather(h_own, 'ctx', axis=0, tiled=True)]
    dot_general x28 -> x6, matrix products: 78.8 us -> 8.67 us  [dot_of(): lax.dot_general(left, right, (((left_dim,), (right_dim,)), ((), ())), pre...]
    ppermute x0 -> x18, waiting for transfers between devices: none -> 46.3 us  [the longest x14 44.8 us: swap_over(): lax.ppermute(value, 'ctx', [(place, place ^ 1 << bit) for place in range(...]
    psum x2 -> x0, waiting for transfers between devices: 35.1 us -> none  [norm_backward(): lax.psum(part_grad.astype(jnp.bfloat16), 'tp').astype(jnp.float32)]
  transfers between devices with their start and end apart: 13 -> 23, of which waited for: 10 -> 10; matrix products, arithmetic and copies ran while one was open for 19% -> 18% of each run, Pallas kernels for 0% -> 12%
where the time goes in v1:
time: 231 us; the launch traced here: 229 us
  waiting for transfers between devices  69.5 us (30%)
  starting transfers between devices  42.7 us (18%)
  local copies, waits for them, and re-layouts  38 us (16%)
  Pallas kernels  29.2 us (13%)
  blocking collectives  15.6 us (7%)
  between operations  14.7 us (6%)
  other arithmetic  11 us (5%)
  matrix products  8.67 us (4%)
    ppermute x14, waiting for transfers between devices, swap_over(): lax.ppermute(value, 'ctx', [(place, place ^ 1 << bit) for place in range(...  44.8 us
    pallas_call x8, Pallas kernels, call(): pl.pallas_call(kernel, out_shape=[jax.ShapeDtypeStruct(shape, dtype) for...  29.2 us
    all_to_all x4, starting transfers between devices, on_device_paired(): to_heads = lambda value: lax.all_to_all(value, 'ctx', 0, 0, tiled=True)  23.3 us
    all_to_all x4, waiting for transfers between devices, on_device_paired(): to_heads = lambda value: lax.all_to_all(value, 'ctx', 0, 0, tiled=True)  22.4 us
    ppermute x14, starting transfers between devices, swap_over(): lax.ppermute(value, 'ctx', [(place, place ^ 1 << bit) for place in range(...  19.1 us
    all_to_all x1, blocking collectives, on_device_paired(): to_heads = lambda value: lax.all_to_all(value, 'ctx', 0, 0, tiled=True)  13.4 us
    unnamed x83, local copies, waits for them, and re-layouts  13.1 us
    dot_general x6, matrix products, dot_of(): lax.dot_general(left, right, (((left_dim,), (right_dim,)), ((), ())), pre...  8.67 us
  transfers between devices with their start and end apart: 23, of which 10 were waited for; matrix products, arithmetic and copies ran while one was open for 18% of the time, Pallas kernels for 12%

profile of v1, /device:TPU:0, one launch (start us, length us, event | category | flops | bytes accessed | tf_op | source)
XLA Modules:
  0.0 229.3 jit_solution(16882612656163059473)
XLA Ops:
  8.2 2.3 all-gather
  11.4 1.9 copy-done
  15.3 2.6 %shard_map.254 = (bf16[16,176,128]{2,1,0:T(8,128)(2,1)}, bf16[128,512]{1,0:T(8,128)(2,1)}, bf16[128,1024]{1,0:T(8,128)(2,1)}) custom-call(s32[1]{0:T(128)} %bitcast.rank_ref, bf16[2,256,512]{2,1,0:T(8,128)(2,1)S(1)} %bitcast.92, f32[1,1024]{1,0:T(1,128)S(1)} %bitcast.99, f32[1,1024]{1,0:T(1,128)S(1)} %bitcast.102, bf16[3,1024,512]{2,1,0:T(8,128)(2,1)S(1)} %copy-done, ...), custom_call_target="tpu_custom_call" | custom-call | flops 100000000 | bytes 4000000 | tf_op jit(solution)/shard_map/pallas_call | solution.py:817
  17.9 8.4 %all-to-all-start = ((bf16[16,176,128]{2,1,0:T(8,128)(2,1)}), bf16[16,176,128]{2,1,0:T(8,128)(2,1)S(1)}, u32[]{:S(2)}, u32[]{:S(2)}) async-start(bf16[16,176,128]{2,1,0:T(8,128)(2,1)} %get-tuple-element.38), calls=%async_computation | async-start | bytes 1441792 | tf_op jit(solution)/shard_map/all_to_all | solution.py:902
  27.1 18.1 %all-to-all-done.recv_ref = bf16[16,176,128]{2,1,0:T(8,128)(2,1)S(1)} async-done(((bf16[16,176,128]{2,1,0:T(8,128)(2,1)}), bf16[16,176,128]{2,1,0:T(8,128)(2,1)S(1)}, u32[]{:S(2)}, u32[]{:S(2)}) %all-to-all-start) | async-done | bytes 720928 | tf_op jit(solution)/shard_map/all_to_all | solution.py:902
  45.2 3.9 %shard_map.255 = (bf16[16,32,128]{2,1,0:T(8,128)(2,1)S(1)}, f32[64,1024]{1,0:T(8,128)S(1)}, f32[1,1024]{1,0:T(1,128)S(1)}) custom-call(f32[1]{0:T(128)} %bitcast.2.slope_ref, s32[1]{0:T(128)} %bitcast.3.place_ref, bf16[16,176,128]{2,1,0:T(8,128)(2,1)S(1)} %all-to-all-done.recv_ref), custom_call_target="tpu_custom_call" | custom-call | flops 100000000 | bytes 4000000 | tf_op jit(solution)/shard_map/pallas_call | solution.py:817
  49.1 13.4 %all_to_all.25.recv_ref = bf16[16,32,128]{2,1,0:T(8,128)(2,1)S(1)} all-to-all(bf16[16,32,128]{2,1,0:T(8,128)(2,1)S(1)} %get-tuple-element.39), channel_id=1, replica_groups=mesh['ctx'=16,'tp'=2] {'ctx'}, dimensions={0} | all-to-all | bytes 262144 | tf_op jit(solution)/shard_map/all_to_all | solution.py:902
  64.6 8.1 %shard_map.257 = (f32[128,1024]{1,0:T(8,128)S(1)}, bf16[128,1024]{1,0:T(8,128)(2,1)S(1)}, bf16[128,2048]{1,0:T(8,128)(2,1)S(1)}, bf16[128,2048]{1,0:T(8,128)(2,1...) custom-call(s32[1]{0:T(128)} %bitcast.rank_ref, ...), custom_call_target="tpu_custom_call" | custom-call | flops 100000000 | bytes 4000000 | tf_op jit(solution)/shard_map/pallas_call | solution.py:817
  80.4 1.8 copy.77
  84.6 1.8 collective-permute-start.8
  87.5 2.9 %shard_map.258 = (bf16[128,512]{1,0:T(8,128)(2,1)}, f32[128,512]{1,0:T(8,128)S(1)}, bf16[128,1024]{1,0:T(8,128)(2,1)S(1)}, bf16[16,32,128]{2,1,0:T(8,128)(2,1)}, f32[8,512]{1,0:T(8,128)S(1)}) custom-call(s32[1]{0:T(128)} %bitcast.rank_ref, bf16[2,256,512]{2,1,0:T(8,128)(2,1)S(1)} %bitcast.95, bf16[128,1536]{1,0:T(8,128)(2,1)} %get-tuple-element.41.own_ref, ...), custom_call_target="tpu_custom_call" | custom-call | flops 100000000 | bytes 4000000 | tf_op jit(solution)/shard_map/pallas_call | solution.py:817
  91.8 1.8 copy.74
  97.3 1.8 collective-permute-done.8
  103.9 7.2 %collective-permute-done.4 = bf16[512,512]{1,0:T(8,128)(2,1)S(1)} collective-permute-done((bf16[512,512]{1,0:T(8,128)(2,1)S(1)}, bf16[512,512]{1,0:T(8,128)(2,1)S(1)}, u32[]{:S(2)}, u32[]{:S(2)}) %collective-permute-start.4) | collective-permute-done | bytes 524320 | tf_op jit(solution)/shard_map/ppermute | solution.py:842
  113.9 2.7 %convolution_convert_fusion = bf16[256,2048]{1,0:T(8,128)(2,1)} fusion(bf16[256,256]{0,1:T(8,128)(2,1)S(1)} %bitcast.116, bf16[256,2048]{1,0:T(8,128)(2,1)} %copy-done.27), kind=kOutput, calls=%fused_computation.2 | convolution fusion | flops 268959744 | bytes 2228224 | tf_op jit(solution)/shard_map/dot_general | solution.py:429
  120.5 2.2 collective-permute-start.6
  125.7 3.3 %collective-permute-start.7 = (bf16[64,512]{1,0:T(8,128)(2,1)S(1)}, bf16[64,512]{1,0:T(8,128)(2,1)S(1)}, u32[]{:S(2)}, u32[]{:S(2)}) collective-permute-start(bf16[64,512]{1,0:T(8,128)(2,1)S(1)} %dynamic-slice_convert_fusion.6), channel_id=1, source_target_pairs={{0,16},{2,18},{4,20},{6,22},{8,24},{10,26},{12,28},{14,30},{16,0},... | collective-permute-start | bytes 196616 | tf_op jit(solution)/shard_map/ppermute | solution.py:842
  131.5 4.4 %all-to-all-start.2 = ((bf16[16,32,128]{2,1,0:T(8,128)(2,1)}), bf16[16,32,128]{2,1,0:T(8,128)(2,1)S(1)}, u32[]{:S(2)}, u32[]{:S(2)}) async-start(bf16[16,32,128]{2,1,0:T(8,128)(2,1)} %get-tuple-element.45), calls=%async_computation.2 | async-start | bytes 262144 | tf_op jit(solution)/shard_map/all_to_all | solution.py:902
  137.3 6.5 %collective-permute-done.15 = bf16[256,2048]{1,0:T(8,128)(2,1)} collective-permute-done((bf16[256,2048]{1,0:T(8,128)(2,1)}, bf16[256,2048]{1,0:T(8,128)(2,1)}, u32[]{:S(2)}, u32[]{:S(2)}) %collective-permute-start.15) | collective-permute-done | bytes 1048608 | tf_op jit(solution)/shard_map/ppermute | solution.py:842
  143.8 2.1 convolution_add_fusion
  147.4 1.7 collective-permute-start.16
  150.7 8.5 %shard_map.259 = bf16[16,256,128]{2,1,0:T(8,128)(2,1)} custom-call(f32[1]{0:T(128)} %bitcast.2.slope_ref, s32[1]{0:T(128)} %bitcast.3.place_ref, s32[1]{0:T(128)} %bitcast.rank_ref, bf16[16,176,128]{2,1,0:T(8,128)(2,1)S(1)} %all-to-all-done.recv_ref, bf16[16,32,128]{2,1,0:T(8,128)(2,1)S(1)} %all-to-all-done.2.grad_ref, f32[64,1024]{1,0:T(8,128)S(1)} %copy-done.7, ...), custom_call_target="tpu_custom_call" | custom-call | flops 100000000 | bytes 4000000 | tf_op jit(solution)/shard_map/pallas_call | solution.py:817
  159.2 4.7 %all-to-all-start.3 = ((bf16[16,256,128]{2,1,0:T(8,128)(2,1)}), bf16[16,256,128]{2,1,0:T(8,128)(2,1)S(1)}, u32[]{:S(2)}, u32[]{:S(2)}) async-start(bf16[16,256,128]{2,1,0:T(8,128)(2,1)} %shard_map.259), calls=%async_computation.3 | async-start | bytes 2097152 | tf_op jit(solution)/shard_map/all_to_all | solution.py:902
  163.9 1.8 convolution_add_fusion.1
  165.8 2.0 collective-permute-start.11
  169.7 2.4 %collective-permute-start.17 = (bf16[64,2048]{1,0:T(8,128)(2,1)}, bf16[64,2048]{1,0:T(8,128)(2,1)}, u32[]{:S(2)}, u32[]{:S(2)}) collective-permute-start(bf16[64,2048]{1,0:T(8,128)(2,1)} %dynamic-slice_convert_fusion.2), channel_id=1, source_target_pairs={{0,16},{2,18},{4,20},{6,22},{8,24},{10,26},{12,28},{14,30},{16,0},... | collective-permute-start | bytes 786440 | tf_op jit(solution)/shard_map/ppermute | solution.py:842
  172.1 26.5 %collective-permute-done.11 = bf16[128,2048]{1,0:T(8,128)(2,1)S(1)} collective-permute-done((bf16[128,2048]{1,0:T(8,128)(2,1)S(1)}, bf16[128,2048]{1,0:T(8,128)(2,1)S(1)}, u32[]{:S(2)}, u32[]{:S(2)}) %collective-permute-start.11) | collective-permute-done | bytes 524320 | tf_op jit(solution)/shard_map/ppermute | solution.py:842
  199.9 1.9 copy-done.1
  203.4 1.8 add_bitcast_fusion
  207.4 5.8 %all-to-all-start.4 = ((f32[16,1,384]{2,1,0:T(1,128)}), f32[16,1,384]{2,1,0:T(1,128)S(1)}, u32[]{:S(2)}, u32[]{:S(2)}) async-start(f32[16,1,384]{2,1,0:T(1,128)} %reshape.192), calls=%async_computation.4 | async-start | bytes 49152 | tf_op jit(solution)/shard_map/all_to_all | solution.py:902
  213.2 1.8 convert_add_fusion.3
  216.8 3.8 %all-to-all-done.4 = f32[16,1,384]{2,1,0:T(1,128)S(1)} async-done(((f32[16,1,384]{2,1,0:T(1,128)}), f32[16,1,384]{2,1,0:T(1,128)S(1)}, u32[]{:S(2)}, u32[]{:S(2)}) %all-to-all-start.4) | async-done | bytes 24608 | tf_op jit(solution)/shard_map/all_to_all | solution.py:902
  (176 shorter events, 54.9 us)
Async XLA Ops:
  17.9 44.6 %copy-start.2 = (bf16[512,1024]{1,0:T(8,128)(2,1)S(1)}, bf16[512,1024]{1,0:T(8,128)(2,1)}, u32[]{:S(2)}) copy-start(bf16[512,1024]{1,0:T(8,128)(2,1)} %w_out_ref.1) | copy-start | bytes 3145732
  17.9 44.6 %copy-start.20 = (f32[512]{0:T(512)S(1)}, f32[512]{0:T(512)}, u32[]{:S(2)}) copy-start(f32[512]{0:T(512)} %param.22) | copy-start | bytes 6148
  17.9 46.7 %copy-start.14 = (f32[1024]{0:T(1024)S(1)}, f32[1024]{0:T(1024)}, u32[]{:S(2)}) copy-start(f32[1024]{0:T(1024)} %param.23) | copy-start | bytes 12292
  17.9 46.7 %copy-start.17 = (f32[2048]{0:T(1024)S(1)}, f32[2048]{0:T(1024)}, u32[]{:S(2)}) copy-start(f32[2048]{0:T(1024)} %param.26) | copy-start | bytes 24580
  17.9 46.7 %copy-start.19 = (f32[1024]{0:T(1024)S(1)}, f32[1024]{0:T(1024)}, u32[]{:S(2)}) copy-start(f32[1024]{0:T(1024)} %param.24) | copy-start | bytes 12292
  17.9 27.3 %all-to-all-start = ((bf16[16,176,128]{2,1,0:T(8,128)(2,1)}), bf16[16,176,128]{2,1,0:T(8,128)(2,1)S(1)}, u32[]{:S(2)}, u32[]{:S(2)}) async-start(bf16[16,176,128]{2,1,0:T(8,128)(2,1)} %get-tuple-element.38), calls=%async_computation | async-start | bytes 1441792 | tf_op jit(solution)/shard_map/all_to_all | solution.py:902
  26.3 87.6 %all-gather.3.cloned.1.call-start = ((), (), s32[]{:S(2)}) async-start(), calls=%async_computation.5 | async-start | bytes 2228224 | tf_op jit(solution)/shard_map/all_gather | solution.py:924
  49.1 13.4 %copy-start.6 = (f32[64,1024]{1,0:T(8,128)}, f32[64,1024]{1,0:T(8,128)S(1)}, u32[]{:S(2)}) copy-start(f32[64,1024]{1,0:T(8,128)S(1)} %get-tuple-element.46.out_ref) | copy-start | bytes 786436
  63.0 1.6 collective-permute-start
  74.9 12.6 %collective-permute-start.1 = (bf16[128,1536]{1,0:T(8,128)(2,1)}, bf16[128,1536]{1,0:T(8,128)(2,1)}, u32[]{:S(2)}, u32[]{:S(2)}) collective-permute-start(bf16[128,1536]{1,0:T(8,128)(2,1)} %get-tuple-element.41.own_ref), channel_id=1, source_target_pairs={{0,1},{1,0},{2,3},{3,2},{4,5},{5,4},{6,7},{7,6},{8,9},{9,8},{10,11... | collective-permute-start | bytes 1179656 | tf_op jit(solution)/shard_map/ppermute | solution.py:901
  79.0 23.7 %collective-permute-start.14 = (bf16[128,2048]{1,0:T(8,128)(2,1)S(1)}, bf16[128,2048]{1,0:T(8,128)(2,1)}, u32[]{:S(2)}, u32[]{:S(2)}) collective-permute-start(bf16[128,2048]{1,0:T(8,128)(2,1)S(1)} %get-tuple-element.61), channel_id=1, source_target_pairs={{0,2},{2,0},{4,6},{6,4},{8,10},{10,8},{12,14},{14,12},{16,18},{18,... | collective-permute-start | bytes 1572872 | tf_op jit(solution)/shard_map/ppermute | solution.py:842
  80.1 37.8 %collective-permute-start.9 = (bf16[128,2048]{1,0:T(8,128)(2,1)S(1)}, bf16[128,2048]{1,0:T(8,128)(2,1)}, u32[]{:S(2)}, u32[]{:S(2)}) collective-permute-start(bf16[128,2048]{1,0:T(8,128)(2,1)S(1)} %get-tuple-element.60), channel_id=1, source_target_pairs={{0,4},{2,6},{4,0},{6,2},{8,12},{10,14},{12,8},{14,10},{16,20},{18,... | collective-permute-start | bytes 1572872 | tf_op jit(solution)/shard_map/ppermute | solution.py:842
  84.6 14.5 %collective-permute-start.8 = (bf16[128,512]{0,1:T(8,128)(2,1)}, bf16[128,512]{0,1:T(8,128)(2,1)}, u32[]{:S(2)}, u32[]{:S(2)}) collective-permute-start(bf16[128,512]{0,1:T(8,128)(2,1)} %bitcast.36), channel_id=1, source_target_pairs={{0,4},{2,6},{4,0},{6,2},{8,12},{10,14},{12,8},{14,10},{16,20},{18,... | collective-permute-start | bytes 393224 | tf_op jit(solution)/shard_map/ppermute | solution.py:842
  94.8 6.5 %collective-permute-start.13 = (bf16[128,512]{0,1:T(8,128)(2,1)S(1)}, bf16[128,512]{0,1:T(8,128)(2,1)S(1)}, u32[]{:S(2)}, u32[]{:S(2)}) collective-permute-start(bf16[128,512]{0,1:T(8,128)(2,1)S(1)} %bitcast.120), channel_id=1, source_target_pairs={{0,2},{2,0},{4,6},{6,4},{8,10},{10,8},{12,14},{14,12},{16,18},{18,... | collective-permute-start | bytes 393224 | tf_op jit(solution)/shard_map/ppermute | solution.py:842
  96.2 14.9 %collective-permute-start.4 = (bf16[512,512]{1,0:T(8,128)(2,1)S(1)}, bf16[512,512]{1,0:T(8,128)(2,1)S(1)}, u32[]{:S(2)}, u32[]{:S(2)}) collective-permute-start(bf16[512,512]{1,0:T(8,128)(2,1)S(1)} %convolution_convert_fusion.2), channel_id=1, source_target_pairs={{0,2},{2,0},{4,6},{6,4},{8,10},{10,8},{12,14},{14,12},{16,18},{18,... | collective-permute-start | bytes 1572872 | tf_op jit(solution)/shard_map/ppermute | solution.py:842
  113.1 7.2 %collective-permute-start.5 = (bf16[256,512]{1,0:T(8,128)(2,1)}, bf16[256,512]{1,0:T(8,128)(2,1)S(1)}, u32[]{:S(2)}, u32[]{:S(2)}) collective-permute-start(bf16[256,512]{1,0:T(8,128)(2,1)} %dynamic-slice_convert_fusion.4), channel_id=1, source_target_pairs={{0,4},{2,6},{4,0},{6,2},{8,12},{10,14},{12,8},{14,10},{16,20},{18,... | collective-permute-start | bytes 786440 | tf_op jit(solution)/shard_map/ppermute | solution.py:842
  113.9 35.8 %collective-permute-start.2 = (bf16[2048,512]{1,0:T(8,128)(2,1)}, bf16[2048,512]{1,0:T(8,128)(2,1)}, u32[]{:S(2)}, u32[]{:S(2)}) collective-permute-start(bf16[2048,512]{1,0:T(8,128)(2,1)} %all-gather.3.cloned.1.call-done.own_ref), channel_id=1, source_target_pairs={{0,1},{1,0},{2,3},{3,2},{4,5},{5,4},{6,7},{7,6},{8,9},{9,8},{10,11... | collective-permute-start | bytes 6291464 | tf_op jit(solution)/shard_map/ppermute | solution.py:901
  116.7 27.1 %collective-permute-start.15 = (bf16[256,2048]{1,0:T(8,128)(2,1)}, bf16[256,2048]{1,0:T(8,128)(2,1)}, u32[]{:S(2)}, u32[]{:S(2)}) collective-permute-start(bf16[256,2048]{1,0:T(8,128)(2,1)} %convolution_convert_fusion), channel_id=1, source_target_pairs={{0,4},{2,6},{4,0},{6,2},{8,12},{10,14},{12,8},{14,10},{16,20},{18,... | collective-permute-start | bytes 3145736 | tf_op jit(solution)/shard_map/ppermute | solution.py:842
  119.0 11.8 %copy-start.37 = (bf16[256,1,2,2,64]{0,4,1,2,3:T(8,128)(2,1)S(1)}, bf16[256,1,2,2,64]{0,4,1,2,3:T(8,128)(2,1)}, u32[]{:S(2)}) copy-start(bf16[256,1,2,2,64]{0,4,1,2,3:T(8,128)(2,1)} %get-tuple-element.69) | copy-start | bytes 393220
  120.4 16.2 %copy-start.38 = (bf16[256,1,2,2,64]{0,4,1,2,3:T(8,128)(2,1)S(1)}, bf16[256,1,2,2,64]{0,4,1,2,3:T(8,128)(2,1)}, u32[]{:S(2)}) copy-start(bf16[256,1,2,2,64]{0,4,1,2,3:T(8,128)(2,1)} %get-tuple-element.65) | copy-start | bytes 393220
  120.5 5.1 %collective-permute-start.6 = (bf16[128,512]{1,0:T(8,128)(2,1)S(1)}, bf16[128,512]{1,0:T(8,128)(2,1)S(1)}, u32[]{:S(2)}, u32[]{:S(2)}) collective-permute-start(bf16[128,512]{1,0:T(8,128)(2,1)S(1)} %dynamic-slice_convert_fusion.5), channel_id=1, source_target_pairs={{0,8},{2,10},{4,12},{6,14},{8,0},{10,2},{12,4},{14,6},{16,24},{18,... | collective-permute-start | bytes 393224 | tf_op jit(solution)/shard_map/ppermute | solution.py:842
  124.1 39.8 %collective-permute-start.10 = (bf16[256,2048]{1,0:T(8,128)(2,1)}, bf16[256,2048]{1,0:T(8,128)(2,1)}, u32[]{:S(2)}, u32[]{:S(2)}) collective-permute-start(bf16[256,2048]{1,0:T(8,128)(2,1)} %convolution_convert_fusion.1), channel_id=1, source_target_pairs={{0,2},{2,0},{4,6},{6,4},{8,10},{10,8},{12,14},{14,12},{16,18},{18,... | collective-permute-start | bytes 3145736 | tf_op jit(solution)/shard_map/ppermute | solution.py:842
  125.7 11.0 %collective-permute-start.7 = (bf16[64,512]{1,0:T(8,128)(2,1)S(1)}, bf16[64,512]{1,0:T(8,128)(2,1)S(1)}, u32[]{:S(2)}, u32[]{:S(2)}) collective-permute-start(bf16[64,512]{1,0:T(8,128)(2,1)S(1)} %dynamic-slice_convert_fusion.6), channel_id=1, source_target_pairs={{0,16},{2,18},{4,20},{6,22},{8,24},{10,26},{12,28},{14,30},{16,0},... | collective-permute-start | bytes 196616 | tf_op jit(solution)/shard_map/ppermute | solution.py:842
  131.5 18.2 %all-to-all-start.2 = ((bf16[16,32,128]{2,1,0:T(8,128)(2,1)}), bf16[16,32,128]{2,1,0:T(8,128)(2,1)S(1)}, u32[]{:S(2)}, u32[]{:S(2)}) async-start(bf16[16,32,128]{2,1,0:T(8,128)(2,1)} %get-tuple-element.45), calls=%async_computation.2 | async-start | bytes 262144 | tf_op jit(solution)/shard_map/all_to_all | solution.py:902
  147.4 20.4 %collective-permute-start.16 = (bf16[128,2048]{1,0:T(8,128)(2,1)}, bf16[128,2048]{1,0:T(8,128)(2,1)}, u32[]{:S(2)}, u32[]{:S(2)}) collective-permute-start(bf16[128,2048]{1,0:T(8,128)(2,1)} %dynamic-slice_convert_fusion), channel_id=1, source_target_pairs={{0,8},{2,10},{4,12},{6,14},{8,0},{10,2},{12,4},{14,6},{16,24},{18,... | collective-permute-start | bytes 1572872 | tf_op jit(solution)/shard_map/ppermute | solution.py:842
  159.2 40.7 %all-to-all-start.3 = ((bf16[16,256,128]{2,1,0:T(8,128)(2,1)}), bf16[16,256,128]{2,1,0:T(8,128)(2,1)S(1)}, u32[]{:S(2)}, u32[]{:S(2)}) async-start(bf16[16,256,128]{2,1,0:T(8,128)(2,1)} %shard_map.259), calls=%async_computation.3 | async-start | bytes 2097152 | tf_op jit(solution)/shard_map/all_to_all | solution.py:902
  165.8 32.9 %collective-permute-start.11 = (bf16[128,2048]{1,0:T(8,128)(2,1)S(1)}, bf16[128,2048]{1,0:T(8,128)(2,1)S(1)}, u32[]{:S(2)}, u32[]{:S(2)}) collective-permute-start(bf16[128,2048]{1,0:T(8,128)(2,1)S(1)} %dynamic-slice_convert_fusion.1), channel_id=1, source_target_pairs={{0,8},{2,10},{4,12},{6,14},{8,0},{10,2},{12,4},{14,6},{16,24},{18,... | collective-permute-start | bytes 1572872 | tf_op jit(solution)/shard_map/ppermute | solution.py:842
  168.9 30.6 %copy-start.32 = (f32[128,2048]{1,0:T(8,128)}, f32[128,2048]{1,0:T(8,128)S(1)}, u32[]{:S(2)}) copy-start(f32[128,2048]{1,0:T(8,128)S(1)} %convert_add_fusion) | copy-start | bytes 3145732
  169.7 33.7 %collective-permute-start.17 = (bf16[64,2048]{1,0:T(8,128)(2,1)}, bf16[64,2048]{1,0:T(8,128)(2,1)}, u32[]{:S(2)}, u32[]{:S(2)}) collective-permute-start(bf16[64,2048]{1,0:T(8,128)(2,1)} %dynamic-slice_convert_fusion.2), channel_id=1, source_target_pairs={{0,16},{2,18},{4,20},{6,22},{8,24},{10,26},{12,28},{14,30},{16,0},... | collective-permute-start | bytes 786440 | tf_op jit(solution)/shard_map/ppermute | solution.py:842
  199.6 13.7 %collective-permute-start.12 = (bf16[64,2048]{1,0:T(8,128)(2,1)}, bf16[64,2048]{1,0:T(8,128)(2,1)}, u32[]{:S(2)}, u32[]{:S(2)}) collective-permute-start(bf16[64,2048]{1,0:T(8,128)(2,1)} %dynamic-slice_convert_fusion.3), channel_id=1, source_target_pairs={{0,16},{2,18},{4,20},{6,22},{8,24},{10,26},{12,28},{14,30},{16,0},... | collective-permute-start | bytes 786440 | tf_op jit(solution)/shard_map/ppermute | solution.py:842
  203.3 2.0 collective-permute-start.3
  207.4 13.2 %all-to-all-start.4 = ((f32[16,1,384]{2,1,0:T(1,128)}), f32[16,1,384]{2,1,0:T(1,128)S(1)}, u32[]{:S(2)}, u32[]{:S(2)}) async-start(f32[16,1,384]{2,1,0:T(1,128)} %reshape.192), calls=%async_computation.4 | async-start | bytes 49152 | tf_op jit(solution)/shard_map/all_to_all | solution.py:902
  (32 other events, 132.0 us)
Sparse Core Ops, SparseCore 0:
  30.5 65.9 all-gather.2

commit v2 on v1

--- a/solution.py
+++ b/solution.py
@@ -21,9 +21,12 @@
 QUERIES = SOURCES * HALF
 SEG_ROW = 5 * HDIM // 2
 FWD_ROWS = SEG_ROW + 16
-BACK_ROWS = SEG_ROW + 3 * HDIM // 2
 GELU_A = math.sqrt(2.0 / math.pi)
 GELU_B = 0.044715
+
+DOWN_BITS = (0, 1, 2, 3)
+UP_BITS = (2, 0, 1, 3)
+GATHERED = (0, 8, 4, 12, 1, 9, 5, 13, 2, 10, 6, 14, 3, 11, 7, 15)
 
 
 def head_slopes(first_head, head_count):
@@ -418,32 +421,69 @@
     ref[index + 1, first_row : first_row + count, :] = two.astype(ref.dtype)
 
 
-def both_halves(ref, first_row, count):
-    return jnp.concatenate(
-        [ref[0, first_row : first_row + count, :], ref[1, first_row : first_row + count, :]],
-        axis=1,
-    )
-
-
 def dot_of(left, right, left_dim, right_dim):
     return lax.dot_general(
         left, right, (((left_dim,), (right_dim,)), ((), ())), preferred_element_type=jnp.float32
     )
 
 
-def qkv_kernel(rank_ref, x_ref, gain_ref, bias_ref, w_ref, b_ref, seg_ref, send_ref, own_ref, h_ref):
+def put_halves(ref, rank, own_ref, other_ref):
+    width = own_ref.shape[1]
+    ref[:, pl.ds(pl.multiple_of(rank * width, width), width)] = own_ref[...]
+    ref[:, pl.ds(pl.multiple_of((1 - rank) * width, width), width)] = other_ref[...]
+
+
+def put_stripes(ref, first_lane, turned_ref, chosen, order, value):
+    side = 2 * HALF
+    for number in range(1 << len(order)):
+        source = 0
+        for depth, bit in enumerate(order):
+            source |= ((number >> (len(order) - 1 - depth)) & 1) << bit
+        start = pl.multiple_of((source + (value << chosen)) * HALF, HALF)
+        row, lane = (number * HALF) % side, first_lane + (number * HALF) // side * side
+        ref[row : row + HALF, lane : lane + side] = turned_ref[pl.ds(start, HALF), :]
+
+
+def qkv_kernel(
+    rank_ref,
+    place_ref,
+    x_own_ref,
+    x_other_ref,
+    cot_own_ref,
+    cot_other_ref,
+    gain_ref,
+    bias_ref,
+    w_ref,
+    b_ref,
+    seg_ref,
+    send_ref,
+    x_ref,
+    cot_ref,
+    mine_ref,
+    theirs_ref,
+    h_ref,
+    turn_ref,
+):
     step = pl.program_id(0)
-    rows = own_ref.shape[0]
-    width = own_ref.shape[1]
+    rows, width = x_own_ref.shape
     heads = width // HDIM
 
     @pl.when(step == 0)
     def _():
-        normed, _ = norm_stats(both_halves(x_ref, 0, rows).astype(jnp.float32))
+        put_halves(x_ref, rank_ref[0], x_own_ref, x_other_ref)
+        normed, _ = norm_stats(x_ref[...].astype(jnp.float32))
         h_ref[...] = (normed * gain_ref[...] + bias_ref[...]).astype(jnp.bfloat16)
-        own_ref[...] = h_ref[:, pl.ds(pl.multiple_of(rank_ref[0] * width, width), width)]
-
-    flat = jnp.dot(h_ref[...], w_ref[0], preferred_element_type=jnp.float32) + b_ref[0]
+
+    @pl.when(step == 2)
+    def _():
+        put_halves(cot_ref, rank_ref[0], cot_own_ref, cot_other_ref)
+        turn_ref[...] = cot_ref[...].astype(jnp.float32).T.astype(jnp.bfloat16)
+        bit = (place_ref[0] >> DOWN_BITS[0]) & 1
+        put_stripes(mine_ref, 0, turn_ref, DOWN_BITS[0], DOWN_BITS[1:], bit)
+        put_stripes(theirs_ref, 0, turn_ref, DOWN_BITS[0], DOWN_BITS[1:], 1 - bit)
+
+    bias = jnp.where(step == 0, b_ref[0:1], jnp.where(step == 2, b_ref[1:2], 0.0))
+    flat = jnp.dot(h_ref[...], w_ref[0], preferred_element_type=jnp.float32) + bias
     turned = flat.T
 
     @pl.when(step == 0)
@@ -503,7 +543,28 @@
     )
 
 
-def forward_kernel(slope_ref, place_ref, recv_ref, send_ref, out_ref, lse_ref, key_ref):
+def put_rows(ref, *pieces):
+    first = 0
+    for piece in pieces:
+        ref[first : first + piece.shape[0], :] = piece[...]
+        first += piece.shape[0]
+
+
+def forward_kernel(
+    slope_ref,
+    place_ref,
+    recv_ref,
+    tokens_ref,
+    far_ref,
+    near_ref,
+    corner_ref,
+    send_ref,
+    out_ref,
+    lse_ref,
+    joined_ref,
+    key_ref,
+):
+    put_rows(joined_ref, tokens_ref, far_ref, near_ref, corner_ref)
     count = recv_ref.shape[0]
     block = 2 * HALF
     slope, place = slope_ref[0], place_ref[0]
@@ -564,7 +625,9 @@
 
 def mlp_kernel(
     rank_ref,
+    place_ref,
     x_ref,
+    cot_ref,
     own_ref,
     other_ref,
     gain_ref,
@@ -573,12 +636,14 @@
     b_up_ref,
     down_ref,
     middle_ref,
-    hidden_ref,
     act_ref,
     back_ref,
+    mine_ref,
     b_grad_ref,
     share_ref,
     swap_ref,
+    hidden_ref,
+    turn_ref,
     grad_acc,
     mlp_acc,
 ):
@@ -589,13 +654,18 @@
     @pl.when(step == 0)
     def _():
         middle = (
-            both_halves(x_ref, 0, rows).astype(jnp.float32)
+            x_ref[...].astype(jnp.float32)
             + own_ref[...].astype(jnp.float32)
             + other_ref[...].astype(jnp.float32)
         )
         middle_ref[...] = middle
         normed, _ = norm_stats(middle.astype(jnp.bfloat16).astype(jnp.float32))
         hidden_ref[...] = (normed * gain_ref[...] + bias_ref[...]).astype(jnp.bfloat16)
+        turn_ref[...] = hidden_ref[...].astype(jnp.float32).T.astype(jnp.bfloat16)
+        bit = (place_ref[0] >> UP_BITS[0]) & 1
+        put_stripes(mine_ref, 0, turn_ref, UP_BITS[0], UP_BITS[1:], bit)
+        first = back_ref.shape[1] - mine_ref.shape[1]
+        put_stripes(back_ref, first, turn_ref, UP_BITS[0], UP_BITS[1:], 1 - bit)
         grad_acc[...] = jnp.zeros_like(grad_acc)
         mlp_acc[...] = jnp.zeros_like(mlp_acc)
 
@@ -603,9 +673,10 @@
     act, slope = gelu_pair(pre)
     act = act.astype(jnp.bfloat16)
     act_ref[...] = act
-    grad_act = dot_of(both_halves(x_ref, rows, rows), down_ref[...], 1, 1)
+    grad_act = dot_of(cot_ref[...], down_ref[...], 1, 1)
     grad_pre = (grad_act * slope).astype(jnp.bfloat16)
-    back_ref[...] = grad_pre
+    chunk = grad_pre.shape[1]
+    back_ref[:, pl.ds(pl.multiple_of(step * chunk, chunk), chunk)] = grad_pre
     b_grad_ref[...] = jnp.sum(grad_pre.astype(jnp.float32), axis=0, keepdims=True)
     grad_acc[...] += dot_of(grad_pre, up_ref[...], 1, 1)
     mlp_acc[...] += jnp.dot(act, down_ref[...], preferred_element_type=jnp.float32)
@@ -629,7 +700,8 @@
 
 def middle_kernel(
     rank_ref,
-    x_ref,
+    place_ref,
+    cot_ref,
     own_ref,
     other_ref,
     middle_ref,
@@ -637,14 +709,20 @@
     gain_ref,
     b_down_ref,
     w_out_ref,
+    line_ref,
+    line_x_ref,
     mixed_ref,
     grad_ref,
-    low_ref,
     send_ref,
+    mine_ref,
+    theirs_ref,
     small_ref,
+    joined_ref,
     wide_ref,
+    turn_ref,
 ):
     rows, width = mixed_ref.shape
+    put_rows(joined_ref, line_ref, line_x_ref)
     own = pl.ds(pl.multiple_of(rank_ref[0] * width, width), width)
     mixed_ref[...] = (
         middle_ref[:, own]
@@ -656,10 +734,13 @@
         jnp.float32
     )
     normed, inverse = norm_stats(middle_ref[...].astype(jnp.bfloat16).astype(jnp.float32))
-    cot = both_halves(x_ref, rows, rows).astype(jnp.float32)
+    cot = cot_ref[...].astype(jnp.float32)
     grad = cot + norm_back(whole, normed, inverse, gain_ref[...])
     low = grad.astype(jnp.bfloat16)
-    low_ref[...] = low
+    turn_ref[...] = grad.T.astype(jnp.bfloat16)
+    bit = (place_ref[0] >> UP_BITS[0]) & 1
+    put_stripes(mine_ref, 0, turn_ref, UP_BITS[0], UP_BITS[1:], bit)
+    put_stripes(theirs_ref, 0, turn_ref, UP_BITS[0], UP_BITS[1:], 1 - bit)
     wide_ref[0:1] = jnp.sum(whole * normed, axis=0, keepdims=True)
     wide_ref[1:2] = jnp.sum(whole, axis=0, keepdims=True)
     wide_ref[2:3] = jnp.sum(grad, axis=0, keepdims=True)
@@ -675,24 +756,20 @@
 def backward_kernel(
     slope_ref,
     place_ref,
-    rank_ref,
     recv_ref,
     grad_ref,
     out_ref,
     lse_ref,
-    own_ref,
-    other_ref,
     send_ref,
+    low_ref,
     key_ref,
     value_ref,
     key_acc,
     value_acc,
-    all_ref,
-    weight_ref,
 ):
     count = recv_ref.shape[0]
     block = 2 * HALF
-    slope, place, rank = slope_ref[0], place_ref[0], rank_ref[0]
+    slope, place = slope_ref[0], place_ref[0]
     starts = doc_starts(recv_ref)
     for source in range(count):
         there = slice(source * block, (source + 1) * block)
@@ -727,45 +804,57 @@
             lane = lax.broadcasted_iota(jnp.int32, piece.shape, 1)
             mine = lane // HALF == place
             is_low = place == 0
-            all_ref[0:HDIM, index * block : (index + 1) * block] = jnp.where(
+            low_ref[0:HDIM, index * block : (index + 1) * block] = jnp.where(
                 mine, jnp.where(is_low, piece, other), 0.0
             ).astype(jnp.bfloat16)
-            all_ref[0:HDIM, (index + 1) * block : (index + 2) * block] = jnp.where(
+            low_ref[0:HDIM, (index + 1) * block : (index + 2) * block] = jnp.where(
                 mine, jnp.where(is_low, other, piece), 0.0
             ).astype(jnp.bfloat16)
-    all_ref[HDIM : 2 * HDIM, :] = key_acc[...].astype(jnp.bfloat16)
-    all_ref[2 * HDIM :, :] = value_acc[...].astype(jnp.bfloat16)
+    low_ref[HDIM : 2 * HDIM, :] = key_acc[...].astype(jnp.bfloat16)
+    low_ref[2 * HDIM :, :] = value_acc[...].astype(jnp.bfloat16)
     for source in range(count):
         there = slice(source * block, (source + 1) * block)
-        send_ref[source, 0 : 2 * HDIM, :] = all_ref[HDIM:, there]
-    width = own_ref.shape[1]
-    weight_ref[:, pl.ds(pl.multiple_of(rank * width, width), width)] = jnp.dot(
-        all_ref[...], own_ref[...], preferred_element_type=jnp.float32
-    )
-    weight_ref[:, pl.ds(pl.multiple_of((1 - rank) * width, width), width)] = jnp.dot(
-        all_ref[...], other_ref[...], preferred_element_type=jnp.float32
-    )
-    for index in range(0, count, 2):
+        send_ref[source, 0 : 2 * HDIM, :] = low_ref[HDIM:, there]
+
+
+def weight_kernel(
+    rank_ref, device_ref, gain_ref, bias_ref, grad_ref, *refs
+):
+    own_refs, other_refs = refs[:2], refs[2:4]
+    send_ref, wide_ref, order_ref, acc_ref = refs[4:]
+    block = 2 * HALF
+    first = 0
+    for own_ref, other_ref in zip(own_refs, other_refs):
+        put_halves(wide_ref.at[first : first + own_ref.shape[0]], rank_ref[0], own_ref, other_ref)
+        first += own_ref.shape[0]
+    for position, code in enumerate(GATHERED):
+        source = device_ref[0] ^ code
+        order_ref[:, position * block : (position + 1) * block] = grad_ref[
+            :, pl.ds(pl.multiple_of(source * block, block), block)
+        ]
+    acc_ref[...] = jnp.zeros_like(acc_ref)
+
+    def add(step, carry):
+        here = pl.ds(pl.multiple_of(step * 2 * block, 2 * block), 2 * block)
+        normed, _ = norm_stats(wide_ref[here, :].astype(jnp.float32))
+        hidden = (normed * gain_ref[...] + bias_ref[...]).astype(jnp.bfloat16)
+        acc_ref[...] += jnp.dot(order_ref[:, here], hidden, preferred_element_type=jnp.float32)
+        return carry
+
+    lax.fori_loop(0, first // (2 * block), add, 0)
+    for index in range(0, send_ref.shape[0], 2):
         pack_pair(
-            send_ref,
-            index,
-            SEG_ROW,
-            3 * HDIM // 2,
-            weight_ref[:, index * HALF : (index + 2) * HALF],
+            send_ref, index, 0, 3 * HDIM // 2, acc_ref[:, index * HALF : (index + 2) * HALF]
         )
 
 
-def hidden_kernel(recv_ref, w_ref, part_ref, weight_ref, b_ref, acc_ref):
+def hidden_kernel(recv_ref, w_ref, part_ref, b_ref, acc_ref):
     step = pl.program_id(0)
     count = recv_ref.shape[0]
 
     @pl.when(step == 0)
     def _():
         acc_ref[...] = jnp.zeros_like(acc_ref)
-        for index in range(0, count, 2):
-            weight_ref[index // 2] = recv_ref[index, SEG_ROW:, :].astype(jnp.float32) + recv_ref[
-                index + 1, SEG_ROW:, :
-            ].astype(jnp.float32)
 
     def add(turned):
         acc_ref[...] += dot_of(turned, w_ref[0], 0, 1)
@@ -800,7 +889,7 @@
 def input_kernel(rank_ref, x_ref, own_ref, other_ref, gain_ref, grad_ref, out_ref, small_ref, wide_ref):
     rows, width = out_ref.shape
     own = pl.ds(pl.multiple_of(rank_ref[0] * width, width), width)
-    normed, inverse = norm_stats(both_halves(x_ref, 0, rows).astype(jnp.float32))
+    normed, inverse = norm_stats(x_ref[...].astype(jnp.float32))
     whole = own_ref[...].astype(jnp.float32) + other_ref[...].astype(jnp.float32)
     wide_ref[0:1] = jnp.sum(whole * normed, axis=0, keepdims=True)
     wide_ref[1:2] = jnp.sum(whole, axis=0, keepdims=True)
@@ -809,61 +898,218 @@
     out_ref[...] = (grad_ref[...] + wide_ref[8:, own]).astype(jnp.bfloat16)
 
 
-def call(kernel, outs, ins, scratch=(), grid=None, in_specs=None, out_specs=None, cost=None):
+def call(
+    kernel,
+    outs,
+    ins,
+    scratch=(),
+    grid=None,
+    in_specs=None,
+    out_specs=None,
+    after=(),
+    mebibytes=16,
+    flops=10**8,
+):
     vmem = pl.BlockSpec(memory_space=pltpu.VMEM)
     smem = pl.BlockSpec(memory_space=pltpu.SMEM)
-    specs = in_specs or [smem if value.ndim == 1 else vmem for value in ins]
+    specs = list(in_specs or [smem if value.ndim == 1 else vmem for value in ins])
     options = {} if grid is None else {"grid": grid}
+    taken = len(ins)
+    waits = len(after)
+
+    def body(*refs):
+        kernel(*refs[:taken], *refs[taken + waits :])
+
     return pl.pallas_call(
-        kernel,
+        body,
         out_shape=[jax.ShapeDtypeStruct(shape, dtype) for shape, dtype in outs],
-        in_specs=specs,
+        in_specs=specs + [pl.BlockSpec(memory_space=pl.ANY)] * waits,
         out_specs=out_specs or [vmem] * len(outs),
         scratch_shapes=list(scratch),
-        compiler_params=pltpu.CompilerParams(vmem_limit_bytes=48 * 1024 * 1024),
+        compiler_params=pltpu.CompilerParams(vmem_limit_bytes=mebibytes * 1024 * 1024),
         cost_estimate=pl.CostEstimate(
-            flops=cost or 10**8, bytes_accessed=4 * 10**6, transcendentals=0
+            flops=flops // 10**4, bytes_accessed=1024, transcendentals=0
         ),
         **options,
-    )(*ins)
-
-
-def stripes(left, ctx_bits, axis_bits, chosen, value):
-    dims = (left.shape[0],) + (2,) * len(ctx_bits) + (-1,)
-    spread = left.reshape(dims)
-    at = 1 + ctx_bits.index(chosen)
-    kept = lax.dynamic_index_in_dim(spread, value, at, keepdims=False)
-    rest = [bit for bit in ctx_bits if bit != chosen]
-    order = [0] + [1 + rest.index(bit) for bit in axis_bits] + [1 + len(rest)]
-    return jnp.transpose(kept, order).reshape(left.shape[0], -1)
+    )(*ins, *after)
+
+
+def stripe_rows(ref, first, count):
+    side = 2 * HALF
+    blocks = [
+        ref[:, pl.ds(pl.multiple_of(first + part * side, side), side)]
+        for part in range(count // side)
+    ]
+    return jnp.concatenate(blocks, axis=0)
+
+
+def wide_product(bit, piece, left_ref, left_got_ref, right_ref, right_got_ref):
+    turned, columns, got_first = piece
+    half = left_ref.shape[1] // 2
+    if turned:
+        right = jnp.concatenate([right_ref[...], right_got_ref[...]], axis=1)
+    else:
+        right = jnp.concatenate([right_ref[:, 0:columns], right_got_ref[:, 0:columns]], axis=0)
+    left = jnp.concatenate(
+        [
+            stripe_rows(left_ref, bit * half, half),
+            stripe_rows(left_got_ref, got_first + bit * half, half),
+        ],
+        axis=1,
+    )
+    return dot_of(left, right, 1, 1 if turned else 0)
+
+
+def group_products(groups, place_ref, ins, wanted):
+    at = 0
+    for number, (order, pieces) in enumerate(groups):
+        bit = bit_at(place_ref, order[1])
+        first = 0
+        for piece in pieces:
+            here = slice(first, first + piece[1])
+            first = here.stop
+            yield number, here, wide_product(
+                bit if wanted else 1 - bit, piece, *ins[4 * at : 4 * at + 4]
+            )
+            at += 1
+
+
+def split_rows(bit, acc_ref, send_ref, keep_ref):
+    half = keep_ref.shape[0]
+    send_ref[...] = acc_ref[pl.ds(pl.multiple_of((1 - bit) * half, half), half), :].astype(
+        send_ref.dtype
+    )
+    keep_ref[...] = acc_ref[pl.ds(pl.multiple_of(bit * half, half), half), :].astype(
+        keep_ref.dtype
+    )
+
+
+def bit_at(place_ref, bit):
+    return (place_ref[0] >> bit) & 1
+
+
+def product_kernel(groups, place_ref, *refs):
+    kinds = len(groups)
+    for number, here, value in group_products(groups, place_ref, refs[:-kinds], False):
+        refs[number - kinds][:, here] = value.astype(jnp.bfloat16)
+
+
+def product_add_kernel(groups, place_ref, *refs):
+    kinds = len(groups)
+    got, sends, keeps, accs = (
+        refs[first * kinds : (first + 1) * kinds or None] for first in range(-4, 0)
+    )
+    for number, here, value in group_products(groups, place_ref, refs[: -4 * kinds], True):
+        accs[number][:, here] = value + got[number][:, here].astype(jnp.float32)
+    for number, (order, _) in enumerate(groups):
+        split_rows(bit_at(place_ref, order[2]), accs[number], sends[number], keeps[number])
+
+
+def add_kernel(groups, place_ref, *refs):
+    kinds = len(groups)
+    send_ref, keep_ref, acc_ref = refs[2 * kinds :]
+    first = 0
+    for number in range(kinds):
+        here = slice(first, first + refs[number].shape[1])
+        first = here.stop
+        acc_ref[:, here] = refs[number][...].astype(jnp.float32) + refs[kinds + number][
+            ...
+        ].astype(jnp.float32)
+    split_rows(bit_at(place_ref, groups[0][0][3]), acc_ref, send_ref, keep_ref)
+
+
+def last_kernel(keep_ref, got_ref, *out_refs):
+    first = 0
+    for ref in out_refs:
+        here = slice(first, first + ref.shape[1])
+        first = here.stop
+        ref[...] = keep_ref[:, here].astype(jnp.float32) + got_ref[:, here].astype(jnp.float32)
+
+
+def held(value, after):
+    return pl.pallas_call(
+        lambda *refs: None,
+        out_shape=jax.ShapeDtypeStruct(value.shape, value.dtype),
+        in_specs=[pl.BlockSpec(memory_space=pl.ANY)] * (1 + len(after)),
+        out_specs=pl.BlockSpec(memory_space=pl.ANY),
+        input_output_aliases={0: 0},
+    )(value, *after)
 
 
 def swap_over(value, bit, count):
     return lax.ppermute(value, "ctx", [(place, place ^ (1 << bit)) for place in range(count)])
 
 
-def reduce_rows(left, right, right_dim, place, count, order, gather):
-    bits = tuple(reversed(range(count.bit_length() - 1)))
-    bit_of = lambda bit: (place >> bit) & 1
-    if gather:
-        first, order = order[0], order[1:]
-        mine = stripes(left, bits, order, first, bit_of(first))
-        theirs = stripes(left, bits, order, first, 1 - bit_of(first))
-        left = jnp.concatenate([mine, swap_over(theirs, first, count)], axis=0)
-        right = jnp.concatenate([right, swap_over(right, first, count)], axis=0)
-        bits = order
-    first, order = order[0], order[1:]
-    send = dot_of(
-        stripes(left, bits, order, first, 1 - bit_of(first)), right, 0, right_dim
-    ).astype(jnp.bfloat16)
-    keep = dot_of(stripes(left, bits, order, first, bit_of(first)), right, 0, right_dim)
-    total = keep + swap_over(send, first, count).astype(jnp.float32)
-    for bit in order:
-        half = total.shape[0] // 2
-        send = lax.dynamic_slice_in_dim(total, (1 - bit_of(bit)) * half, half, 0)
-        keep = lax.dynamic_slice_in_dim(total, bit_of(bit) * half, half, 0)
-        total = keep + swap_over(send.astype(jnp.bfloat16), bit, count).astype(jnp.float32)
-    return total
+class Reductions:
+    def __init__(self, groups, device, count, ins):
+        self.groups, self.device, self.count, self.ins = groups, device, count, ins
+        self.columns = [sum(piece[1] for piece in pieces) for _, pieces in groups]
+        self.rows = ins[0].shape[1] // 2
+
+    def shapes(self, rows, dtype):
+        return [((rows, columns), dtype) for columns in self.columns]
+
+    def swap(self, sent, stage):
+        return [
+            swap_over(value, order[stage], self.count)
+            for value, (order, _) in zip(sent, self.groups)
+        ]
+
+    def first(self, after):
+        sent = call(
+            functools.partial(product_kernel, self.groups),
+            self.shapes(self.rows, jnp.bfloat16),
+            [self.device] + self.ins,
+            after=after,
+            mebibytes=60,
+            flops=10**15,
+        )
+        self.got = self.swap(sent, 1)
+        return sent
+
+    def second(self, after):
+        half = self.rows // 2
+        kinds = len(self.groups)
+        results = call(
+            functools.partial(product_add_kernel, self.groups),
+            self.shapes(half, jnp.bfloat16) * 2,
+            [self.device] + self.ins + self.got,
+            scratch=[pltpu.VMEM((self.rows, columns), jnp.float32) for columns in self.columns],
+            after=after,
+            mebibytes=60,
+            flops=10**15,
+        )
+        self.keep = results[kinds:]
+        self.got = self.swap(results[:kinds], 2)
+        return results[:kinds]
+
+    def third(self, after):
+        quarter = self.rows // 4
+        wide = sum(self.columns)
+        sent, self.keep = call(
+            functools.partial(add_kernel, self.groups),
+            [((quarter, wide), jnp.bfloat16)] * 2,
+            [self.device] + list(self.keep) + list(self.got),
+            scratch=[pltpu.VMEM((2 * quarter, wide), jnp.float32)],
+            after=after,
+            mebibytes=60,
+            flops=2 * 10**9,
+        )
+        self.got = swap_over(sent, self.groups[0][0][3], self.count)
+        return [sent]
+
+    def last(self):
+        return call(
+            last_kernel,
+            [
+                ((self.rows // 4, piece[1]), jnp.float32)
+                for _, pieces in self.groups
+                for piece in pieces
+            ],
+            [self.keep, self.got],
+            mebibytes=60,
+            flops=10**9,
+        )
 
 
 def on_device_paired(
@@ -903,37 +1149,69 @@
     smem = pl.BlockSpec(memory_space=pltpu.SMEM)
     whole = lambda *shape: pl.BlockSpec(shape, lambda step: (0,) * len(shape))
 
-    pair_in = lax.all_gather(jnp.concatenate([tokens, cotangent], axis=0), "tp")
-    b_three = jnp.stack([b_qv[0], jnp.zeros_like(b_qv[0]), b_qv[1]]).reshape(3, 1, width)
-    sent, h_own, _ = call(
+    device = place.reshape(1)
+    sent, full_in, full_cot, cot_mine, cot_theirs = call(
         qkv_kernel,
-        [((count, FWD_ROWS, rows), bf16), ((rows, width), bf16), ((rows, model), bf16)],
-        [rank, pair_in, gain_one, bias_one, w_qkv, b_three, segment_ids.reshape(1, rows)],
+        [
+            ((count, FWD_ROWS, rows), bf16),
+            ((rows, model), bf16),
+            ((rows, model), bf16),
+            ((rows, model // 2), bf16),
+            ((rows, model // 2), bf16),
+        ],
+        [
+            rank,
+            device,
+            tokens,
+            other_core(tokens),
+            cotangent,
+            other_core(cotangent),
+            gain_one,
+            bias_one,
+            w_qkv,
+            b_qv,
+            segment_ids.reshape(1, rows),
+        ],
+        scratch=[pltpu.VMEM((rows, model), bf16), pltpu.VMEM((model, rows), bf16)],
         grid=(3,),
-        in_specs=[
-            smem,
-            whole(2, 2 * rows, width),
+        in_specs=[smem, smem]
+        + [whole(rows, width)] * 4
+        + [
             whole(1, model),
             whole(1, model),
             pl.BlockSpec((1, model, width), lambda step: (step, 0, 0)),
-            pl.BlockSpec((1, 1, width), lambda step: (step, 0, 0)),
+            whole(2, width),
             whole(1, rows),
         ],
-        out_specs=[whole(count, FWD_ROWS, rows), whole(rows, width), whole(rows, model)],
-    )
-    h_all_own = lax.all_gather(h_own, "ctx", axis=0, tiled=True)
-    h_all_other = other_core(h_all_own)
-    got = to_heads(sent)
-    attn_sent, attn_raw, lse = call(
+        out_specs=[
+            whole(count, FWD_ROWS, rows),
+            whole(rows, model),
+            whole(rows, model),
+            whole(rows, model // 2),
+            whole(rows, model // 2),
+        ],
+        mebibytes=60,
+        flops=3 * 10**9,
+    )
+    cot_got = swap_over(cot_theirs, DOWN_BITS[0], count)
+    bit_x, bit_y, bit_z, bit_far = range(4)
+    far, near = swap_over(tokens, bit_far, count), swap_over(tokens, bit_z, count)
+    corner = swap_over(far, bit_z, count)
+    got = to_heads(held(sent, [far, near]))
+    attn_sent, attn_raw, lse, line = call(
         forward_kernel,
         [
             ((count, HDIM // 2, rows), bf16),
             ((HDIM, all_tokens // 2), f32),
             ((1, all_tokens // 2), f32),
-        ],
-        [slope, side, got],
+            ((4 * rows, width), bf16),
+        ],
+        [slope, side, got, tokens, far, near, corner],
         scratch=[pltpu.VMEM((all_tokens, HDIM), bf16)],
-    )
+        mebibytes=24,
+        flops=4 * 10**9,
+    )
+    line_x = swap_over(line, bit_x, count)
     attn_got = to_heads(attn_sent)
     part, attn_turned = call(
         out_kernel,
@@ -942,20 +1220,22 @@
         scratch=[pltpu.VMEM((rows, model), f32)],
     )
     chunk = 512
-    middle, h_two, act, grad_pre, grad_b_up, share, swap = call(
+    middle, act, grad_pre, h_mine, grad_b_up, share, swap = call(
         mlp_kernel,
         [
             ((rows, model), f32),
-            ((rows, model), bf16),
             ((rows, hidden), bf16),
-            ((rows, hidden), bf16),
+            ((rows, hidden + model // 2), bf16),
+            ((rows, model // 2), bf16),
             ((1, hidden), f32),
             ((rows, width), f32),
             ((rows, model + width), bf16),
         ],
         [
             rank,
-            pair_in,
+            device,
+            full_in,
+            full_cot,
             part,
             other_core(part),
             gain_two,
@@ -965,11 +1245,9 @@
             w_down,
         ],
         grid=(hidden // chunk,),
-        in_specs=[
-            smem,
-            whole(2, 2 * rows, width),
-            whole(rows, model),
-            whole(rows, model),
+        in_specs=[smem, smem]
+        + [whole(rows, model)] * 4
+        + [
             whole(1, model),
             whole(1, model),
             pl.BlockSpec((model, chunk), lambda step: (0, step)),
@@ -978,27 +1256,37 @@
         ],
         out_specs=[
             whole(rows, model),
-            whole(rows, model),
             pl.BlockSpec((rows, chunk), lambda step: (0, step)),
-            pl.BlockSpec((rows, chunk), lambda step: (0, step)),
+            whole(rows, hidden + model // 2),
+            whole(rows, model // 2),
             pl.BlockSpec((1, chunk), lambda step: (0, step)),
             whole(rows, width),
             whole(rows, model + width),
         ],
-        scratch=[pltpu.VMEM((rows, model), f32), pltpu.VMEM((rows, model), f32)],
-    )
-    mixed, grad_mid, grad_low, grad_sent, small_two = call(
+        scratch=[
+            pltpu.VMEM((rows, model), bf16),
+            pltpu.VMEM((model, rows), bf16),
+            pltpu.VMEM((rows, model), f32),
+            pltpu.VMEM((rows, model), f32),
+        ],
+        mebibytes=56,
+        flops=7 * 10**9,
+    )
+    mixed, grad_mid, grad_sent, low_mine, out_theirs, small_two, plane = call(
         middle_kernel,
         [
             ((rows, width), bf16),
             ((rows, width), f32),
-            ((rows, model), bf16),
             ((count, HDIM // 2, rows), bf16),
+            ((rows, model // 2), bf16),
+            ((rows, model // 2), bf16),
             ((8, width), f32),
+            ((8 * rows, width), bf16),
         ],
         [
             rank,
-            pair_in,
+            device,
+            full_cot,
             swap,
             other_core(swap),
             middle,
@@ -1006,59 +1294,98 @@
             gain_two,
             b_down.reshape(1, width),
             w_out,
-        ],
-        scratch=[pltpu.VMEM((rows + 8, model), f32)],
-    )
-    cot_full = jnp.concatenate([pair_in[0, rows:], pair_in[1, rows:]], axis=1)
-    bit_x, bit_y, bit_z, bit_far = 0, 1, 2, 3
-    grad_down = reduce_rows(
-        cot_full, act, 0, place, count, (bit_x, bit_y, bit_z, bit_far), True
-    )
-    grad_up = reduce_rows(
-        h_two, grad_pre, 0, place, count, (bit_y, bit_x, bit_z, bit_far), True
-    )
-    grad_out = reduce_rows(
-        grad_low, attn_turned, 1, place, count, (bit_x, bit_y, bit_z, bit_far), False
-    )
-    (back_sent,) = call(
+            line,
+            line_x,
+        ],
+        scratch=[pltpu.VMEM((rows + 8, model), f32), pltpu.VMEM((model, rows), bf16)],
+        mebibytes=60,
+        flops=2 * 10**9,
+    )
+    back_other = swap_over(grad_pre, UP_BITS[0], count)
+    reductions = Reductions(
+        (
+            (DOWN_BITS, ((False, hidden, 0),)),
+            (UP_BITS, ((False, hidden, hidden), (True, width, 0))),
+        ),
+        device,
+        count,
+        [cot_mine, cot_got, act, swap_over(act, DOWN_BITS[0], count)]
+        + [h_mine, back_other, grad_pre, back_other]
+        + [low_mine, swap_over(out_theirs, UP_BITS[0], count)]
+        + [attn_turned, swap_over(attn_turned, UP_BITS[0], count)],
+    )
+    grad_got = to_heads(grad_sent)
+    gathered = [plane, swap_over(plane, bit_y, count)]
+    gathered += [other_core(value) for value in gathered]
+    first_sent = reductions.first([])
+    back_sent, back_low = call(
         backward_kernel,
-        [((count, BACK_ROWS, rows), bf16)],
-        [slope, side, rank, got, to_heads(grad_sent), attn_raw, lse, h_all_own, h_all_other],
+        [((count, SEG_ROW, rows), bf16), ((3 * HDIM, all_tokens), bf16)],
+        [slope, side, got, grad_got, attn_raw, lse],
         scratch=[
             pltpu.VMEM((all_tokens, HDIM), bf16),
             pltpu.VMEM((all_tokens, HDIM), bf16),
             pltpu.VMEM((HDIM, all_tokens), f32),
             pltpu.VMEM((HDIM, all_tokens), f32),
+        ],
+        after=[first_sent[0]],
+        mebibytes=56,
+        flops=10**10,
+    )
+    (weight_sent,) = call(
+        weight_kernel,
+        [((count, 3 * HDIM // 2, rows), bf16)],
+        [rank, device, gain_one, bias_one, back_low] + gathered,
+        scratch=[
+            pltpu.VMEM((all_tokens, model), bf16),
             pltpu.VMEM((3 * HDIM, all_tokens), bf16),
             pltpu.VMEM((3 * HDIM, model), f32),
         ],
-    )
+        mebibytes=56,
+        flops=6 * 10**9,
+    )
+    weight_got = to_heads(weight_sent)
+    second_sent = reductions.second([weight_sent])
+    third_sent = reductions.third([weight_got])
     back_got = to_heads(back_sent)
-    part_one, grad_qkv, sums = call(
+    part_one, sums = call(
         hidden_kernel,
         [
             ((rows, model), bf16),
-            ((heads, BACK_ROWS - SEG_ROW, rows), f32),
             ((3, 8, width), f32),
         ],
         [back_got, w_qkv],
         grid=(3,),
         in_specs=[
-            whole(count, BACK_ROWS, rows),
+            whole(count, SEG_ROW, rows),
             pl.BlockSpec((1, model, width), lambda step: (step, 0, 0)),
         ],
         out_specs=[
             whole(rows, model),
-            whole(heads, BACK_ROWS - SEG_ROW, rows),
             pl.BlockSpec((1, 8, width), lambda step: (step, 0, 0)),
         ],
         scratch=[pltpu.VMEM((rows, model), f32)],
+        after=[second_sent[0]],
+        flops=3 * 10**9,
     )
     input_grad, small_one = call(
         input_kernel,
         [((rows, width), bf16), ((8, width), f32)],
-        [rank, pair_in, part_one, other_core(part_one), gain_one, grad_mid],
+        [rank, full_in, part_one, other_core(part_one), gain_one, grad_mid],
         scratch=[pltpu.VMEM((rows + 8, model), f32)],
+        after=[third_sent[0]],
+    )
+    grad_down, grad_up, grad_out = reductions.last()
+    stripe = model // count
+    grad_qkv = (
+        weight_got.astype(f32)
+        .reshape(heads, 2, 3 * HDIM // 2, 2 * stripe)
+        .sum(axis=1)
+        .reshape(heads, 3 * HDIM // 2, 2, stripe)
+        .transpose(0, 2, 1, 3)
+        .reshape(heads, 3, HDIM, stripe)
+        .transpose(1, 3, 0, 2)
+        .reshape(3, stripe, width)
     )
     share_w = width // count
     vectors = jnp.concatenate(
@@ -1073,14 +1400,6 @@
     lanes = vectors.shape[0] * share_w
     spread = vectors.transpose(1, 0, 2).reshape(count, 1, lanes)
     total = jnp.sum(to_heads(spread), axis=0).reshape(-1, share_w)
-    stripe = model // count
-    grad_qkv = (
-        grad_qkv.reshape(heads, 3 * HDIM // 2, 2, stripe)
-        .transpose(0, 2, 1, 3)
-        .reshape(heads, 3, HDIM, stripe)
-        .transpose(1, 3, 0, 2)
-        .reshape(3, stripe, width)
-    )
     return (
         mixed,
         input_grad,

time: 231 us -> 206 us (0.89)
  Pallas kernels: 29.2 us -> 58 us
  local copies, waits for them, and re-layouts: 38 us -> 17.2 us
  between operations: 14.7 us -> 1.04 us
  other arithmetic: 11 us -> 1.85 us
  matrix products: 8.67 us -> 0 us
  waiting for transfers between devices: 69.5 us -> 73.9 us
  blocking collectives: 15.6 us -> 12.4 us
    pallas_call x8 -> x14, Pallas kernels: 29.2 us -> 58 us  [the longest x13 58 us: call(): pl.pallas_call(body, out_shape=[jax.ShapeDtypeStruct(shape, dtype) for sh...]
    dot_general x6 -> x0, matrix products: 8.67 us -> none  [dot_of(): lax.dot_general(left, right, (((left_dim,), (right_dim,)), ((), ())), pre...]
    slice x4 -> x0, local copies, waits for them, and re-layouts: 4.79 us -> none  [the longest x3 4.03 us: on_device_paired(): cot_full = jnp.concatenate([pair_in[0, rows:], pair_in[1, rows:]], axis=1)]
    pallas_call x4 -> x1, local copies, waits for them, and re-layouts: 4.31 us -> 0.51 us  [call(): pl.pallas_call(body, out_shape=[jax.ShapeDtypeStruct(shape, dtype) for sh...]
    transpose x3 -> x0, other arithmetic: 3.69 us -> none  [the longest x2 2.47 us: on_device_paired(): return (mixed, input_grad, total[0], total[1], grad_qkv, total[2:4], grad...]
    convert_element_type x7 -> x0, local copies, waits for them, and re-layouts: 3.38 us -> none  [reduce_rows(): send.astype(jnp.bfloat16)]
    concatenate x3 -> x0, other arithmetic: 3.29 us -> none  [the longest x2 2.31 us: reduce_rows(): left = jnp.concatenate([mine, swap_over(theirs, first, count)], axis=0)]
    all_to_all x4 -> x5, waiting for transfers between devices: 22.4 us -> 25.6 us  [on_device_paired(): to_heads = lambda value: lax.all_to_all(value, 'ctx', 0, 0, tiled=True)]
  transfers between devices with their start and end apart: 23 -> 27, of which waited for: 10 -> 14; matrix products, arithmetic and copies ran while one was open for 18% -> 4% of each run, Pallas kernels for 12% -> 25%
where the time goes in v2:
time: 206 us; the launch traced here: 205 us
  waiting for transfers between devices  73.9 us (36%)
  Pallas kernels  58 us (28%)
  starting transfers between devices  40.8 us (20%)
  local copies, waits for them, and re-layouts  17.2 us (8%)
  blocking collectives  12.4 us (6%)
    pallas_call x13, Pallas kernels, call(): pl.pallas_call(body, out_shape=[jax.ShapeDtypeStruct(shape, dtype) for sh...  58 us
    ppermute x15, waiting for transfers between devices, swap_over(): lax.ppermute(value, 'ctx', [(place, place ^ 1 << bit) for place in range(...  45.3 us
    all_to_all x5, waiting for transfers between devices, on_device_paired(): to_heads = lambda value: lax.all_to_all(value, 'ctx', 0, 0, tiled=True)  25.6 us
    all_to_all x5, starting transfers between devices, on_device_paired(): to_heads = lambda value: lax.all_to_all(value, 'ctx', 0, 0, tiled=True)  22.4 us
    ppermute x15, starting transfers between devices, swap_over(): lax.ppermute(value, 'ctx', [(place, place ^ 1 << bit) for place in range(...  17.6 us
    all_to_all x1, blocking collectives, on_device_paired(): to_heads = lambda value: lax.all_to_all(value, 'ctx', 0, 0, tiled=True)  12.4 us
    unnamed x72, local copies, waits for them, and re-layouts  11.3 us
  transfers between devices with their start and end apart: 27, of which 14 were waited for; matrix products, arithmetic and copies ran while one was open for 4% of the time, Pallas kernels for 25%

profile of v2, /device:TPU:0, one launch (start us, length us, event | category | flops | bytes accessed | tf_op | source)
XLA Modules:
  0.0 205.1 jit_solution(12519488899674818704)
XLA Ops:
  1.2 4.0 %collective-permute-start.2 = (bf16[128,512]{1,0:T(8,128)(2,1)}, bf16[128,512]{1,0:T(8,128)(2,1)S(1)}, u32[]{:S(2)}, u32[]{:S(2)}) collective-permute-start(bf16[128,512]{1,0:T(8,128)(2,1)} %refs_3_.1), channel_id=1, source_target_pairs={{0,16},{2,18},{4,20},{6,22},{8,24},{10,26},{12,28},{14,30},{16,0},... | collective-permute-start | bytes 393224 | tf_op jit(solution)/shard_map/ppermute | solution.py:1040
  7.5 5.3 %shard_map.254 = (bf16[16,176,128]{2,1,0:T(8,128)(2,1)}, bf16[128,1024]{1,0:T(8,128)(2,1)}, bf16[128,1024]{1,0:T(8,128)(2,1)}, bf16[128,512]{1,0:T(8,128)(2,1)}, bf16[128,512]{1,0:T(8,128)(2,1)}) custom-call(s32[1]{0:T(128)} %bitcast.refs_0_, s32[1]{0:T(128)} %bitcast.1.refs_1_.refs_0_, bf16[128,512]{1,0:T(8,128)(2,1)} %refs_3_.1, ...), custom_call_target="tpu_custom_call" | custom-call | flops 300000 | bytes 1024 | tf_op jit(solution)/shard_map/pallas_call | solution.py:923
  13.5 6.0 %all-to-all-start = ((bf16[16,176,128]{2,1,0:T(8,128)(2,1)}), bf16[16,176,128]{2,1,0:T(8,128)(2,1)S(1)}, u32[]{:S(2)}, u32[]{:S(2)}) async-start(bf16[16,176,128]{2,1,0:T(8,128)(2,1)} %shard_map.255), calls=%async_computation | async-start | bytes 1441792 | tf_op jit(solution)/shard_map/all_to_all | solution.py:1148
  19.5 1.9 collective-permute-start.4
  21.5 13.9 %collective-permute-done.4.refs_6_ = bf16[128,512]{1,0:T(8,128)(2,1)S(1)} collective-permute-done((bf16[128,512]{1,0:T(8,128)(2,1)}, bf16[128,512]{1,0:T(8,128)(2,1)S(1)}, u32[]{:S(2)}, u32[]{:S(2)}) %collective-permute-start.4) | collective-permute-done | bytes 131104 | tf_op jit(solution)/shard_map/ppermute | solution.py:1040
  35.4 2.8 %all-to-all-done.refs_2_ = bf16[16,176,128]{2,1,0:T(8,128)(2,1)S(1)} async-done(((bf16[16,176,128]{2,1,0:T(8,128)(2,1)}), bf16[16,176,128]{2,1,0:T(8,128)(2,1)S(1)}, u32[]{:S(2)}, u32[]{:S(2)}) %all-to-all-start) | async-done | bytes 720928 | tf_op jit(solution)/shard_map/all_to_all | solution.py:1148
  40.1 3.9 %shard_map.256 = (bf16[16,32,128]{2,1,0:T(8,128)(2,1)S(1)}, f32[64,1024]{1,0:T(8,128)S(1)}, f32[1,1024]{1,0:T(1,128)S(1)}, bf16[512,512]{1,0:T(8,128)(2,1)S(1)}) custom-call(f32[1]{0:T(128)} %bitcast.5.refs_0_, s32[1]{0:T(128)} %bitcast.6.refs_1_, bf16[16,176,128]{2,1,0:T(8,128)(2,1)S(1)} %all-to-all-done.refs_2_, bf16[128,512]{1,0:T(8,128)(2,1)S(1)} %copy-done.7, ...), custom_call_target="tpu_custom_call" | custom-call | flops 400000 | bytes 1024 | tf_op jit(solution)/shard_map/pallas_call | solution.py:923
  44.1 12.4 %all_to_all.30.refs_1_ = bf16[16,32,128]{2,1,0:T(8,128)(2,1)S(1)} all-to-all(bf16[16,32,128]{2,1,0:T(8,128)(2,1)S(1)} %get-tuple-element.59), channel_id=1, replica_groups=mesh['ctx'=16,'tp'=2] {'ctx'}, dimensions={0} | all-to-all | bytes 262144 | tf_op jit(solution)/shard_map/all_to_all | solution.py:1148
  59.2 9.2 %shard_map.258 = (f32[128,1024]{1,0:T(8,128)}, bf16[128,2048]{1,0:T(8,128)(2,1)}, bf16[128,2560]{1,0:T(8,128)(2,1)}, bf16[128,512]{1,0:T(8,128)(2,1)}, f32[1,204...) custom-call(s32[1]{0:T(128)} %bitcast.refs_0_, s32[1]{0:T(128)} %bitcast.1.refs_1_.refs_0_, ...), custom_call_target="tpu_custom_call" | custom-call | flops 700000 | bytes 1024 | tf_op jit(solution)/shard_map/pallas_call | solution.py:923
  73.5 4.3 %shard_map.259 = (bf16[128,512]{1,0:T(8,128)(2,1)}, f32[128,512]{1,0:T(8,128)}, bf16[16,32,128]{2,1,0:T(8,128)(2,1)}, bf16[128,512]{1,0:T(8,128)(2,1)}, bf16[128...) custom-call(s32[1]{0:T(128)} %bitcast.refs_0_, s32[1]{0:T(128)} %bitcast.1.refs_1_.refs_0_, ...), custom_call_target="tpu_custom_call" | custom-call | flops 200000 | bytes 1024 | tf_op jit(solution)/shard_map/pallas_call | solution.py:923
  78.4 3.7 %all-to-all-start.2 = ((bf16[16,32,128]{2,1,0:T(8,128)(2,1)}), bf16[16,32,128]{2,1,0:T(8,128)(2,1)S(1)}, u32[]{:S(2)}, u32[]{:S(2)}) async-start(bf16[16,32,128]{2,1,0:T(8,128)(2,1)} %get-tuple-element.66), calls=%async_computation.2 | async-start | bytes 262144 | tf_op jit(solution)/shard_map/all_to_all | solution.py:1148
  82.1 4.9 %collective-permute-done.8.refs_2_ = bf16[128,512]{1,0:T(8,128)(2,1)S(1)} collective-permute-done((bf16[128,512]{1,0:T(8,128)(2,1)S(1)}, bf16[128,512]{1,0:T(8,128)(2,1)S(1)}, u32[]{:S(2)}, u32[]{:S(2)}) %collective-permute-start.8) | collective-permute-done | bytes 131104 | tf_op jit(solution)/shard_map/ppermute | solution.py:1040
  87.5 2.3 %collective-permute-done.12.refs_12_ = bf16[512,128]{1,0:T(8,128)(2,1)S(1)} collective-permute-done((bf16[512,128]{1,0:T(8,128)(2,1)S(1)}, bf16[512,128]{1,0:T(8,128)(2,1)S(1)}, u32[]{:S(2)}, u32[]{:S(2)}) %collective-permute-start.12) | collective-permute-done | bytes 131104 | tf_op jit(solution)/shard_map/ppermute | solution.py:1040
  89.9 2.9 %collective-permute-done.11.refs_10_ = bf16[128,512]{1,0:T(8,128)(2,1)S(1)} collective-permute-done((bf16[128,512]{1,0:T(8,128)(2,1)}, bf16[128,512]{1,0:T(8,128)(2,1)S(1)}, u32[]{:S(2)}, u32[]{:S(2)}) %collective-permute-start.11) | collective-permute-done | bytes 131104 | tf_op jit(solution)/shard_map/ppermute | solution.py:1040
  93.6 4.0 %shard_map.260 = (bf16[256,2048]{1,0:T(8,128)(2,1)}, bf16[256,2560]{1,0:T(8,128)(2,1)}) custom-call(s32[1]{0:T(128)} %bitcast.1.refs_1_.refs_0_, bf16[128,512]{1,0:T(8,128)(2,1)} %get-tuple-element.69.refs_1_, bf16[128,512]{1,0:T(8,128)(2,1)} %copy-done.33, bf16[128,2048]{1,0:T(8,128)(2,1)} %get-tuple-element.71.refs_3_, ...), custom_call_target="tpu_custom_call" | custom-call | flops 99999997952 | bytes 1024 | tf_op jit(solution)/shard_map/pallas_call | solution.py:923
  99.5 7.2 %shard_map.261 = (bf16[16,160,128]{2,1,0:T(8,128)(2,1)}, bf16[192,2048]{1,0:T(8,128)(2,1)}) custom-call(f32[1]{0:T(128)} %bitcast.5.refs_0_, s32[1]{0:T(128)} %bitcast.6.refs_1_, bf16[16,176,128]{2,1,0:T(8,128)(2,1)} %copy-done.1, bf16[16,32,128]{2,1,0:T(8,128)(2,1)} %copy-done.25, f32[64,1024]{1,0:T(8,128)} %copy-done.14, f32[1,1024]{1,0:T(1,128)} %copy-done.16, ...), custom_call_target="tpu_custom_call" | custom-call | flops 1000000 | bytes 1024 | tf_op jit(solution)/shard_map/pallas_call | solution.py:923
  106.7 3.6 %all-to-all-start.3 = ((bf16[16,160,128]{2,1,0:T(8,128)(2,1)}), bf16[16,160,128]{2,1,0:T(8,128)(2,1)S(1)}, u32[]{:S(2)}, u32[]{:S(2)}) async-start(bf16[16,160,128]{2,1,0:T(8,128)(2,1)} %get-tuple-element.78), calls=%async_computation.3 | async-start | bytes 1310720 | tf_op jit(solution)/shard_map/all_to_all | solution.py:1148
  110.4 3.4 %collective-permute-done.15.refs_6_ = bf16[1024,512]{1,0:T(8,128)(2,1)S(1)} collective-permute-done((bf16[1024,512]{1,0:T(8,128)(2,1)}, bf16[1024,512]{1,0:T(8,128)(2,1)S(1)}, u32[]{:S(2)}, u32[]{:S(2)}) %collective-permute-start.15) | collective-permute-done | bytes 1048608 | tf_op jit(solution)/shard_map/ppermute | solution.py:1040
  114.0 2.5 %collective-permute-done.17.refs_8_ = bf16[1024,512]{1,0:T(8,128)(2,1)S(1)} collective-permute-done((bf16[1024,512]{1,0:T(8,128)(2,1)S(1)}, bf16[1024,512]{1,0:T(8,128)(2,1)S(1)}, u32[]{:S(2)}, u32[]{:S(2)}) %collective-permute-start.17) | collective-permute-done | bytes 1048608 | tf_op jit(solution)/shard_map/ppermute | solution.py:1147
  117.5 8.4 %shard_map.262.refs_15_ = bf16[16,96,128]{2,1,0:T(8,128)(2,1)} custom-call(s32[1]{0:T(128)} %bitcast.refs_0_, s32[1]{0:T(128)} %bitcast.1.refs_1_.refs_0_, f32[1,1024]{1,0:T(1,128)} %bitcast.43, f32[1,1024]{1,0:T(1,128)} %bitcast.52, bf16[192,2048]{1,0:T(8,128)(2,1)} %get-tuple-element.80.refs_4_, bf16[1024,512]{1,0:T(8,128)(2,1)} %get-tuple-element.81.refs_5_, ...), custom_call_target="tpu_custom_call" | custom-call | flops 600000 | bytes 1024 | tf_op jit(solution)/shard_map/pallas_call | solution.py:923
  125.9 8.2 %all-to-all-done.3.refs_0_ = bf16[16,160,128]{2,1,0:T(8,128)(2,1)S(1)} async-done(((bf16[16,160,128]{2,1,0:T(8,128)(2,1)}), bf16[16,160,128]{2,1,0:T(8,128)(2,1)S(1)}, u32[]{:S(2)}, u32[]{:S(2)}) %all-to-all-start.3) | async-done | bytes 655392 | tf_op jit(solution)/shard_map/all_to_all | solution.py:1148
  134.1 4.2 %all-to-all-start.4 = ((bf16[16,96,128]{2,1,0:T(8,128)(2,1)}), bf16[16,96,128]{2,1,0:T(8,128)(2,1)}, u32[]{:S(2)}, u32[]{:S(2)}) async-start(bf16[16,96,128]{2,1,0:T(8,128)(2,1)} %shard_map.262.refs_15_), calls=%async_computation.4 | async-start | bytes 786432 | tf_op jit(solution)/shard_map/all_to_all | solution.py:1148
  138.3 8.5 %collective-permute-done.13.refs_13_ = bf16[256,2048]{1,0:T(8,128)(2,1)} collective-permute-done((bf16[256,2048]{1,0:T(8,128)(2,1)}, bf16[256,2048]{1,0:T(8,128)(2,1)}, u32[]{:S(2)}, u32[]{:S(2)}) %collective-permute-start.13) | collective-permute-done | bytes 1048608 | tf_op jit(solution)/shard_map/ppermute | solution.py:1040
  146.8 5.5 %shard_map.263 = (bf16[128,2048]{1,0:T(8,128)(2,1)}, bf16[128,2560]{1,0:T(8,128)(2,1)}, bf16[128,2048]{1,0:T(8,128)(2,1)}, bf16[128,2560]{1,0:T(8,128)(2,1)}) custom-call(s32[1]{0:T(128)} %bitcast.1.refs_1_.refs_0_, bf16[128,512]{1,0:T(8,128)(2,1)} %get-tuple-element.69.refs_1_, bf16[128,512]{1,0:T(8,128)(2,1)} %copy-done.33, ...), custom_call_target="tpu_custom_call" | custom-call | flops 99999997952 | bytes 1024 | tf_op jit(solution)/shard_map/pallas_call | solution.py:923
  155.4 2.3 %shard_map.264 = (bf16[128,1024]{1,0:T(8,128)(2,1)}, f32[3,8,512]{2,1,0:T(8,128)S(1)}) custom-call(bf16[16,160,128]{2,1,0:T(8,128)(2,1)S(1)} %all-to-all-done.3.refs_0_, bf16[3,1024,512]{2,1,0:T(8,128)(2,1)S(1)} %copy-done, bf16[128,2048]{1,0:T(8,128)(2,1)S(1)} %copy-done.6), custom_call_target="tpu_custom_call" | custom-call | flops 300000 | bytes 1024 | tf_op jit(solution)/shard_map/pallas_call | solution.py:923
  159.9 6.8 %collective-permute-done.19.refs_3_ = bf16[128,2048]{1,0:T(8,128)(2,1)} collective-permute-done((bf16[128,2048]{1,0:T(8,128)(2,1)}, bf16[128,2048]{1,0:T(8,128)(2,1)}, u32[]{:S(2)}, u32[]{:S(2)}) %collective-permute-start.19) | collective-permute-done | bytes 524320 | tf_op jit(solution)/shard_map/ppermute | solution.py:1040
  166.7 2.6 %collective-permute-done.20.refs_4_ = bf16[128,2560]{1,0:T(8,128)(2,1)} collective-permute-done((bf16[128,2560]{1,0:T(8,128)(2,1)}, bf16[128,2560]{1,0:T(8,128)(2,1)}, u32[]{:S(2)}, u32[]{:S(2)}) %collective-permute-start.20) | collective-permute-done | bytes 655392 | tf_op jit(solution)/shard_map/ppermute | solution.py:1040
  169.3 3.1 %shard_map.265 = (bf16[64,4608]{1,0:T(8,128)(2,1)}, bf16[64,4608]{1,0:T(8,128)(2,1)}) custom-call(s32[1]{0:T(128)} %bitcast.1.refs_1_.refs_0_, bf16[128,2048]{1,0:T(8,128)(2,1)} %get-tuple-element.85.refs_1_, bf16[128,2560]{1,0:T(8,128)(2,1)} %get-tuple-element.86.refs_2_, bf16[128,2048]{1,0:T(8,128)(2,1)} %collective-permute-done.19.refs_3_, ...), custom_call_target="tpu_custom_call" | custom-call | flops 200000 | bytes 1024 | tf_op jit(solution)/shard_map/pallas_call | solution.py:923
  174.6 2.1 %shard_map.266 = (bf16[128,512]{1,0:T(8,128)(2,1)}, f32[8,512]{1,0:T(8,128)S(1)}) custom-call(s32[1]{0:T(128)} %bitcast.refs_0_, bf16[128,1024]{1,0:T(8,128)(2,1)S(1)} %copy-done.3, bf16[128,1024]{1,0:T(8,128)(2,1)} %get-tuple-element.83.refs_2_, bf16[128,1024]{1,0:T(8,128)(2,1)S(1)} %collective-permute-done.18.refs_3_, f32[1,1024]{1,0:T(1,128)S(1)} %bitcast.44, ...), custom_call_target="tpu_custom_call" | custom-call | flops 10000 | bytes 1024 | tf_op jit(solution)/shard_map/pallas_call | solution.py:923
  177.6 5.0 %all-to-all-start.5 = ((f32[16,1,384]{2,1,0:T(1,128)}), f32[16,1,384]{2,1,0:T(1,128)S(1)}, u32[]{:S(2)}, u32[]{:S(2)}) async-start(f32[16,1,384]{2,1,0:T(1,128)} %reshape.137), calls=%async_computation.5 | async-start | bytes 49152 | tf_op jit(solution)/shard_map/all_to_all | solution.py:1148
  185.4 14.7 %all-to-all-done.5 = f32[16,1,384]{2,1,0:T(1,128)S(1)} async-done(((f32[16,1,384]{2,1,0:T(1,128)}), f32[16,1,384]{2,1,0:T(1,128)S(1)}, u32[]{:S(2)}, u32[]{:S(2)}) %all-to-all-start.5) | async-done | bytes 24608 | tf_op jit(solution)/shard_map/all_to_all | solution.py:1148
  202.8 2.3 %shard_map.267 = (f32[64,2048]{1,0:T(8,128)}, f32[64,2048]{1,0:T(8,128)}, f32[64,512]{1,0:T(8,128)}) custom-call(bf16[64,4608]{1,0:T(8,128)(2,1)} %get-tuple-element.94.refs_0_, bf16[64,4608]{1,0:T(8,128)(2,1)} %copy-done.23), custom_call_target="tpu_custom_call" | custom-call | flops 100000 | bytes 1024 | tf_op jit(solution)/shard_map/pallas_call | solution.py:923
  (134 shorter events, 32.3 us)
Async XLA Ops:
  0.6 6.2 %collective-permute-start = (bf16[128,512]{1,0:T(8,128)(2,1)}, bf16[128,512]{1,0:T(8,128)(2,1)S(1)}, u32[]{:S(2)}, u32[]{:S(2)}) collective-permute-start(bf16[128,512]{1,0:T(8,128)(2,1)} %refs_3_.1), channel_id=1, source_target_pairs={{0,1},{1,0},{2,3},{3,2},{4,5},{5,4},{6,7},{7,6},{8,9},{9,8},{10,11... | collective-permute-start | bytes 393224 | tf_op jit(solution)/shard_map/ppermute | solution.py:1147
  1.2 5.7 %collective-permute-start.1 = (bf16[128,512]{1,0:T(8,128)(2,1)}, bf16[128,512]{1,0:T(8,128)(2,1)S(1)}, u32[]{:S(2)}, u32[]{:S(2)}) collective-permute-start(bf16[128,512]{1,0:T(8,128)(2,1)} %refs_4_.1), channel_id=1, source_target_pairs={{0,1},{1,0},{2,3},{3,2},{4,5},{5,4},{6,7},{7,6},{8,9},{9,8},{10,11... | collective-permute-start | bytes 393224 | tf_op jit(solution)/shard_map/ppermute | solution.py:1147
  1.2 11.6 %collective-permute-start.2 = (bf16[128,512]{1,0:T(8,128)(2,1)}, bf16[128,512]{1,0:T(8,128)(2,1)S(1)}, u32[]{:S(2)}, u32[]{:S(2)}) collective-permute-start(bf16[128,512]{1,0:T(8,128)(2,1)} %refs_3_.1), channel_id=1, source_target_pairs={{0,16},{2,18},{4,20},{6,22},{8,24},{10,26},{12,28},{14,30},{16,0},... | collective-permute-start | bytes 393224 | tf_op jit(solution)/shard_map/ppermute | solution.py:1040
  5.3 7.6 %collective-permute-start.3 = (bf16[128,512]{1,0:T(8,128)(2,1)}, bf16[128,512]{1,0:T(8,128)(2,1)S(1)}, u32[]{:S(2)}, u32[]{:S(2)}) collective-permute-start(bf16[128,512]{1,0:T(8,128)(2,1)} %refs_3_.1), channel_id=1, source_target_pairs={{0,8},{2,10},{4,12},{6,14},{8,0},{10,2},{12,4},{14,6},{16,24},{18,... | collective-permute-start | bytes 393224 | tf_op jit(solution)/shard_map/ppermute | solution.py:1040
  7.5 30.7 %copy-start.7 = (bf16[128,512]{1,0:T(8,128)(2,1)S(1)}, bf16[128,512]{1,0:T(8,128)(2,1)}, u32[]{:S(2)}) copy-start(bf16[128,512]{1,0:T(8,128)(2,1)} %refs_3_.1) | copy-start | bytes 393220
  12.8 43.6 %copy-start.2 = (bf16[512,1024]{1,0:T(8,128)(2,1)S(1)}, bf16[512,1024]{1,0:T(8,128)(2,1)}, u32[]{:S(2)}) copy-start(bf16[512,1024]{1,0:T(8,128)(2,1)} %refs_9_.3) | copy-start | bytes 3145732
  12.8 43.6 %copy-start.17 = (f32[512]{0:T(512)S(1)}, f32[512]{0:T(512)}, u32[]{:S(2)}) copy-start(f32[512]{0:T(512)} %param.22) | copy-start | bytes 6148
  13.5 24.6 %all-to-all-start = ((bf16[16,176,128]{2,1,0:T(8,128)(2,1)}), bf16[16,176,128]{2,1,0:T(8,128)(2,1)S(1)}, u32[]{:S(2)}, u32[]{:S(2)}) async-start(bf16[16,176,128]{2,1,0:T(8,128)(2,1)} %shard_map.255), calls=%async_computation | async-start | bytes 1441792 | tf_op jit(solution)/shard_map/all_to_all | solution.py:1148
  19.5 15.9 %collective-permute-start.4 = (bf16[128,512]{1,0:T(8,128)(2,1)}, bf16[128,512]{1,0:T(8,128)(2,1)S(1)}, u32[]{:S(2)}, u32[]{:S(2)}) collective-permute-start(bf16[128,512]{1,0:T(8,128)(2,1)} %copy-done.8), channel_id=1, source_target_pairs={{0,8},{2,10},{4,12},{6,14},{8,0},{10,2},{12,4},{14,6},{16,24},{18,... | collective-permute-start | bytes 393224 | tf_op jit(solution)/shard_map/ppermute | solution.py:1040
  38.2 30.3 %copy-start.1 = (bf16[16,176,128]{2,1,0:T(8,128)(2,1)}, bf16[16,176,128]{2,1,0:T(8,128)(2,1)S(1)}, u32[]{:S(2)}) copy-start(bf16[16,176,128]{2,1,0:T(8,128)(2,1)S(1)} %all-to-all-done.refs_2_) | copy-start | bytes 2162692
  44.1 24.4 %copy-start.5 = (bf16[512,512]{1,0:T(8,128)(2,1)}, bf16[512,512]{1,0:T(8,128)(2,1)S(1)}, u32[]{:S(2)}) copy-start(bf16[512,512]{1,0:T(8,128)(2,1)S(1)} %get-tuple-element.64.refs_10_) | copy-start | bytes 1572868
  56.9 1.6 collective-permute-start.5
  57.0 14.3 %collective-permute-start.7 = (bf16[512,512]{1,0:T(8,128)(2,1)S(1)}, bf16[512,512]{1,0:T(8,128)(2,1)S(1)}, u32[]{:S(2)}, u32[]{:S(2)}) collective-permute-start(bf16[512,512]{1,0:T(8,128)(2,1)S(1)} %get-tuple-element.64.refs_10_), channel_id=1, source_target_pairs={{0,2},{2,0},{4,6},{6,4},{8,10},{10,8},{12,14},{14,12},{16,18},{18,... | collective-permute-start | bytes 1572872 | tf_op jit(solution)/shard_map/ppermute | solution.py:1040
  68.5 24.2 %collective-permute-start.10 = (bf16[128,2560]{1,0:T(8,128)(2,1)}, bf16[128,2560]{1,0:T(8,128)(2,1)S(1)}, u32[]{:S(2)}, u32[]{:S(2)}) collective-permute-start(bf16[128,2560]{1,0:T(8,128)(2,1)} %get-tuple-element.73.refs_7_), channel_id=1, source_target_pairs={{0,8},{2,10},{4,12},{6,14},{8,0},{10,2},{12,4},{14,6},{16,24},{18,... | collective-permute-start | bytes 1966088 | tf_op jit(solution)/shard_map/ppermute | solution.py:1040
  69.3 3.4 %collective-permute-start.6 = (bf16[128,1536]{1,0:T(8,128)(2,1)}, bf16[128,1536]{1,0:T(8,128)(2,1)S(1)}, u32[]{:S(2)}, u32[]{:S(2)}) collective-permute-start(bf16[128,1536]{1,0:T(8,128)(2,1)} %get-tuple-element.61.refs_3_), channel_id=1, source_target_pairs={{0,1},{1,0},{2,3},{3,2},{4,5},{5,4},{6,7},{7,6},{8,9},{9,8},{10,11... | collective-permute-start | bytes 1179656 | tf_op jit(solution)/shard_map/ppermute | solution.py:1147
  69.3 20.6 %collective-permute-start.9 = (bf16[128,2048]{1,0:T(8,128)(2,1)}, bf16[128,2048]{1,0:T(8,128)(2,1)}, u32[]{:S(2)}, u32[]{:S(2)}) collective-permute-start(bf16[128,2048]{1,0:T(8,128)(2,1)} %get-tuple-element.71.refs_3_), channel_id=1, source_target_pairs={{0,2},{2,0},{4,6},{6,4},{8,10},{10,8},{12,14},{14,12},{16,18},{18,... | collective-permute-start | bytes 1572872 | tf_op jit(solution)/shard_map/ppermute | solution.py:1040
  69.9 17.1 %collective-permute-start.8 = (bf16[128,512]{1,0:T(8,128)(2,1)S(1)}, bf16[128,512]{1,0:T(8,128)(2,1)S(1)}, u32[]{:S(2)}, u32[]{:S(2)}) collective-permute-start(bf16[128,512]{1,0:T(8,128)(2,1)S(1)} %copy-done.32), channel_id=1, source_target_pairs={{0,2},{2,0},{4,6},{6,4},{8,10},{10,8},{12,14},{14,12},{16,18},{18,... | collective-permute-start | bytes 393224 | tf_op jit(solution)/shard_map/ppermute | solution.py:1040
  71.4 18.5 %collective-permute-start.12 = (bf16[512,128]{1,0:T(8,128)(2,1)S(1)}, bf16[512,128]{1,0:T(8,128)(2,1)S(1)}, u32[]{:S(2)}, u32[]{:S(2)}) collective-permute-start(bf16[512,128]{1,0:T(8,128)(2,1)S(1)} %get-tuple-element.76.refs_11_), channel_id=1, source_target_pairs={{0,8},{2,10},{4,12},{6,14},{8,0},{10,2},{12,4},{14,6},{16,24},{18,... | collective-permute-start | bytes 393224 | tf_op jit(solution)/shard_map/ppermute | solution.py:1040
  77.7 15.0 %collective-permute-start.11 = (bf16[128,512]{1,0:T(8,128)(2,1)}, bf16[128,512]{1,0:T(8,128)(2,1)S(1)}, u32[]{:S(2)}, u32[]{:S(2)}) collective-permute-start(bf16[128,512]{1,0:T(8,128)(2,1)} %get-tuple-element.75), channel_id=1, source_target_pairs={{0,8},{2,10},{4,12},{6,14},{8,0},{10,2},{12,4},{14,6},{16,24},{18,... | collective-permute-start | bytes 393224 | tf_op jit(solution)/shard_map/ppermute | solution.py:1040
  78.4 20.4 %all-to-all-start.2 = ((bf16[16,32,128]{2,1,0:T(8,128)(2,1)}), bf16[16,32,128]{2,1,0:T(8,128)(2,1)S(1)}, u32[]{:S(2)}, u32[]{:S(2)}) async-start(bf16[16,32,128]{2,1,0:T(8,128)(2,1)} %get-tuple-element.66), calls=%async_computation.2 | async-start | bytes 262144 | tf_op jit(solution)/shard_map/all_to_all | solution.py:1148
  87.0 26.9 %collective-permute-start.15 = (bf16[1024,512]{1,0:T(8,128)(2,1)}, bf16[1024,512]{1,0:T(8,128)(2,1)S(1)}, u32[]{:S(2)}, u32[]{:S(2)}) collective-permute-start(bf16[1024,512]{1,0:T(8,128)(2,1)} %get-tuple-element.81.refs_5_), channel_id=1, source_target_pairs={{0,4},{2,6},{4,0},{6,2},{8,12},{10,14},{12,8},{14,10},{16,20},{18,... | collective-permute-start | bytes 3145736 | tf_op jit(solution)/shard_map/ppermute | solution.py:1040
  97.6 49.2 %collective-permute-start.14 = (bf16[256,2560]{1,0:T(8,128)(2,1)}, bf16[256,2560]{1,0:T(8,128)(2,1)}, u32[]{:S(2)}, u32[]{:S(2)}) collective-permute-start(bf16[256,2560]{1,0:T(8,128)(2,1)} %get-tuple-element.79), channel_id=1, source_target_pairs={{0,2},{2,0},{4,6},{6,4},{8,10},{10,8},{12,14},{14,12},{16,18},{18,... | collective-permute-start | bytes 3932168 | tf_op jit(solution)/shard_map/ppermute | solution.py:1040
  106.7 27.4 %all-to-all-start.3 = ((bf16[16,160,128]{2,1,0:T(8,128)(2,1)}), bf16[16,160,128]{2,1,0:T(8,128)(2,1)S(1)}, u32[]{:S(2)}, u32[]{:S(2)}) async-start(bf16[16,160,128]{2,1,0:T(8,128)(2,1)} %get-tuple-element.78), calls=%async_computation.3 | async-start | bytes 1310720 | tf_op jit(solution)/shard_map/all_to_all | solution.py:1148
  110.3 3.6 %collective-permute-start.16 = (bf16[1024,512]{1,0:T(8,128)(2,1)S(1)}, bf16[1024,512]{1,0:T(8,128)(2,1)S(1)}, u32[]{:S(2)}, u32[]{:S(2)}) collective-permute-start(bf16[1024,512]{1,0:T(8,128)(2,1)S(1)} %copy-done.19), channel_id=1, source_target_pairs={{0,1},{1,0},{2,3},{3,2},{4,5},{5,4},{6,7},{7,6},{8,9},{9,8},{10,11... | collective-permute-start | bytes 3145736 | tf_op jit(solution)/shard_map/ppermute | solution.py:1147
  113.8 2.7 %collective-permute-start.17 = (bf16[1024,512]{1,0:T(8,128)(2,1)S(1)}, bf16[1024,512]{1,0:T(8,128)(2,1)S(1)}, u32[]{:S(2)}, u32[]{:S(2)}) collective-permute-start(bf16[1024,512]{1,0:T(8,128)(2,1)S(1)} %collective-permute-done.15.refs_6_), channel_id=1, source_target_pairs={{0,1},{1,0},{2,3},{3,2},{4,5},{5,4},{6,7},{7,6},{8,9},{9,8},{10,11... | collective-permute-start | bytes 3145736 | tf_op jit(solution)/shard_map/ppermute | solution.py:1147
  113.8 32.9 %collective-permute-start.13 = (bf16[256,2048]{1,0:T(8,128)(2,1)}, bf16[256,2048]{1,0:T(8,128)(2,1)}, u32[]{:S(2)}, u32[]{:S(2)}) collective-permute-start(bf16[256,2048]{1,0:T(8,128)(2,1)} %get-tuple-element.77.refs_6_), channel_id=1, source_target_pairs={{0,4},{2,6},{4,0},{6,2},{8,12},{10,14},{12,8},{14,10},{16,20},{18,... | collective-permute-start | bytes 3145736 | tf_op jit(solution)/shard_map/ppermute | solution.py:1040
  134.1 35.2 %all-to-all-start.4 = ((bf16[16,96,128]{2,1,0:T(8,128)(2,1)}), bf16[16,96,128]{2,1,0:T(8,128)(2,1)}, u32[]{:S(2)}, u32[]{:S(2)}) async-start(bf16[16,96,128]{2,1,0:T(8,128)(2,1)} %shard_map.262.refs_15_), calls=%async_computation.4 | async-start | bytes 786432 | tf_op jit(solution)/shard_map/all_to_all | solution.py:1148
  152.3 17.0 %collective-permute-start.20 = (bf16[128,2560]{1,0:T(8,128)(2,1)}, bf16[128,2560]{1,0:T(8,128)(2,1)}, u32[]{:S(2)}, u32[]{:S(2)}) collective-permute-start(bf16[128,2560]{1,0:T(8,128)(2,1)} %get-tuple-element.87), channel_id=1, source_target_pairs={{0,4},{2,6},{4,0},{6,2},{8,12},{10,14},{12,8},{14,10},{16,20},{18,... | collective-permute-start | bytes 1966088 | tf_op jit(solution)/shard_map/ppermute | solution.py:1040
  153.1 13.5 %collective-permute-start.19 = (bf16[128,2048]{1,0:T(8,128)(2,1)}, bf16[128,2048]{1,0:T(8,128)(2,1)}, u32[]{:S(2)}, u32[]{:S(2)}) collective-permute-start(bf16[128,2048]{1,0:T(8,128)(2,1)} %get-tuple-element.82.refs_2_), channel_id=1, source_target_pairs={{0,8},{2,10},{4,12},{6,14},{8,0},{10,2},{12,4},{14,6},{16,24},{18,... | collective-permute-start | bytes 1572872 | tf_op jit(solution)/shard_map/ppermute | solution.py:1040
  157.6 14.9 %collective-permute-start.18 = (bf16[128,1024]{1,0:T(8,128)(2,1)}, bf16[128,1024]{1,0:T(8,128)(2,1)S(1)}, u32[]{:S(2)}, u32[]{:S(2)}) collective-permute-start(bf16[128,1024]{1,0:T(8,128)(2,1)} %get-tuple-element.83.refs_2_), channel_id=1, source_target_pairs={{0,1},{1,0},{2,3},{3,2},{4,5},{5,4},{6,7},{7,6},{8,9},{9,8},{10,11... | collective-permute-start | bytes 786440 | tf_op jit(solution)/shard_map/ppermute | solution.py:1147
  172.4 29.6 %collective-permute-start.21 = (bf16[64,4608]{1,0:T(8,128)(2,1)}, bf16[64,4608]{1,0:T(8,128)(2,1)S(1)}, u32[]{:S(2)}, u32[]{:S(2)}) collective-permute-start(bf16[64,4608]{1,0:T(8,128)(2,1)} %get-tuple-element.88.refs_6_), channel_id=1, source_target_pairs={{0,16},{2,18},{4,20},{6,22},{8,24},{10,26},{12,28},{14,30},{16,0},... | collective-permute-start | bytes 1769480 | tf_op jit(solution)/shard_map/ppermute | solution.py:1040
  177.6 22.5 %all-to-all-start.5 = ((f32[16,1,384]{2,1,0:T(1,128)}), f32[16,1,384]{2,1,0:T(1,128)S(1)}, u32[]{:S(2)}, u32[]{:S(2)}) async-start(f32[16,1,384]{2,1,0:T(1,128)} %reshape.137), calls=%async_computation.5 | async-start | bytes 49152 | tf_op jit(solution)/shard_map/all_to_all | solution.py:1148
  (31 other events, 170.8 us)

commit v3 on v2

--- a/solution.py
+++ b/solution.py
@@ -635,6 +635,9 @@
     up_ref,
     b_up_ref,
     down_ref,
+    line_ref,
+    line_x_ref,
+    attn_ref,
     middle_ref,
     act_ref,
     back_ref,
@@ -642,6 +645,7 @@
     b_grad_ref,
     share_ref,
     swap_ref,
+    joined_ref,
     hidden_ref,
     turn_ref,
     grad_acc,
@@ -661,11 +665,15 @@
         middle_ref[...] = middle
         normed, _ = norm_stats(middle.astype(jnp.bfloat16).astype(jnp.float32))
         hidden_ref[...] = (normed * gain_ref[...] + bias_ref[...]).astype(jnp.bfloat16)
+        put_rows(joined_ref, line_ref, line_x_ref)
         turn_ref[...] = hidden_ref[...].astype(jnp.float32).T.astype(jnp.bfloat16)
         bit = (place_ref[0] >> UP_BITS[0]) & 1
         put_stripes(mine_ref, 0, turn_ref, UP_BITS[0], UP_BITS[1:], bit)
-        first = back_ref.shape[1] - mine_ref.shape[1]
+        first = back_ref.shape[1] - mine_ref.shape[1] - width
         put_stripes(back_ref, first, turn_ref, UP_BITS[0], UP_BITS[1:], 1 - bit)
+        first += mine_ref.shape[1]
+        for part in range(0, width, rows):
+            back_ref[:, first + part : first + part + rows] = attn_ref[part : part + rows, :]
         grad_acc[...] = jnp.zeros_like(grad_acc)
         mlp_acc[...] = jnp.zeros_like(mlp_acc)
 
@@ -709,20 +717,16 @@
     gain_ref,
     b_down_ref,
     w_out_ref,
-    line_ref,
-    line_x_ref,
     mixed_ref,
     grad_ref,
     send_ref,
     mine_ref,
     theirs_ref,
     small_ref,
-    joined_ref,
     wide_ref,
     turn_ref,
 ):
     rows, width = mixed_ref.shape
-    put_rows(joined_ref, line_ref, line_x_ref)
     own = pl.ds(pl.multiple_of(rank_ref[0] * width, width), width)
     mixed_ref[...] = (
         middle_ref[:, own]
@@ -947,7 +951,20 @@
     turned, columns, got_first = piece
     half = left_ref.shape[1] // 2
     if turned:
-        right = jnp.concatenate([right_ref[...], right_got_ref[...]], axis=1)
+        first, tokens = right_got_ref.shape[1] - columns, right_ref.shape[1]
+        right = jnp.concatenate(
+            [
+                jnp.concatenate(
+                    [
+                        right_ref[part : part + tokens, :],
+                        right_got_ref[:, first + part : first + part + tokens],
+                    ],
+                    axis=1,
+                )
+                for part in range(0, columns, tokens)
+            ],
+            axis=0,
+        )
     else:
         right = jnp.concatenate([right_ref[:, 0:columns], right_got_ref[:, 0:columns]], axis=0)
     left = jnp.concatenate(
@@ -1208,6 +1225,7 @@
         ],
         [slope, side, got, tokens, far, near, corner],
         scratch=[pltpu.VMEM((all_tokens, HDIM), bf16)],
+        after=[cot_got],
         mebibytes=24,
         flops=4 * 10**9,
     )
@@ -1220,16 +1238,17 @@
         scratch=[pltpu.VMEM((rows, model), f32)],
     )
     chunk = 512
-    middle, act, grad_pre, h_mine, grad_b_up, share, swap = call(
+    middle, act, grad_pre, h_mine, grad_b_up, share, swap, plane = call(
         mlp_kernel,
         [
             ((rows, model), f32),
             ((rows, hidden), bf16),
-            ((rows, hidden + model // 2), bf16),
+            ((rows, hidden + model // 2 + width), bf16),
             ((rows, model // 2), bf16),
             ((1, hidden), f32),
             ((rows, width), f32),
             ((rows, model + width), bf16),
+            ((8 * rows, width), bf16),
         ],
         [
             rank,
@@ -1243,6 +1262,9 @@
             w_up,
             b_up.reshape(1, hidden),
             w_down,
+            line,
+            line_x,
+            attn_turned,
         ],
         grid=(hidden // chunk,),
         in_specs=[smem, smem]
@@ -1253,15 +1275,19 @@
             pl.BlockSpec((model, chunk), lambda step: (0, step)),
             pl.BlockSpec((1, chunk), lambda step: (0, step)),
             pl.BlockSpec((chunk, model), lambda step: (step, 0)),
+            whole(4 * rows, width),
+            whole(4 * rows, width),
+            whole(width, rows),
         ],
         out_specs=[
             whole(rows, model),
             pl.BlockSpec((rows, chunk), lambda step: (0, step)),
-            whole(rows, hidden + model // 2),
+            whole(rows, hidden + model // 2 + width),
             whole(rows, model // 2),
             pl.BlockSpec((1, chunk), lambda step: (0, step)),
             whole(rows, width),
             whole(rows, model + width),
+            whole(8 * rows, width),
         ],
         scratch=[
             pltpu.VMEM((rows, model), bf16),
@@ -1272,7 +1298,9 @@
         mebibytes=56,
         flops=7 * 10**9,
     )
-    mixed, grad_mid, grad_sent, low_mine, out_theirs, small_two, plane = call(
+    gathered = [plane, swap_over(plane, bit_y, count)]
+    gathered += [other_core(value) for value in gathered]
+    mixed, grad_mid, grad_sent, low_mine, out_theirs, small_two = call(
         middle_kernel,
         [
             ((rows, width), bf16),
@@ -1281,7 +1309,6 @@
             ((rows, model // 2), bf16),
             ((rows, model // 2), bf16),
             ((8, width), f32),
-            ((8 * rows, width), bf16),
         ],
         [
             rank,
@@ -1294,8 +1321,6 @@
             gain_two,
             b_down.reshape(1, width),
             w_out,
-            line,
-            line_x,
         ],
         scratch=[pltpu.VMEM((rows + 8, model), f32), pltpu.VMEM((model, rows), bf16)],
         mebibytes=60,
@@ -1312,12 +1337,10 @@
         [cot_mine, cot_got, act, swap_over(act, DOWN_BITS[0], count)]
         + [h_mine, back_other, grad_pre, back_other]
         + [low_mine, swap_over(out_theirs, UP_BITS[0], count)]
-        + [attn_turned, swap_over(attn_turned, UP_BITS[0], count)],
+        + [attn_turned, back_other],
     )
     grad_got = to_heads(grad_sent)
-    gathered = [plane, swap_over(plane, bit_y, count)]
-    gathered += [other_core(value) for value in gathered]
-    first_sent = reductions.first([])
+    first_sent = reductions.first([grad_got, gathered[1]])
     back_sent, back_low = call(
         backward_kernel,
         [((count, SEG_ROW, rows), bf16), ((3 * HDIM, all_tokens), bf16)],
@@ -1328,7 +1351,7 @@
             pltpu.VMEM((HDIM, all_tokens), f32),
             pltpu.VMEM((HDIM, all_tokens), f32),
         ],
-        after=[first_sent[0]],
+        after=[first_sent[0]] + gathered[2:],
         mebibytes=56,
         flops=10**10,
     )
@@ -1346,7 +1369,7 @@
     )
     weight_got = to_heads(weight_sent)
     second_sent = reductions.second([weight_sent])
-    third_sent = reductions.third([weight_got])
+    third_sent = reductions.third([])
     back_got = to_heads(back_sent)
     part_one, sums = call(
         hidden_kernel,

time: 206 us -> 201 us (0.976)
  waiting for transfers between devices: 73.9 us -> 51.8 us
  starting transfers between devices: 40.8 us -> 54.1 us
  Pallas kernels: 58 us -> 60.3 us
    all_to_all x5, waiting for transfers between devices: 25.6 us -> 5.94 us  [on_device_paired(): to_heads = lambda value: lax.all_to_all(value, 'ctx', 0, 0, tiled=True)]
    all_to_all x5, starting transfers between devices: 22.4 us -> 29.1 us  [on_device_paired(): to_heads = lambda value: lax.all_to_all(value, 'ctx', 0, 0, tiled=True)]
    ppermute x15 -> x14, starting transfers between devices: 17.6 us -> 23.8 us  [swap_over(): lax.ppermute(value, 'ctx', [(place, place ^ 1 << bit) for place in range(...]
    ppermute x15 -> x14, waiting for transfers between devices: 45.3 us -> 39.1 us  [swap_over(): lax.ppermute(value, 'ctx', [(place, place ^ 1 << bit) for place in range(...]
    ppermute x7, waiting for transfers between devices: 2.92 us -> 6.78 us  [on_device_paired(): other_core = lambda value: lax.ppermute(value, 'tp', [(0, 1), (1, 0)])]
    pallas_call x13, Pallas kernels: 58 us -> 60.3 us  [call(): pl.pallas_call(body, out_shape=[jax.ShapeDtypeStruct(shape, dtype) for sh...]
    unnamed x72 -> x76, local copies, waits for them, and re-layouts: 11.3 us -> 12.1 us
  transfers between devices with their start and end apart: 27 -> 26, of which waited for: 14 -> 14; matrix products, arithmetic and copies ran while one was open for 4% -> 3% of each run, Pallas kernels for 25% -> 21%
where the time goes in v3:
time: 201 us; the launch traced here: 199 us
  Pallas kernels  60.3 us (30%)
  starting transfers between devices  54.1 us (27%)
  waiting for transfers between devices  51.8 us (26%)
  local copies, waits for them, and re-layouts  17.3 us (9%)
  blocking collectives  13.1 us (7%)
    pallas_call x13, Pallas kernels, call(): pl.pallas_call(body, out_shape=[jax.ShapeDtypeStruct(shape, dtype) for sh...  60.3 us
    ppermute x14, waiting for transfers between devices, swap_over(): lax.ppermute(value, 'ctx', [(place, place ^ 1 << bit) for place in range(...  39.1 us
    all_to_all x5, starting transfers between devices, on_device_paired(): to_heads = lambda value: lax.all_to_all(value, 'ctx', 0, 0, tiled=True)  29.1 us
    ppermute x14, starting transfers between devices, swap_over(): lax.ppermute(value, 'ctx', [(place, place ^ 1 << bit) for place in range(...  23.8 us
    all_to_all x1, blocking collectives, on_device_paired(): to_heads = lambda value: lax.all_to_all(value, 'ctx', 0, 0, tiled=True)  13.1 us
    unnamed x76, local copies, waits for them, and re-layouts  12.1 us
    ppermute x7, waiting for transfers between devices, on_device_paired(): other_core = lambda value: lax.ppermute(value, 'tp', [(0, 1), (1, 0)])  6.78 us
    all_to_all x5, waiting for transfers between devices, on_device_paired(): to_heads = lambda value: lax.all_to_all(value, 'ctx', 0, 0, tiled=True)  5.94 us
  transfers between devices with their start and end apart: 26, of which 14 were waited for; matrix products, arithmetic and copies ran while one was open for 3% of the time, Pallas kernels for 21%

profile of v3, /device:TPU:0, one launch (start us, length us, event | category | flops | bytes accessed | tf_op | source)
XLA Modules:
  0.0 199.4 jit_solution(15173618731531852717)
XLA Ops:
  1.2 4.0 %collective-permute-start.2 = (bf16[128,512]{1,0:T(8,128)(2,1)}, bf16[128,512]{1,0:T(8,128)(2,1)S(1)}, u32[]{:S(2)}, u32[]{:S(2)}) collective-permute-start(bf16[128,512]{1,0:T(8,128)(2,1)} %refs_3_.1), channel_id=1, source_target_pairs={{0,16},{2,18},{4,20},{6,22},{8,24},{10,26},{12,28},{14,30},{16,0},... | collective-permute-start | bytes 393224 | tf_op jit(solution)/shard_map/ppermute | solution.py:1057
  7.5 5.2 %shard_map.254 = (bf16[16,176,128]{2,1,0:T(8,128)(2,1)}, bf16[128,1024]{1,0:T(8,128)(2,1)}, bf16[128,1024]{1,0:T(8,128)(2,1)}, bf16[128,512]{1,0:T(8,128)(2,1)}, bf16[128,512]{1,0:T(8,128)(2,1)}) custom-call(s32[1]{0:T(128)} %bitcast.refs_0_, s32[1]{0:T(128)} %bitcast.1.refs_1_.refs_0_, bf16[128,512]{1,0:T(8,128)(2,1)} %refs_3_.1, ...), custom_call_target="tpu_custom_call" | custom-call | flops 300000 | bytes 1024 | tf_op jit(solution)/shard_map/pallas_call | solution.py:927
  13.5 6.1 %all-to-all-start = ((bf16[16,176,128]{2,1,0:T(8,128)(2,1)}), bf16[16,176,128]{2,1,0:T(8,128)(2,1)S(1)}, u32[]{:S(2)}, u32[]{:S(2)}) async-start(bf16[16,176,128]{2,1,0:T(8,128)(2,1)} %shard_map.255), calls=%async_computation | async-start | bytes 1441792 | tf_op jit(solution)/shard_map/all_to_all | solution.py:1165
  19.5 2.0 collective-permute-start.5
  23.0 4.1 %collective-permute-done.5.refs_7_.refs_2_ = bf16[128,512]{1,0:T(8,128)(2,1)S(1)} collective-permute-done((bf16[128,512]{1,0:T(8,128)(2,1)S(1)}, bf16[128,512]{1,0:T(8,128)(2,1)S(1)}, u32[]{:S(2)}, u32[]{:S(2)}) %collective-permute-start.5) | collective-permute-done | bytes 131104 | tf_op jit(solution)/shard_map/ppermute | solution.py:1057
  27.1 8.3 %collective-permute-done.4.refs_6_ = bf16[128,512]{1,0:T(8,128)(2,1)S(1)} collective-permute-done((bf16[128,512]{1,0:T(8,128)(2,1)}, bf16[128,512]{1,0:T(8,128)(2,1)S(1)}, u32[]{:S(2)}, u32[]{:S(2)}) %collective-permute-start.4) | collective-permute-done | bytes 131104 | tf_op jit(solution)/shard_map/ppermute | solution.py:1057
  35.4 2.8 %all-to-all-done.refs_2_ = bf16[16,176,128]{2,1,0:T(8,128)(2,1)S(1)} async-done(((bf16[16,176,128]{2,1,0:T(8,128)(2,1)}), bf16[16,176,128]{2,1,0:T(8,128)(2,1)S(1)}, u32[]{:S(2)}, u32[]{:S(2)}) %all-to-all-start) | async-done | bytes 720928 | tf_op jit(solution)/shard_map/all_to_all | solution.py:1165
  40.1 3.9 %shard_map.256 = (bf16[16,32,128]{2,1,0:T(8,128)(2,1)S(1)}, f32[64,1024]{1,0:T(8,128)S(1)}, f32[1,1024]{1,0:T(1,128)S(1)}, bf16[512,512]{1,0:T(8,128)(2,1)S(1)}) custom-call(f32[1]{0:T(128)} %bitcast.5.refs_0_, s32[1]{0:T(128)} %bitcast.6.refs_1_, bf16[16,176,128]{2,1,0:T(8,128)(2,1)S(1)} %all-to-all-done.refs_2_, bf16[128,512]{1,0:T(8,128)(2,1)S(1)} %copy-done.7, ...), custom_call_target="tpu_custom_call" | custom-call | flops 400000 | bytes 1024 | tf_op jit(solution)/shard_map/pallas_call | solution.py:927
  44.9 13.1 %all_to_all.30.refs_1_ = bf16[16,32,128]{2,1,0:T(8,128)(2,1)S(1)} all-to-all(bf16[16,32,128]{2,1,0:T(8,128)(2,1)S(1)} %get-tuple-element.60), channel_id=1, replica_groups=mesh['ctx'=16,'tp'=2] {'ctx'}, dimensions={0} | all-to-all | bytes 262144 | tf_op jit(solution)/shard_map/all_to_all | solution.py:1165
  61.6 10.0 %shard_map.258 = (f32[128,1024]{1,0:T(8,128)}, bf16[128,2048]{1,0:T(8,128)(2,1)}, bf16[128,3072]{1,0:T(8,128)(2,1)}, bf16[128,512]{1,0:T(8,128)(2,1)}, f32[1,204...) custom-call(s32[1]{0:T(128)} %bitcast.refs_0_, ...), custom_call_target="tpu_custom_call" | custom-call | flops 700000 | bytes 1024 | tf_op jit(solution)/shard_map/pallas_call | solution.py:927
  72.4 2.5 %collective-permute-start.10 = (bf16[128,3072]{1,0:T(8,128)(2,1)}, bf16[128,3072]{1,0:T(8,128)(2,1)S(1)}, u32[]{:S(2)}, u32[]{:S(2)}) collective-permute-start(bf16[128,3072]{1,0:T(8,128)(2,1)} %get-tuple-element.74.refs_7_), channel_id=1, source_target_pairs={{0,8},{2,10},{4,12},{6,14},{8,0},{10,2},{12,4},{14,6},{16,24},{18,... | collective-permute-start | bytes 2359304 | tf_op jit(solution)/shard_map/ppermute | solution.py:1057
  77.6 3.6 %shard_map.259 = (bf16[128,512]{1,0:T(8,128)(2,1)}, f32[128,512]{1,0:T(8,128)}, bf16[16,32,128]{2,1,0:T(8,128)(2,1)}, bf16[128,512]{1,0:T(8,128)(2,1)}, bf16[128,512]{1,0:T(8,128)(2,1)}, /*index=5*/f32[8,512]{1,0:T(8,128)}) custom-call(s32[1]{0:T(128)} %bitcast.refs_0_, s32[1]{0:T(128)} %bitcast.1.refs_1_.refs_0_, ...), custom_call_target="tpu_custom_call" | custom-call | flops 200000 | bytes 1024 | tf_op jit(solution)/shard_map/pallas_call | solution.py:927
  81.2 4.1 %all-to-all-start.2 = ((bf16[16,32,128]{2,1,0:T(8,128)(2,1)}), bf16[16,32,128]{2,1,0:T(8,128)(2,1)S(1)}, u32[]{:S(2)}, u32[]{:S(2)}) async-start(bf16[16,32,128]{2,1,0:T(8,128)(2,1)} %get-tuple-element.68), calls=%async_computation.2 | async-start | bytes 262144 | tf_op jit(solution)/shard_map/all_to_all | solution.py:1165
  87.3 10.3 %collective-permute-done.11.refs_10_ = bf16[128,512]{1,0:T(8,128)(2,1)S(1)} collective-permute-done((bf16[128,512]{1,0:T(8,128)(2,1)}, bf16[128,512]{1,0:T(8,128)(2,1)S(1)}, u32[]{:S(2)}, u32[]{:S(2)}) %collective-permute-start.11) | collective-permute-done | bytes 131104 | tf_op jit(solution)/shard_map/ppermute | solution.py:1057
  99.8 4.4 %shard_map.260 = (bf16[256,2048]{1,0:T(8,128)(2,1)}, bf16[256,2560]{1,0:T(8,128)(2,1)}) custom-call(s32[1]{0:T(128)} %bitcast.1.refs_1_.refs_0_, bf16[128,512]{1,0:T(8,128)(2,1)} %get-tuple-element.71.refs_1_, bf16[128,512]{1,0:T(8,128)(2,1)} %copy-done.16, bf16[128,2048]{1,0:T(8,128)(2,1)} %get-tuple-element.72.refs_3_, bf16[128,2048]{1,0:T(8,128)(2,1)} %copy-done.35, ...), custom_call_target="tpu_custom_call" | custom-call | flops 99999997952 | bytes 1024 | tf_op jit(solution)/shard_map/pallas_call | solution.py:927
  106.0 3.3 %collective-permute-done.13.refs_7_ = bf16[1024,512]{1,0:T(8,128)(2,1)S(1)} collective-permute-done((bf16[1024,512]{1,0:T(8,128)(2,1)S(1)}, bf16[1024,512]{1,0:T(8,128)(2,1)S(1)}, u32[]{:S(2)}, u32[]{:S(2)}) %collective-permute-start.13) | collective-permute-done | bytes 1048608 | tf_op jit(solution)/shard_map/ppermute | solution.py:1164
  110.7 7.3 %shard_map.261 = (bf16[16,160,128]{2,1,0:T(8,128)(2,1)}, bf16[192,2048]{1,0:T(8,128)(2,1)}) custom-call(f32[1]{0:T(128)} %bitcast.5.refs_0_, s32[1]{0:T(128)} %bitcast.6.refs_1_, bf16[16,176,128]{2,1,0:T(8,128)(2,1)} %copy-done.1, bf16[16,32,128]{2,1,0:T(8,128)(2,1)} %copy-done.25, f32[64,1024]{1,0:T(8,128)} %copy-done.12, f32[1,1024]{1,0:T(1,128)} %copy-done.18, ...), custom_call_target="tpu_custom_call" | custom-call | flops 1000000 | bytes 1024 | tf_op jit(solution)/shard_map/pallas_call | solution.py:927
  117.9 5.3 %all-to-all-start.3 = ((bf16[16,160,128]{2,1,0:T(8,128)(2,1)}), bf16[16,160,128]{2,1,0:T(8,128)(2,1)}, u32[]{:S(2)}, u32[]{:S(2)}) async-start(bf16[16,160,128]{2,1,0:T(8,128)(2,1)} %get-tuple-element.79), calls=%async_computation.3 | async-start | bytes 1310720 | tf_op jit(solution)/shard_map/all_to_all | solution.py:1165
  123.2 8.4 %shard_map.262.refs_15_ = bf16[16,96,128]{2,1,0:T(8,128)(2,1)} custom-call(s32[1]{0:T(128)} %bitcast.refs_0_, s32[1]{0:T(128)} %bitcast.1.refs_1_.refs_0_, f32[1,1024]{1,0:T(1,128)} %bitcast.43, f32[1,1024]{1,0:T(1,128)} %bitcast.52, bf16[192,2048]{1,0:T(8,128)(2,1)} %get-tuple-element.81.refs_4_, bf16[1024,512]{1,0:T(8,128)(2,1)} %get-tuple-element.77.refs_5_, ...), custom_call_target="tpu_custom_call" | custom-call | flops 600000 | bytes 1024 | tf_op jit(solution)/shard_map/pallas_call | solution.py:927
  131.6 2.9 %collective-permute-done.15.refs_13_ = bf16[256,2048]{1,0:T(8,128)(2,1)S(1)} collective-permute-done((bf16[256,2048]{1,0:T(8,128)(2,1)}, bf16[256,2048]{1,0:T(8,128)(2,1)S(1)}, u32[]{:S(2)}, u32[]{:S(2)}) %collective-permute-start.15) | collective-permute-done | bytes 1048608 | tf_op jit(solution)/shard_map/ppermute | solution.py:1057
  134.5 5.7 %collective-permute-done.16.refs_14_ = bf16[256,2560]{1,0:T(8,128)(2,1)S(1)} collective-permute-done((bf16[256,2560]{1,0:T(8,128)(2,1)}, bf16[256,2560]{1,0:T(8,128)(2,1)S(1)}, u32[]{:S(2)}, u32[]{:S(2)}) %collective-permute-start.16) | collective-permute-done | bytes 1310752 | tf_op jit(solution)/shard_map/ppermute | solution.py:1057
  141.3 6.1 %shard_map.263 = (bf16[128,2048]{1,0:T(8,128)(2,1)}, bf16[128,2560]{1,0:T(8,128)(2,1)}, bf16[128,2048]{1,0:T(8,128)(2,1)}, bf16[128,2560]{1,0:T(8,128)(2,1)}) custom-call(s32[1]{0:T(128)} %bitcast.1.refs_1_.refs_0_, bf16[128,512]{1,0:T(8,128)(2,1)} %get-tuple-element.71.refs_1_, bf16[128,512]{1,0:T(8,128)(2,1)} %copy-done.16, ...), custom_call_target="tpu_custom_call" | custom-call | flops 99999997952 | bytes 1024 | tf_op jit(solution)/shard_map/pallas_call | solution.py:927
  147.5 3.4 %collective-permute-start.18 = (bf16[128,2048]{1,0:T(8,128)(2,1)}, bf16[128,2048]{1,0:T(8,128)(2,1)}, u32[]{:S(2)}, u32[]{:S(2)}) collective-permute-start(bf16[128,2048]{1,0:T(8,128)(2,1)} %get-tuple-element.82.refs_2_), channel_id=1, source_target_pairs={{0,8},{2,10},{4,12},{6,14},{8,0},{10,2},{12,4},{14,6},{16,24},{18,... | collective-permute-start | bytes 1572872 | tf_op jit(solution)/shard_map/ppermute | solution.py:1057
  150.9 4.2 %all-to-all-start.5 = ((bf16[16,96,128]{2,1,0:T(8,128)(2,1)}), bf16[16,96,128]{2,1,0:T(8,128)(2,1)}, u32[]{:S(2)}, u32[]{:S(2)}) async-start(bf16[16,96,128]{2,1,0:T(8,128)(2,1)} %shard_map.262.refs_15_), calls=%async_computation.5 | async-start | bytes 786432 | tf_op jit(solution)/shard_map/all_to_all | solution.py:1165
  155.1 7.8 %collective-permute-done.18.refs_3_ = bf16[128,2048]{1,0:T(8,128)(2,1)} collective-permute-done((bf16[128,2048]{1,0:T(8,128)(2,1)}, bf16[128,2048]{1,0:T(8,128)(2,1)}, u32[]{:S(2)}, u32[]{:S(2)}) %collective-permute-start.18) | collective-permute-done | bytes 524320 | tf_op jit(solution)/shard_map/ppermute | solution.py:1057
  163.0 3.2 %shard_map.265 = (bf16[64,4608]{1,0:T(8,128)(2,1)}, bf16[64,4608]{1,0:T(8,128)(2,1)}) custom-call(s32[1]{0:T(128)} %bitcast.1.refs_1_.refs_0_, bf16[128,2048]{1,0:T(8,128)(2,1)} %get-tuple-element.85.refs_1_, bf16[128,2560]{1,0:T(8,128)(2,1)} %get-tuple-element.86.refs_2_, bf16[128,2048]{1,0:T(8,128)(2,1)} %collective-permute-done.18.refs_3_, ...), custom_call_target="tpu_custom_call" | custom-call | flops 200000 | bytes 1024 | tf_op jit(solution)/shard_map/pallas_call | solution.py:927
  166.1 3.4 %collective-permute-start.20 = (bf16[64,4608]{1,0:T(8,128)(2,1)}, bf16[64,4608]{1,0:T(8,128)(2,1)}, u32[]{:S(2)}, u32[]{:S(2)}) collective-permute-start(bf16[64,4608]{1,0:T(8,128)(2,1)} %get-tuple-element.88.refs_6_), channel_id=1, source_target_pairs={{0,16},{2,18},{4,20},{6,22},{8,24},{10,26},{12,28},{14,30},{16,0},... | collective-permute-start | bytes 1769480 | tf_op jit(solution)/shard_map/ppermute | solution.py:1057
  170.6 3.4 %shard_map.264 = (bf16[128,1024]{1,0:T(8,128)(2,1)}, f32[3,8,512]{2,1,0:T(8,128)S(1)}) custom-call(bf16[16,160,128]{2,1,0:T(8,128)(2,1)} %all-to-all-done.3.refs_0_, bf16[3,1024,512]{2,1,0:T(8,128)(2,1)S(1)} %copy-done, bf16[128,2048]{1,0:T(8,128)(2,1)S(1)} %copy-done.5), custom_call_target="tpu_custom_call" | custom-call | flops 300000 | bytes 1024 | tf_op jit(solution)/shard_map/pallas_call | solution.py:927
  177.8 2.1 %shard_map.266 = (bf16[128,512]{1,0:T(8,128)(2,1)}, f32[8,512]{1,0:T(8,128)S(1)}) custom-call(s32[1]{0:T(128)} %bitcast.refs_0_, bf16[128,1024]{1,0:T(8,128)(2,1)S(1)} %copy-done.3, bf16[128,1024]{1,0:T(8,128)(2,1)} %get-tuple-element.83.refs_2_, bf16[128,1024]{1,0:T(8,128)(2,1)S(1)} %collective-permute-done.17.refs_3_, f32[1,1024]{1,0:T(1,128)S(1)} %bitcast.44, ...), custom_call_target="tpu_custom_call" | custom-call | flops 10000 | bytes 1024 | tf_op jit(solution)/shard_map/pallas_call | solution.py:927
  180.8 9.4 %all-to-all-start.4 = ((f32[16,1,384]{2,1,0:T(1,128)}), f32[16,1,384]{2,1,0:T(1,128)S(1)}, u32[]{:S(2)}, u32[]{:S(2)}) async-start(f32[16,1,384]{2,1,0:T(1,128)} %reshape.137), calls=%async_computation.4 | async-start | bytes 49152 | tf_op jit(solution)/shard_map/all_to_all | solution.py:1165
  193.0 2.3 %shard_map.267 = (f32[64,2048]{1,0:T(8,128)}, f32[64,2048]{1,0:T(8,128)}, f32[64,512]{1,0:T(8,128)}) custom-call(bf16[64,4608]{1,0:T(8,128)(2,1)} %get-tuple-element.94.refs_0_, bf16[64,4608]{1,0:T(8,128)(2,1)} %collective-permute-done.20.refs_1_), custom_call_target="tpu_custom_call" | custom-call | flops 100000 | bytes 1024 | tf_op jit(solution)/shard_map/pallas_call | solution.py:927
  195.3 2.2 %all-to-all-done.4 = f32[16,1,384]{2,1,0:T(1,128)S(1)} async-done(((f32[16,1,384]{2,1,0:T(1,128)}), f32[16,1,384]{2,1,0:T(1,128)S(1)}, u32[]{:S(2)}, u32[]{:S(2)}) %all-to-all-start.4) | async-done | bytes 24608 | tf_op jit(solution)/shard_map/all_to_all | solution.py:1165
  (136 shorter events, 33.6 us)
Async XLA Ops:
  0.6 6.2 %collective-permute-start = (bf16[128,512]{1,0:T(8,128)(2,1)}, bf16[128,512]{1,0:T(8,128)(2,1)S(1)}, u32[]{:S(2)}, u32[]{:S(2)}) collective-permute-start(bf16[128,512]{1,0:T(8,128)(2,1)} %refs_3_.1), channel_id=1, source_target_pairs={{0,1},{1,0},{2,3},{3,2},{4,5},{5,4},{6,7},{7,6},{8,9},{9,8},{10,11... | collective-permute-start | bytes 393224 | tf_op jit(solution)/shard_map/ppermute | solution.py:1164
  1.2 5.7 %collective-permute-start.1 = (bf16[128,512]{1,0:T(8,128)(2,1)}, bf16[128,512]{1,0:T(8,128)(2,1)S(1)}, u32[]{:S(2)}, u32[]{:S(2)}) collective-permute-start(bf16[128,512]{1,0:T(8,128)(2,1)} %refs_4_.1), channel_id=1, source_target_pairs={{0,1},{1,0},{2,3},{3,2},{4,5},{5,4},{6,7},{7,6},{8,9},{9,8},{10,11... | collective-permute-start | bytes 393224 | tf_op jit(solution)/shard_map/ppermute | solution.py:1164
  1.2 11.5 %collective-permute-start.2 = (bf16[128,512]{1,0:T(8,128)(2,1)}, bf16[128,512]{1,0:T(8,128)(2,1)S(1)}, u32[]{:S(2)}, u32[]{:S(2)}) collective-permute-start(bf16[128,512]{1,0:T(8,128)(2,1)} %refs_3_.1), channel_id=1, source_target_pairs={{0,16},{2,18},{4,20},{6,22},{8,24},{10,26},{12,28},{14,30},{16,0},... | collective-permute-start | bytes 393224 | tf_op jit(solution)/shard_map/ppermute | solution.py:1057
  5.3 7.5 %collective-permute-start.3 = (bf16[128,512]{1,0:T(8,128)(2,1)}, bf16[128,512]{1,0:T(8,128)(2,1)S(1)}, u32[]{:S(2)}, u32[]{:S(2)}) collective-permute-start(bf16[128,512]{1,0:T(8,128)(2,1)} %refs_3_.1), channel_id=1, source_target_pairs={{0,8},{2,10},{4,12},{6,14},{8,0},{10,2},{12,4},{14,6},{16,24},{18,... | collective-permute-start | bytes 393224 | tf_op jit(solution)/shard_map/ppermute | solution.py:1057
  7.5 30.7 %copy-start.7 = (bf16[128,512]{1,0:T(8,128)(2,1)S(1)}, bf16[128,512]{1,0:T(8,128)(2,1)}, u32[]{:S(2)}) copy-start(bf16[128,512]{1,0:T(8,128)(2,1)} %refs_3_.1) | copy-start | bytes 393220
  12.7 45.3 %copy-start.2 = (bf16[512,1024]{1,0:T(8,128)(2,1)S(1)}, bf16[512,1024]{1,0:T(8,128)(2,1)}, u32[]{:S(2)}) copy-start(bf16[512,1024]{1,0:T(8,128)(2,1)} %refs_9_.3) | copy-start | bytes 3145732
  12.7 45.3 %copy-start.19 = (f32[512]{0:T(512)S(1)}, f32[512]{0:T(512)}, u32[]{:S(2)}) copy-start(f32[512]{0:T(512)} %param.22) | copy-start | bytes 6148
  13.5 24.7 %all-to-all-start = ((bf16[16,176,128]{2,1,0:T(8,128)(2,1)}), bf16[16,176,128]{2,1,0:T(8,128)(2,1)S(1)}, u32[]{:S(2)}, u32[]{:S(2)}) async-start(bf16[16,176,128]{2,1,0:T(8,128)(2,1)} %shard_map.255), calls=%async_computation | async-start | bytes 1441792 | tf_op jit(solution)/shard_map/all_to_all | solution.py:1165
  19.5 7.6 %collective-permute-start.5 = (bf16[128,512]{1,0:T(8,128)(2,1)S(1)}, bf16[128,512]{1,0:T(8,128)(2,1)S(1)}, u32[]{:S(2)}, u32[]{:S(2)}) collective-permute-start(bf16[128,512]{1,0:T(8,128)(2,1)S(1)} %copy-done.37), channel_id=1, source_target_pairs={{0,2},{2,0},{4,6},{6,4},{8,10},{10,8},{12,14},{14,12},{16,18},{18,... | collective-permute-start | bytes 393224 | tf_op jit(solution)/shard_map/ppermute | solution.py:1057
  21.5 13.9 %collective-permute-start.4 = (bf16[128,512]{1,0:T(8,128)(2,1)}, bf16[128,512]{1,0:T(8,128)(2,1)S(1)}, u32[]{:S(2)}, u32[]{:S(2)}) collective-permute-start(bf16[128,512]{1,0:T(8,128)(2,1)} %copy-done.8), channel_id=1, source_target_pairs={{0,8},{2,10},{4,12},{6,14},{8,0},{10,2},{12,4},{14,6},{16,24},{18,... | collective-permute-start | bytes 393224 | tf_op jit(solution)/shard_map/ppermute | solution.py:1057
  27.1 44.5 %copy-start.16 = (bf16[128,512]{1,0:T(8,128)(2,1)}, bf16[128,512]{1,0:T(8,128)(2,1)S(1)}, u32[]{:S(2)}) copy-start(bf16[128,512]{1,0:T(8,128)(2,1)S(1)} %collective-permute-done.5.refs_7_.refs_2_) | copy-start | bytes 393220
  38.2 33.5 %copy-start.1 = (bf16[16,176,128]{2,1,0:T(8,128)(2,1)}, bf16[16,176,128]{2,1,0:T(8,128)(2,1)S(1)}, u32[]{:S(2)}) copy-start(bf16[16,176,128]{2,1,0:T(8,128)(2,1)S(1)} %all-to-all-done.refs_2_) | copy-start | bytes 2162692
  44.1 16.6 %collective-permute-start.7 = (bf16[512,512]{1,0:T(8,128)(2,1)S(1)}, bf16[512,512]{1,0:T(8,128)(2,1)S(1)}, u32[]{:S(2)}, u32[]{:S(2)}) collective-permute-start(bf16[512,512]{1,0:T(8,128)(2,1)S(1)} %get-tuple-element.62.refs_11_), channel_id=1, source_target_pairs={{0,2},{2,0},{4,6},{6,4},{8,10},{10,8},{12,14},{14,12},{16,18},{18,... | collective-permute-start | bytes 1572872 | tf_op jit(solution)/shard_map/ppermute | solution.py:1057
  59.2 1.5 collective-permute-start.6
  71.7 26.9 %collective-permute-start.12 = (bf16[1024,512]{1,0:T(8,128)(2,1)}, bf16[1024,512]{1,0:T(8,128)(2,1)S(1)}, u32[]{:S(2)}, u32[]{:S(2)}) collective-permute-start(bf16[1024,512]{1,0:T(8,128)(2,1)} %get-tuple-element.77.refs_5_), channel_id=1, source_target_pairs={{0,4},{2,6},{4,0},{6,2},{8,12},{10,14},{12,8},{14,10},{16,20},{18,... | collective-permute-start | bytes 3145736 | tf_op jit(solution)/shard_map/ppermute | solution.py:1057
  72.4 26.1 %collective-permute-start.10 = (bf16[128,3072]{1,0:T(8,128)(2,1)}, bf16[128,3072]{1,0:T(8,128)(2,1)S(1)}, u32[]{:S(2)}, u32[]{:S(2)}) collective-permute-start(bf16[128,3072]{1,0:T(8,128)(2,1)} %get-tuple-element.74.refs_7_), channel_id=1, source_target_pairs={{0,8},{2,10},{4,12},{6,14},{8,0},{10,2},{12,4},{14,6},{16,24},{18,... | collective-permute-start | bytes 2359304 | tf_op jit(solution)/shard_map/ppermute | solution.py:1057
  74.9 1.9 collective-permute-start.8
  74.9 22.7 %collective-permute-start.9 = (bf16[128,2048]{1,0:T(8,128)(2,1)}, bf16[128,2048]{1,0:T(8,128)(2,1)S(1)}, u32[]{:S(2)}, u32[]{:S(2)}) collective-permute-start(bf16[128,2048]{1,0:T(8,128)(2,1)} %get-tuple-element.72.refs_3_), channel_id=1, source_target_pairs={{0,2},{2,0},{4,6},{6,4},{8,10},{10,8},{12,14},{14,12},{16,18},{18,... | collective-permute-start | bytes 1572872 | tf_op jit(solution)/shard_map/ppermute | solution.py:1057
  81.2 17.3 %all-to-all-start.2 = ((bf16[16,32,128]{2,1,0:T(8,128)(2,1)}), bf16[16,32,128]{2,1,0:T(8,128)(2,1)S(1)}, u32[]{:S(2)}, u32[]{:S(2)}) async-start(bf16[16,32,128]{2,1,0:T(8,128)(2,1)} %get-tuple-element.68), calls=%async_computation.2 | async-start | bytes 262144 | tf_op jit(solution)/shard_map/all_to_all | solution.py:1165
  85.3 12.3 %collective-permute-start.11 = (bf16[128,512]{1,0:T(8,128)(2,1)}, bf16[128,512]{1,0:T(8,128)(2,1)S(1)}, u32[]{:S(2)}, u32[]{:S(2)}) collective-permute-start(bf16[128,512]{1,0:T(8,128)(2,1)} %get-tuple-element.76), channel_id=1, source_target_pairs={{0,8},{2,10},{4,12},{6,14},{8,0},{10,2},{12,4},{14,6},{16,24},{18,... | collective-permute-start | bytes 393224 | tf_op jit(solution)/shard_map/ppermute | solution.py:1057
  104.2 36.0 %collective-permute-start.16 = (bf16[256,2560]{1,0:T(8,128)(2,1)}, bf16[256,2560]{1,0:T(8,128)(2,1)S(1)}, u32[]{:S(2)}, u32[]{:S(2)}) collective-permute-start(bf16[256,2560]{1,0:T(8,128)(2,1)} %get-tuple-element.80), channel_id=1, source_target_pairs={{0,2},{2,0},{4,6},{6,4},{8,10},{10,8},{12,14},{14,12},{16,18},{18,... | collective-permute-start | bytes 3932168 | tf_op jit(solution)/shard_map/ppermute | solution.py:1057
  105.2 4.1 %collective-permute-start.13 = (bf16[1024,512]{1,0:T(8,128)(2,1)S(1)}, bf16[1024,512]{1,0:T(8,128)(2,1)S(1)}, u32[]{:S(2)}, u32[]{:S(2)}) collective-permute-start(bf16[1024,512]{1,0:T(8,128)(2,1)S(1)} %copy-done.22), channel_id=1, source_target_pairs={{0,1},{1,0},{2,3},{3,2},{4,5},{5,4},{6,7},{7,6},{8,9},{9,8},{10,11... | collective-permute-start | bytes 3145736 | tf_op jit(solution)/shard_map/ppermute | solution.py:1164
  105.2 4.4 %collective-permute-start.14 = (bf16[1024,512]{1,0:T(8,128)(2,1)}, bf16[1024,512]{1,0:T(8,128)(2,1)S(1)}, u32[]{:S(2)}, u32[]{:S(2)}) collective-permute-start(bf16[1024,512]{1,0:T(8,128)(2,1)} %copy-done.23), channel_id=1, source_target_pairs={{0,1},{1,0},{2,3},{3,2},{4,5},{5,4},{6,7},{7,6},{8,9},{9,8},{10,11... | collective-permute-start | bytes 3145736 | tf_op jit(solution)/shard_map/ppermute | solution.py:1164
  105.7 28.8 %collective-permute-start.15 = (bf16[256,2048]{1,0:T(8,128)(2,1)}, bf16[256,2048]{1,0:T(8,128)(2,1)S(1)}, u32[]{:S(2)}, u32[]{:S(2)}) collective-permute-start(bf16[256,2048]{1,0:T(8,128)(2,1)} %get-tuple-element.78.refs_6_), channel_id=1, source_target_pairs={{0,4},{2,6},{4,0},{6,2},{8,12},{10,14},{12,8},{14,10},{16,20},{18,... | collective-permute-start | bytes 3145736 | tf_op jit(solution)/shard_map/ppermute | solution.py:1057
  117.9 33.0 %all-to-all-start.3 = ((bf16[16,160,128]{2,1,0:T(8,128)(2,1)}), bf16[16,160,128]{2,1,0:T(8,128)(2,1)}, u32[]{:S(2)}, u32[]{:S(2)}) async-start(bf16[16,160,128]{2,1,0:T(8,128)(2,1)} %get-tuple-element.79), calls=%async_computation.3 | async-start | bytes 1310720 | tf_op jit(solution)/shard_map/all_to_all | solution.py:1165
  147.4 22.2 %copy-start = (bf16[3,1024,512]{2,1,0:T(8,128)(2,1)S(1)}, bf16[3,1024,512]{2,1,0:T(8,128)(2,1)}, u32[]{:S(2)}) copy-start(bf16[3,1024,512]{2,1,0:T(8,128)(2,1)} %refs_1_.1) | copy-start | bytes 9437188
  147.4 15.6 %collective-permute-start.19 = (bf16[128,2560]{1,0:T(8,128)(2,1)}, bf16[128,2560]{1,0:T(8,128)(2,1)}, u32[]{:S(2)}, u32[]{:S(2)}) collective-permute-start(bf16[128,2560]{1,0:T(8,128)(2,1)} %get-tuple-element.87), channel_id=1, source_target_pairs={{0,4},{2,6},{4,0},{6,2},{8,12},{10,14},{12,8},{14,10},{16,20},{18,... | collective-permute-start | bytes 1966088 | tf_op jit(solution)/shard_map/ppermute | solution.py:1057
  147.5 15.4 %collective-permute-start.18 = (bf16[128,2048]{1,0:T(8,128)(2,1)}, bf16[128,2048]{1,0:T(8,128)(2,1)}, u32[]{:S(2)}, u32[]{:S(2)}) collective-permute-start(bf16[128,2048]{1,0:T(8,128)(2,1)} %get-tuple-element.82.refs_2_), channel_id=1, source_target_pairs={{0,8},{2,10},{4,12},{6,14},{8,0},{10,2},{12,4},{14,6},{16,24},{18,... | collective-permute-start | bytes 1572872 | tf_op jit(solution)/shard_map/ppermute | solution.py:1057
  150.9 29.9 %all-to-all-start.5 = ((bf16[16,96,128]{2,1,0:T(8,128)(2,1)}), bf16[16,96,128]{2,1,0:T(8,128)(2,1)}, u32[]{:S(2)}, u32[]{:S(2)}) async-start(bf16[16,96,128]{2,1,0:T(8,128)(2,1)} %shard_map.262.refs_15_), calls=%async_computation.5 | async-start | bytes 786432 | tf_op jit(solution)/shard_map/all_to_all | solution.py:1165
  166.1 26.9 %collective-permute-start.20 = (bf16[64,4608]{1,0:T(8,128)(2,1)}, bf16[64,4608]{1,0:T(8,128)(2,1)}, u32[]{:S(2)}, u32[]{:S(2)}) collective-permute-start(bf16[64,4608]{1,0:T(8,128)(2,1)} %get-tuple-element.88.refs_6_), channel_id=1, source_target_pairs={{0,16},{2,18},{4,20},{6,22},{8,24},{10,26},{12,28},{14,30},{16,0},... | collective-permute-start | bytes 1769480 | tf_op jit(solution)/shard_map/ppermute | solution.py:1057
  174.0 1.7 collective-permute-start.17
  180.8 16.8 %all-to-all-start.4 = ((f32[16,1,384]{2,1,0:T(1,128)}), f32[16,1,384]{2,1,0:T(1,128)S(1)}, u32[]{:S(2)}, u32[]{:S(2)}) async-start(f32[16,1,384]{2,1,0:T(1,128)} %reshape.137), calls=%async_computation.4 | async-start | bytes 49152 | tf_op jit(solution)/shard_map/all_to_all | solution.py:1165
  (32 other events, 114.9 us)
